TPU v7x, 128 devices: a whole 4x4x4 slice. The times are simulated.
128 devices in a mesh: dp: 128 (over y, x, z, core).
Axes of the slice: x: 4, y: 4, z: 4, core: 2. Of those that a mesh axis runs over, the one named last changes fastest.
Arguments:
- tokens: bfloat16 [32768, 1024], P('dp'), may hold values from -6 to 6
- norm_gain: float32 [1024], replicated, may hold values from 0.5 to 1.5
- qkv_weight: bfloat16 [1024, 3072], replicated, may hold values from -0.1875 to 0.1875
- out_weight: bfloat16 [1024, 1024], replicated, may hold values from -0.5 to 0.5
- ln_gain: float32 [1024], replicated, may hold values from 0.5 to 1.5
- ln_bias: float32 [1024], replicated, may hold values from -1 to 1
- up_weight: bfloat16 [1024, 4096], replicated, may hold values from -0.1875 to 0.1875
- down_weight: bfloat16 [4096, 1024], replicated, may hold values from -0.125 to 0.125
- buckets: int32 [32768, 1], P('dp'), may hold values from 0 to 3, as said below
- router_prob: float32 [32768], P('dp'), may hold values from 0.5 to 1
- heads_active: int32 [128, 3], P('dp'), may hold values from 8 to 16
- doc_lengths: int32 [128, 3], P('dp'), may hold values from 1 to 128, 256 in all within a row
- cotangent: bfloat16 [32768, 1024], P('dp'), may hold values from -24 to 24
Outputs:
- mixed: bfloat16 [32768, 1024], P('dp')
- input_grad: float32 [32768, 1024], P('dp')
- norm_gain_grad: float32 [1024], P('dp')
- qkv_grad: float32 [1024, 3072], P('dp')
- out_grad: float32 [1024, 1024], P('dp')
- ln_gain_grad: float32 [1024], P('dp')
- ln_bias_grad: float32 [1024], P('dp')
- up_grad: float32 [1024, 4096], P('dp')
- down_grad: float32 [4096, 1024], P('dp')
- bucket_counts: int32 [4], replicated
Inputs may be any that keep to these rules, and one draw needn't show every extreme that they name: `buckets`: among the tokens of one device no width level is named by more than 128 tokens, and in every draw some level of some device is named by exactly 128. `doc_lengths`: each row sums to 256 and its largest entry is 128.
All inputs are finite; a program needn't handle non-finite values.
Results may differ from a plain program's by a relative error of at most 0.014.
Values may be sent and summed in bfloat16 or wider, within the bound.
No kernel may reach another device: no remote copies, remote signals or barrier semaphores. Data moves between devices by JAX's collectives and lax.ppermute only.
A program may use at most 320 MiB of HBM per device.

v0:
```python
import functools

import jax
import jax.numpy as jnp
import numpy as np
from jax import lax
from jax.experimental import pallas as pl
from jax.experimental.pallas import tpu as pltpu
from jax.sharding import Mesh
from jax.sharding import PartitionSpec as P

HD = 64
NEST = 4
AX = ("y", "x", "z", "c")

NEG = -1e30
EPS = 1e-05
F32 = jnp.float32
BF16 = jnp.bfloat16
T = 256
D = 1024
FF = 4096
GW = 256
GROUPS = D // GW
FIRST = FF // 2 + 2 * D + 512
SECOND = FF + 512
THIRD = 3 * D + 512 + T
BITS = 9
MIB = 1024 * 1024


def nn(a, b):
    return lax.dot_general(a, b, (((1,), (0,)), ((), ())), preferred_element_type=F32)


def nt(a, b):
    return lax.dot_general(a, b, (((1,), (1,)), ((), ())), preferred_element_type=F32)


def tn(a, b):
    return lax.dot_general(a, b, (((0,), (0,)), ((), ())), preferred_element_type=F32)


def sds(shape, dtype):
    return jax.ShapeDtypeStruct(shape, dtype)


def smem():
    return pl.BlockSpec(memory_space=pltpu.SMEM)


def vmem():
    return pl.BlockSpec(memory_space=pltpu.VMEM)


def hbm():
    return pl.BlockSpec(memory_space=pl.ANY)


def call(kernel, name, flops, moved, **kw):
    return pl.pallas_call(
        kernel,
        name=name,
        compiler_params=pltpu.CompilerParams(vmem_limit_bytes=58 * MIB),
        cost_estimate=pl.CostEstimate(flops=flops, bytes_accessed=moved, transcendentals=0),
        **kw,
    )


def first_halves():
    return lax.broadcasted_iota(jnp.int32, (T, 128), 1) % HD < HD // 2


def low_heads():
    return lax.broadcasted_iota(jnp.int32, (T, 128), 1) < HD


def turned(x, cosine, sine, first):
    parts = []
    for at in range(0, x.shape[1], 128):
        part = x[:, at : at + 128]
        other = jnp.where(first, pltpu.roll(part, 128 - HD // 2, 1), pltpu.roll(part, HD // 2, 1))
        parts.append(part * cosine + other * sine)
    return jnp.concatenate(parts, 1)


def doc_start(lengths, place):
    end_0 = lengths[0, 0]
    end_1 = end_0 + lengths[0, 1]
    return jnp.where(place >= end_1, end_1, jnp.where(place >= end_0, end_0, 0))


def of_doc(lengths, place, values):
    end_0 = lengths[0, 0]
    end_1 = end_0 + lengths[0, 1]
    return jnp.where(
        place >= end_1, values[0, 2], jnp.where(place >= end_0, values[0, 1], values[0, 0])
    )


def normalized(middle):
    shifted = middle - jnp.mean(middle, -1, keepdims=True)
    rstd = lax.rsqrt(jnp.mean(shifted * shifted, -1, keepdims=True) + EPS)
    return shifted * rstd, rstd


def load(src, dst, sem):
    copy = pltpu.make_async_copy(src, dst, sem)
    copy.start()
    return copy


def columns(j, size):
    return pl.ds(pl.multiple_of(j * size, size), size)


def upright(row):
    return jnp.broadcast_to(row, (8, T)).T[:, :1]


def layer_kernel(
    lengths,
    heads,
    order,
    norm_gain,
    inverse,
    ln_gain,
    ln_bias,
    router,
    bucket,
    tokens_hbm,
    cot_hbm,
    wqkv_hbm,
    wo_hbm,
    up_hbm,
    down_hbm,
    first_mine,
    first_other,
    second_mine,
    second_other,
    third_mine,
    third_other,
    mixed_out,
    input_grad_out,
    tokens,
    cot,
    wqkv,
    wo,
    up,
    down,
    qkv,
    normed,
    merged,
    zed,
    gb,
    act,
    act_turned,
    gp,
    turned_f,
    left,
    middle,
    grad_mid,
    ga,
    gqkv,
    mixed,
    lines_f,
    lines,
    bias,
    active,
    level,
    in_sem,
    ffn_sem,
    act_sem,
    gp_sem,
    left_sem,
    group_sem,
    gb_sem,
    ga_sem,
    out_sem,
):
    core = order[0, 4]
    firsts, seconds, thirds = (
        (first_mine, first_other),
        (second_mine, second_other),
        (third_mine, third_other),
    )
    loads = [load(tokens_hbm, tokens, in_sem.at[0])]
    for n in range(3):
        loads.append(load(wqkv_hbm.at[:, n * D : (n + 1) * D], wqkv.at[n], in_sem.at[1 + n]))

    def ffn_loads(j):
        at = columns(j, D)
        return (
            pltpu.make_async_copy(up_hbm.at[:, at], up.at[:, at], ffn_sem.at[0, j]),
            pltpu.make_async_copy(down_hbm.at[at, :], down.at[at, :], ffn_sem.at[1, j]),
        )

    stores = []

    def store_left(n, value, axis, refs, at):
        turned_f[...] = value.astype(F32).T.reshape(turned_f.shape)
        for side, ref in enumerate(refs):
            half = core if side == 0 else 1 - core
            for i in range(4):
                if axis == 0:
                    rows = turned_f[i, :, :, half]
                elif axis == 1:
                    rows = turned_f[:, i, :, half]
                else:
                    rows = turned_f[:, :, i, half]
                left[side, n, pl.ds(128 * i, 128), :] = rows.reshape(128, T).astype(BF16)
            dst = ref.at[pl.ds(at, 512), :]
            stores.append(load(left.at[side, n], dst, left_sem.at[side, n]))

    def block_stores(src, j, refs, at, sem):
        rows = pl.ds(pl.multiple_of(at + T * j, T), T)
        return [
            pltpu.make_async_copy(src.at[:, columns(j, T)], ref.at[rows, :], sem.at[side, j])
            for side, ref in enumerate(refs)
        ]

    first = first_halves()
    low = low_heads()
    zero = jnp.zeros((T, 128), BF16)
    scale = HD**-0.5
    place = lax.broadcasted_iota(jnp.int32, (T, 128), 0)
    phase = (place - doc_start(lengths, place)).astype(F32) * inverse[...]
    cosine = jnp.cos(phase)
    sine = jnp.sin(phase)
    sine = jnp.where(first, -sine, sine)
    row = lax.broadcasted_iota(jnp.int32, (T, T), 0)
    col = lax.broadcasted_iota(jnp.int32, (T, T), 1)
    bias[...] = jnp.where((col >= doc_start(lengths, row)) & (col <= row), 0.0, NEG)
    active[...] = of_doc(lengths, place, heads)
    level[...] = upright(bucket[...])
    prob = upright(router[...])

    loads[0].wait()
    resid = tokens[...].astype(F32)
    rscale = lax.rsqrt(jnp.mean(resid * resid, -1, keepdims=True) + EPS)
    normed[...] = (resid * rscale * norm_gain[...]).astype(BF16)
    for n in range(3):
        loads[1 + n].wait()
        if n == 1:
            loads.append(load(cot_hbm, cot, in_sem.at[4]))
        if n == 2:
            loads.append(load(wo_hbm, wo, in_sem.at[5]))
            for copy in ffn_loads(0) + ffn_loads(1):
                copy.start()
        part = nn(normed[...], wqkv[n])
        qkv[n] = (turned(part, cosine, sine, first) if n < 2 else part).astype(BF16)

    def attend(g, carry):
        for pair in range(2):
            lanes = pl.ds(pl.multiple_of(g * GW + 128 * pair, 128), 128)
            qp, kp, vp = qkv[0, :, lanes], qkv[1, :, lanes], qkv[2, :, lanes]
            out = jnp.zeros((T, 128), F32)
            for side in range(2):
                keep = low if side == 0 else ~low
                s = nt(qp, jnp.where(keep, kp, zero)) * scale + bias[...]
                e = jnp.exp(s - jnp.max(s, -1, keepdims=True))
                p = (e / jnp.sum(e, -1, keepdims=True)).astype(BF16)
                out = out + nn(p, jnp.where(keep, vp, zero))
            head = 4 * g + 2 * pair + jnp.where(low, 0, 1)
            merged[:, lanes] = jnp.where(head < active[...], out, 0.0).astype(BF16)

        @pl.when((g > 0) & (g < NEST - 1))
        def _():
            for copy in ffn_loads(g + 1):
                copy.start()

        return carry

    lax.fori_loop(0, GROUPS, attend, 0)
    loads[5].wait()
    middle[...] = tokens[...].astype(F32) + nn(merged[...], wo[...])
    normed_mid, _ = normalized(middle[...])
    zed[...] = (normed_mid * ln_gain[...] + ln_bias[...]).astype(BF16)
    loads[4].wait()
    gb[...] = (cot[...].astype(F32) * prob).astype(BF16)
    for j in range(4):
        for copy in block_stores(gb, j, firsts, FF // 2, gb_sem):
            copy.start()

    def act_stores(j):
        rows = columns(j, 512)
        return [
            pltpu.make_async_copy(act_turned.at[side, rows, :], ref.at[rows, :], act_sem.at[side, j])
            for side, ref in enumerate(firsts)
        ]

    def hidden(j, carry):
        copy_up, copy_down = ffn_loads(j)
        at = columns(j, D)
        copy_up.wait()
        r = jnp.where(level[...] >= j, jnp.maximum(nn(zed[...], up[:, at]), 0.0), 0.0)
        a = (r * r).astype(BF16)
        act[:, at] = a
        by_core = a.T.reshape(16, 2, 32, T)
        low_rows, high_rows = by_core[:, 0].reshape(512, T), by_core[:, 1].reshape(512, T)
        act_turned[0, columns(j, 512), :] = jnp.where(core == 0, low_rows, high_rows)
        act_turned[1, columns(j, 512), :] = jnp.where(core == 0, high_rows, low_rows)
        for copy in act_stores(j):
            copy.start()
        copy_down.wait()
        gp[:, at] = (nt(gb[...], down[at, :]) * 2.0 * r).astype(BF16)
        for q in range(4):
            for copy in block_stores(gp, 4 * j + q, seconds, 0, gp_sem):
                copy.start()
        return carry

    lax.fori_loop(0, NEST, hidden, 0)
    store_left(0, zed[...], 1, seconds, FF)
    store_left(1, normed[...], 2, thirds, 3 * D)
    store_left(2, merged[...], 0, firsts, FF // 2 + 2 * D)

    branch = nn(act[...], down[...]).astype(BF16).astype(F32)
    mid = middle[...]
    mixed[...] = (mid + prob * branch).astype(BF16)
    stores.append(load(mixed, mixed_out, out_sem.at[1]))
    grad_zed = nt(gp[...], up[...]).astype(BF16).astype(F32)
    normed_mid, rstd = normalized(mid)
    ln_gain_part = jnp.sum(grad_zed * normed_mid, 0, keepdims=True)
    ln_bias_part = jnp.sum(grad_zed, 0, keepdims=True)
    grad_norm = grad_zed * ln_gain[...]
    grad = cot[...].astype(F32) + rstd * (
        grad_norm
        - jnp.mean(grad_norm, -1, keepdims=True)
        - normed_mid * jnp.mean(grad_norm * normed_mid, -1, keepdims=True)
    )
    grad_mid[...] = grad
    ga[...] = grad.astype(BF16)
    for j in range(4):
        for copy in block_stores(ga, j, firsts, FF // 2 + D, ga_sem):
            copy.start()

    bias[...] = jnp.where((row >= doc_start(lengths, col)) & (row <= col), 0.0, NEG)

    def group_stores(g):
        return [
            copy
            for n in range(3)
            for copy in block_stores(gqkv.at[n], g, thirds, n * D, group_sem.at[n])
        ]

    def attend_back(g, carry):
        grad_merged = nt(ga[...], wo[columns(g, GW), :])
        for pair in range(2):
            lanes = pl.ds(pl.multiple_of(g * GW + 128 * pair, 128), 128)
            head = 4 * g + 2 * pair + jnp.where(low, 0, 1)
            gm = grad_merged[:, 128 * pair : 128 * pair + 128]
            gm = jnp.where(head < active[...], gm, 0.0).astype(BF16)
            qp, kp, vp = qkv[0, :, lanes], qkv[1, :, lanes], qkv[2, :, lanes]
            k_turned = kp.T
            grad_values = jnp.zeros((T, 128), F32)
            grad_keys = jnp.zeros((T, 128), F32)
            grad_query = []
            for side in range(2):
                keep = low if side == 0 else ~low
                q_head = jnp.where(keep, qp, zero)
                gm_head = jnp.where(keep, gm, zero)
                s = nt(kp, q_head) * scale + bias[...]
                e = jnp.exp(s - jnp.max(s, 0, keepdims=True))
                p = e / jnp.sum(e, 0, keepdims=True)
                grad_p = nt(vp, gm_head)
                grad_values = grad_values + nn(p.astype(BF16), gm_head)
                grad_s = (p * (grad_p - jnp.sum(p * grad_p, 0, keepdims=True))).astype(BF16)
                grad_keys = grad_keys + nn(grad_s, q_head)
                grad_query.append(nn(k_turned[HD * side : HD * side + HD], grad_s))
            grad_q = jnp.concatenate(grad_query, 0).T * scale
            gqkv[0, :, lanes] = turned(grad_q, cosine, -sine, first).astype(BF16)
            gqkv[1, :, lanes] = turned(grad_keys * scale, cosine, -sine, first).astype(BF16)
            gqkv[2, :, lanes] = grad_values.astype(BF16)
        for copy in group_stores(g):
            copy.start()
        return carry

    lax.fori_loop(0, GROUPS, attend_back, 0)

    grad_normed = nt(gqkv[0], wqkv[0]) + nt(gqkv[1], wqkv[1]) + nt(gqkv[2], wqkv[2])
    resid = tokens[...].astype(F32)
    unit = resid * rscale
    gain_part = jnp.sum(grad_normed * unit, 0, keepdims=True)
    grad_unit = grad_normed * norm_gain[...]
    middle[...] = grad_mid[...] + rscale * (
        grad_unit - unit * jnp.mean(grad_unit * unit, -1, keepdims=True)
    )
    stores.append(load(middle, input_grad_out, out_sem.at[3]))

    item = lax.broadcasted_iota(jnp.int32, (128, 1), 0)
    count = jnp.zeros((128, 1), jnp.int32)
    for n in range(NEST):
        total = jnp.sum((bucket[...] == n).astype(jnp.int32), 1, keepdims=True)
        at = item - 3 - BITS * n
        bit = lax.shift_right_logical(total, jnp.clip(at, 0, BITS - 1)) & 1
        count = jnp.where((at >= 0) & (at < BITS), bit, count)
    wide = jnp.where(item == 0, gain_part, jnp.where(item == 1, ln_gain_part, ln_bias_part))
    lines_f[...] = jnp.where(item < 3, wide, count.astype(F32)).T.reshape(lines_f.shape)
    for side, ref in enumerate(thirds):
        half = core if side == 0 else 1 - core
        for i in range(4):
            part = lines_f[:, :, i, half].reshape(128, 128).astype(BF16)
            lines[side, pl.ds(128 * (i % 2), 128), pl.ds(128 * (i // 2), 128)] = part
        dst = ref.at[pl.ds(3 * D + 512, T), :]
        stores.append(load(lines.at[side], dst, out_sem.at[4 + side]))

    for j in range(NEST):
        for copy in act_stores(j):
            copy.wait()
        for copy in block_stores(gb, j, firsts, FF // 2, gb_sem):
            copy.wait()
        for copy in block_stores(ga, j, firsts, FF // 2 + D, ga_sem):
            copy.wait()
        for copy in group_stores(j):
            copy.wait()
    for j in range(FF // T):
        for copy in block_stores(gp, j, seconds, 0, gp_sem):
            copy.wait()
    for copy in stores:
        copy.wait()


def layer(lengths, heads, order, norm_gain, inverse, ln_gain, ln_bias, router, bucket, *arrays):
    firsts = sds((FIRST, T), BF16)
    seconds = sds((SECOND, T), BF16)
    thirds = sds((THIRD, T), BF16)
    row_b = sds((T, D), BF16)
    row_f = sds((T, D), F32)
    scratch = [
        row_b,
        row_b,
        sds((3, D, D), BF16),
        sds((D, D), BF16),
        sds((D, FF), BF16),
        sds((FF, D), BF16),
        sds((3, T, D), BF16),
        row_b,
        row_b,
        row_b,
        row_b,
        sds((T, FF), BF16),
        sds((2, FF // 2, T), BF16),
        sds((T, FF), BF16),
        sds((4, 4, 4, 2, 8, T), F32),
        sds((2, 3, 512, T), BF16),
        row_f,
        row_f,
        row_b,
        sds((3, T, D), BF16),
        row_b,
        sds((4, 4, 4, 2, 8, 128), F32),
        sds((2, T, T), BF16),
        sds((T, T), F32),
        sds((T, 128), jnp.int32),
        sds((T, 1), jnp.int32),
    ]
    semaphores = [(6,), (2, NEST), (2, NEST), (2, FF // T), (2, 3), (3, 2, GROUPS), (2, 4), (2, 4)]
    semaphores.append((6,))
    return call(
        layer_kernel,
        "layer",
        12 * T * D * (3 * D + FF),
        40 * MIB,
        in_specs=[smem()] * 3 + [vmem()] * 6 + [hbm()] * 6,
        out_specs=[hbm()] * 8,
        out_shape=[firsts, firsts, seconds, seconds, thirds, thirds, row_b, row_f],
        scratch_shapes=[pltpu.VMEM(s.shape, s.dtype) for s in scratch]
        + [pltpu.SemaphoreType.DMA(s) for s in semaphores],
    )(lengths, heads, order, norm_gain, inverse, ln_gain, ln_bias, router, bucket, *arrays)


def load_left(refs, at, rows, order, axis, left, sem):
    return [
        load(
            ref.at[pl.ds(pl.multiple_of(at + rows * order[axis, i], rows), rows), :],
            left.at[pl.ds(rows * i, rows), pl.ds(T * m, T)],
            sem.at[i, m],
        )
        for i in range(4)
        for m, ref in enumerate(refs)
    ]


def load_right(refs, at, right, sem):
    return [
        load(
            ref.at[pl.ds(at + T * q, T), :],
            right.at[pl.ds(T * m, T), pl.ds(T * q, T)],
            sem.at[m, q],
        )
        for m, ref in enumerate(refs)
        for q in range(D // T)
    ]


def wait(copies):
    for copy in copies:
        copy.wait()


def store_out(out, rows, at, sent, kept, sem):
    return [
        load(out.at[pl.ds(2 * side, 2), rows, at], ref.at[:, rows, at], sem.at[side])
        for side, ref in enumerate((sent, kept))
    ]


def down_grad_kernel(
    order, one, two, sent, kept, act, merged, gb, ga, out, act_sem, merged_sem, gb_sem, ga_sem, sem
):
    refs = (one, two)
    gb_loads = load_right(refs, FF // 2, gb, gb_sem)
    act_loads = load_left(refs, 0, 512, order, 0, act, act_sem)
    merged_loads = load_left(refs, FF // 2 + 2 * D, 128, order, 0, merged, merged_sem)
    ga_loads = load_right(refs, FF // 2 + D, ga, ga_sem)
    stores = []
    wait(gb_loads)
    wide = pl.ds(0, D)
    for i in range(4):
        wait(act_loads[2 * i : 2 * i + 2])
        out[i, :, wide] = nn(act[pl.ds(512 * i, 512), :], gb[...]).astype(BF16)
        if i % 2 == 1:
            ref = (sent, kept)[i // 2]
            src = out.at[pl.ds(i - 1, 2), :, wide]
            stores.append(load(src, ref.at[:, :, wide], sem.at[0, i // 2]))
    wait(merged_loads + ga_loads)
    part = nn(merged[...], ga[...])
    more = pl.ds(D, T)
    for i in range(4):
        rows = part[128 * i : 128 * i + 128].reshape(16, 8, D)
        quarters = [rows[:, :, T * q : T * q + T] for q in range(4)]
        out[i, :, more] = jnp.concatenate(quarters, 1).reshape(512, T).astype(BF16)
    stores += store_out(out, pl.ds(0, 512), more, sent, kept, sem.at[1])
    wait(stores)


def down_grads(order, one, two):
    part = sds((2, 512, D + T), BF16)
    return call(
        down_grad_kernel,
        "down_and_out_grad",
        2 * T * D * (FF + D),
        10 * MIB,
        in_specs=[smem()] + [hbm()] * 2,
        out_specs=[hbm()] * 2,
        out_shape=[part, part],
        scratch_shapes=[
            pltpu.VMEM((FF // 2, 2 * T), BF16),
            pltpu.VMEM((512, 2 * T), BF16),
            pltpu.VMEM((2 * T, D), BF16),
            pltpu.VMEM((2 * T, D), BF16),
            pltpu.VMEM((4, 512, D + T), BF16),
            pltpu.SemaphoreType.DMA((4, 2)),
            pltpu.SemaphoreType.DMA((4, 2)),
            pltpu.SemaphoreType.DMA((2, 4)),
            pltpu.SemaphoreType.DMA((2, 4)),
            pltpu.SemaphoreType.DMA((2, 2)),
        ],
    )(order, one, two)


def wide_kernel(axis, parts, order, one, two, after, sent, kept, left, right, lines, out, *sems):
    left_sem, right_sem, line_sem, sem = sems
    refs = (one, two)
    loads = load_left(refs, parts * D, 128, order, axis, left, left_sem)
    rights = [load_right(refs, n * D, right.at[n], right_sem.at[n]) for n in range(parts)]
    line_loads = []
    if axis == 2:
        for i in range(4):
            block = order[axis, i]
            rows = pl.ds(pl.multiple_of(parts * D + 512 + 128 * (block % 2), 128), 128)
            at = pl.ds(pl.multiple_of(128 * (block // 2), 128), 128)
            for m, ref in enumerate(refs):
                line_loads.append(load(ref.at[rows, at], lines.at[i, m], line_sem.at[i, m]))
    stores = []
    wait(loads)
    every = pl.ds(0, 128)
    for n in range(parts):
        wait(rights[n])
        at = pl.ds(n * D, D)
        out[:, :, at] = nn(left[...], right[n]).astype(BF16).reshape(4, 128, D)
        stores += store_out(out, every, at, sent, kept, sem.at[n])
    if axis == 2:
        wait(line_loads)
        at = pl.ds(parts * D, 128)
        out[:, :, at] = (lines[:, 0].astype(F32) + lines[:, 1].astype(F32)).astype(BF16)
        stores += store_out(out, every, at, sent, kept, sem.at[parts])
    wait(stores)


def wide_grads(name, axis, parts, order, one, two, after):
    width = parts * D + (128 if axis == 2 else 0)
    part = sds((2, 128, width), BF16)
    return call(
        functools.partial(wide_kernel, axis, parts),
        name,
        2 * T * D * D * parts,
        9 * MIB,
        in_specs=[smem()] + [hbm()] * 3,
        out_specs=[hbm()] * 2,
        out_shape=[part, part],
        scratch_shapes=[
            pltpu.VMEM((512, 2 * T), BF16),
            pltpu.VMEM((parts, 2 * T, D), BF16),
            pltpu.VMEM((4, 2, 128, 128), BF16),
            pltpu.VMEM((4, 128, width), BF16),
            pltpu.SemaphoreType.DMA((4, 2)),
            pltpu.SemaphoreType.DMA((parts, 2, 4)),
            pltpu.SemaphoreType.DMA((4, 2)),
            pltpu.SemaphoreType.DMA((parts + 1, 2)),
        ],
    )(order, one, two, after)


def swap_cores(array):
    return lax.ppermute(array, "c", [(0, 1), (1, 0)])


def pairs(mask_0, mask_1):
    perm = []
    for p in range(4):
        perm.append((2 * p, 2 * (p ^ mask_0)))
        perm.append((2 * p + 1, 2 * (p ^ mask_1) + 1))
    return perm


def pick(array, index, dim):
    return lax.dynamic_index_in_dim(array, index, dim, keepdims=False)


def block_order(axis):
    p = lax.axis_index(axis)
    core = lax.axis_index("c")
    return [p ^ (1 + 2 * core), p ^ 2, p, p ^ (3 - 2 * core)]


def ordered(token, *arrays):
    return lax.optimization_barrier((*arrays, token))[:-1]


def chain(sent, kept, axes, shape, done):
    left = [axis for axis in ("y", "x", "z") if axis != axes[0]]
    for axis in axes:
        got = lax.ppermute(sent, (axis, "c"), pairs(1, 3))
        token = yield sent
        got, kept = ordered(token, got, kept)
        more = (got[1].astype(F32) + kept[1].astype(F32)).astype(BF16)
        got_2 = lax.ppermute(more, (axis, "c"), pairs(3, 1))
        token = yield more
        got, kept, got_2 = ordered(token, got, kept, got_2)
        terms = [a.reshape(shape).astype(F32) for a in (got[0], kept[0], got_2)]
        if not left:
            done.append(sum(terms))
            return
        following = axes[axes.index(axis) + 1]
        dim = left.index(following)
        left.pop(dim)
        shape = shape[:dim] + shape[dim + 1 :]
        first, across, own, second = [
            sum(pick(term, at, dim) for term in terms) for at in block_order(following)
        ]
        sent = jnp.stack([first, across]).astype(BF16)
        kept = jnp.stack([own, second])


def take_turns(token, *chains):
    for steps in chains:
        next(steps)
    running = list(chains)
    while running:
        for steps in list(running):
            try:
                token = steps.send(token)
            except StopIteration:
                running.remove(steps)


def body(
    tokens,
    norm_gain,
    qkv_weight,
    out_weight,
    ln_gain,
    ln_bias,
    up_weight,
    down_weight,
    buckets,
    router_prob,
    heads_active,
    doc_lengths,
    cotangent,
):
    core = lax.axis_index("c")
    orders = jnp.stack([jnp.stack(block_order(axis) + [core]) for axis in ("y", "x", "z")])
    orders = orders.astype(jnp.int32)
    norm_gain, ln_gain, ln_bias = [v.reshape(1, D) for v in (norm_gain, ln_gain, ln_bias)]
    router = router_prob.reshape(1, T)
    levels = buckets.reshape(1, T)
    inverse = np.tile(10000.0 ** (-2.0 * np.arange(HD // 2) / HD), 4).reshape(1, 128)
    inverse = jnp.asarray(inverse, F32)

    first, first_other, second, second_other, third, third_other, mixed, input_grad = layer(
        doc_lengths,
        heads_active,
        orders,
        norm_gain,
        inverse,
        ln_gain,
        ln_bias,
        router,
        levels,
        tokens,
        cotangent,
        qkv_weight,
        out_weight,
        up_weight,
        down_weight,
    )
    first_2 = swap_cores(first_other)
    (second_other,) = ordered(first_2, second_other)
    second_2 = swap_cores(second_other)
    (third_other,) = ordered(second_2, third_other)
    third_2 = swap_cores(third_other)
    down_sent, down_kept = down_grads(orders, first, first_2)
    up_sent, up_kept = wide_grads("up_grad", 1, 4, orders, second, second_2, down_sent)
    qkv_sent, qkv_kept = wide_grads("qkv_grad", 2, 3, orders, third, third_2, up_sent)

    down, up, qkv = [], [], []
    take_turns(
        qkv_sent,
        chain(down_sent, down_kept, "yxz", (4, 4, 32, D + T), down),
        chain(up_sent, up_kept, "xyz", (4, 4, 8, FF), up),
        chain(qkv_sent, qkv_kept, "zyx", (4, 4, 8, 3 * D + 128), qkv),
    )
    (down,), (up_grad,), (qkv,) = down, up, qkv
    down_grad = down[:, :D]
    out_grad = down[:, D:].reshape(4, 8, T).transpose(1, 0, 2).reshape(8, D)
    qkv_grad, line = qkv[:, : 3 * D], qkv[:, 3 * D :]
    bits = line[0, 3 : 3 + BITS * NEST].astype(jnp.int32).reshape(NEST, BITS)
    totals = jnp.sum(bits << jnp.arange(BITS, dtype=jnp.int32)[None, :], 1)
    return (
        mixed,
        input_grad,
        line[:, 0],
        qkv_grad,
        out_grad,
        line[:, 1],
        line[:, 2],
        up_grad,
        down_grad,
        totals,
    )


def solution(mesh):
    finer = Mesh(mesh.devices.reshape(4, 4, 4, 2), AX)
    rows = P(AX, None)
    return jax.shard_map(
        body,
        mesh=finer,
        in_specs=(rows, P(), P(), P(), P(), P(), P(), P(), rows, P(AX), rows, rows, rows),
        out_specs=(rows, rows, P(AX), rows, rows, P(AX), P(AX), rows, rows, P()),
        check_vma=False,
    )
```

profile of v0, /device:TPU:0, one launch (start us, length us, event | category | flops | bytes accessed | tf_op | source)
XLA Modules:
  0.0 150.2 jit_solution(16671469221653584512)
XLA Ops:
  1.5 34.6 %layer.1 = (bf16[4608,256]{1,0:T(8,128)(2,1)}, bf16[4608,256]{1,0:T(8,128)(2,1)}, bf16[4608,256]{1,0:T(8,128)(2,1)}, bf16[4608,256]{1,0:T(8,128)(2,1)}, bf16[384...) custom-call(s32[1,3]{1,0:T(1,128)} %lengths.1, s32[1,3]{1,0:T(1,128)} %heads.1, ...), custom_call_target="tpu_custom_call" | custom-call | flops 22548578304 | bytes 41943040 | tf_op jit(solution)/shard_map/layer/pallas_call | solution.py:459
  36.2 4.7 %collective-permute-done.two = bf16[4608,256]{1,0:T(8,128)(2,1)S(1)} collective-permute-done((bf16[4608,256]{1,0:T(8,128)(2,1)}, bf16[4608,256]{1,0:T(8,128)(2,1)S(1)}, u32[]{:S(2)}, u32[]{:S(2)}) %collective-permute-start) | collective-permute-done | bytes 2359328 | tf_op jit(solution)/shard_map/ppermute | solution.py:616
  41.0 1.4 copy-done.5
  42.5 7.9 %down_and_out_grad.1 = (bf16[2,512,1280]{2,1,0:T(8,128)(2,1)}, bf16[2,512,1280]{2,1,0:T(8,128)(2,1)}) custom-call(s32[3,5]{1,0:T(4,128)} %pad_add_fusion.order, bf16[4608,256]{1,0:T(8,128)(2,1)} %get-tuple-element.80.one, bf16[4608,256]{1,0:T(8,128)(2,1)} %copy-done.5), custom_call_target="tpu_custom_call" | custom-call | flops 2684354560 | bytes 10485760 | tf_op jit(solution)/shard_map/down_and_out_grad/pallas_call | solution.py:539
  50.4 1.7 %collective-permute-start.5 = (bf16[2,512,1280]{2,1,0:T(8,128)(2,1)}, bf16[2,512,1280]{2,1,0:T(8,128)(2,1)}, u32[]{:S(2)}, u32[]{:S(2)}) collective-permute-start(bf16[2,512,1280]{2,1,0:T(8,128)(2,1)} %get-tuple-element.81.after), channel_id=1, source_target_pairs={{0,32},{1,97},{32,0},{33,65},{64,96},{65,33},{96,64},{97,1},{2,34}... | collective-permute-start | bytes 7864328 | tf_op jit(solution)/shard_map/ppermute | solution.py:644
  52.1 1.5 %collective-permute-start.2 = (bf16[3840,256]{1,0:T(8,128)(2,1)}, bf16[3840,256]{1,0:T(8,128)(2,1)S(1)}, u32[]{:S(2)}, u32[]{:S(2)}) collective-permute-start(bf16[3840,256]{1,0:T(8,128)(2,1)} %get-tuple-element.78), channel_id=1, source_target_pairs={{0,1},{1,0},{2,3},{3,2},{4,5},{5,4},{6,7},{7,6},{8,9},{9,8},{10,11... | collective-permute-start | bytes 5898248 | tf_op jit(solution)/shard_map/ppermute | solution.py:616
  53.7 7.4 %up_grad.1 = (bf16[2,128,4096]{2,1,0:T(8,128)(2,1)}, bf16[2,128,4096]{2,1,0:T(8,128)(2,1)}) custom-call(s32[3,5]{1,0:T(4,128)} %pad_add_fusion.order, bf16[4608,256]{1,0:T(8,128)(2,1)} %get-tuple-element.79.one, bf16[4608,256]{1,0:T(8,128)(2,1)} %copy-done.4, bf16[2,512,1280]{2,1,0:T(8,128)(2,1)} %get-tuple-element.81.after), custom_call_target="tpu_custom_call" | custom-call | flops 2147483648 | bytes 9437184 | tf_op jit(solution)/shard_map/up_grad/pallas_call | solution.py:594
  61.1 1.6 %collective-permute-start.4 = (bf16[2,128,4096]{2,1,0:T(8,128)(2,1)}, bf16[2,128,4096]{2,1,0:T(8,128)(2,1)}, u32[]{:S(2)}, u32[]{:S(2)}) collective-permute-start(bf16[2,128,4096]{2,1,0:T(8,128)(2,1)} %get-tuple-element.82.after), channel_id=1, source_target_pairs={{0,8},{1,25},{8,0},{9,17},{16,24},{17,9},{24,16},{25,1},{2,10},{3,... | collective-permute-start | bytes 6291464 | tf_op jit(solution)/shard_map/ppermute | solution.py:644
  63.9 6.5 %qkv_grad.1 = (bf16[2,128,3200]{2,1,0:T(8,128)(2,1)}, bf16[2,128,3200]{2,1,0:T(8,128)(2,1)}) custom-call(s32[3,5]{1,0:T(4,128)} %pad_add_fusion.order, bf16[3840,256]{1,0:T(8,128)(2,1)} %get-tuple-element.73.one, bf16[3840,256]{1,0:T(8,128)(2,1)} %copy-done.2, bf16[2,128,4096]{2,1,0:T(8,128)(2,1)} %get-tuple-element.82.after), custom_call_target="tpu_custom_call" | custom-call | flops 1610612736 | bytes 9437184 | tf_op jit(solution)/shard_map/qkv_grad/pallas_call | solution.py:594
  70.5 2.0 %collective-permute-start.3 = (bf16[2,128,3200]{2,1,0:T(8,128)(2,1)}, bf16[2,128,3200]{2,1,0:T(8,128)(2,1)}, u32[]{:S(2)}, u32[]{:S(2)}) collective-permute-start(bf16[2,128,3200]{2,1,0:T(8,128)(2,1)} %get-tuple-element.83), channel_id=1, source_target_pairs={{0,2},{1,7},{2,0},{3,5},{4,6},{5,3},{6,4},{7,1},{8,10},{9,15},{10,... | collective-permute-start | bytes 4915208 | tf_op jit(solution)/shard_map/ppermute | solution.py:644
  72.5 10.0 %collective-permute-done.5 = bf16[2,512,1280]{2,1,0:T(8,128)(2,1)} collective-permute-done((bf16[2,512,1280]{2,1,0:T(8,128)(2,1)}, bf16[2,512,1280]{2,1,0:T(8,128)(2,1)}, u32[]{:S(2)}, u32[]{:S(2)}) %collective-permute-start.5) | collective-permute-done | bytes 2621472 | tf_op jit(solution)/shard_map/ppermute | solution.py:644
  82.4 1.6 %fusion = bf16[512,1280]{1,0:T(8,128)(2,1)S(1)} fusion(bf16[2,512,1280]{2,1,0:T(8,128)(2,1)S(1)} %copy-done, bf16[2,512,1280]{2,1,0:T(8,128)(2,1)} %collective-permute-done.5), kind=kLoop, calls=%fused_computation.3 | loop fusion | flops 2621440 | bytes 3932160 | tf_op jit(solution)/shard_map/convert_element_type | solution.py:647
  84.1 3.2 %collective-permute-start.8 = (bf16[512,1280]{1,0:T(8,128)(2,1)S(1)}, bf16[512,1280]{1,0:T(8,128)(2,1)S(1)}, u32[]{:S(2)}, u32[]{:S(2)}) collective-permute-start(bf16[512,1280]{1,0:T(8,128)(2,1)S(1)} %fusion), channel_id=1, source_target_pairs={{0,96},{1,33},{32,64},{33,1},{64,32},{65,97},{96,0},{97,65},{2,98}... | collective-permute-start | bytes 3932168 | tf_op jit(solution)/shard_map/ppermute | solution.py:648
  87.5 1.5 fusion.1
  89.0 2.8 %collective-permute-start.7 = (bf16[128,4096]{1,0:T(8,128)(2,1)S(1)}, bf16[128,4096]{1,0:T(8,128)(2,1)S(1)}, u32[]{:S(2)}, u32[]{:S(2)}) collective-permute-start(bf16[128,4096]{1,0:T(8,128)(2,1)S(1)} %fusion.1), channel_id=1, source_target_pairs={{0,24},{1,9},{8,16},{9,1},{16,8},{17,25},{24,0},{25,17},{2,26},{3,... | collective-permute-start | bytes 3145736 | tf_op jit(solution)/shard_map/ppermute | solution.py:648
  92.0 1.3 fusion.2
  93.3 4.1 %collective-permute-start.6 = (bf16[128,3200]{1,0:T(8,128)(2,1)S(1)}, bf16[128,3200]{1,0:T(8,128)(2,1)S(1)}, u32[]{:S(2)}, u32[]{:S(2)}) collective-permute-start(bf16[128,3200]{1,0:T(8,128)(2,1)S(1)} %fusion.2), channel_id=1, source_target_pairs={{0,6},{1,3},{2,4},{3,1},{4,2},{5,7},{6,0},{7,5},{8,14},{9,11},{10,... | collective-permute-start | bytes 2457608 | tf_op jit(solution)/shard_map/ppermute | solution.py:648
  97.5 5.5 %collective-permute-done.8 = bf16[512,1280]{1,0:T(8,128)(2,1)S(1)} collective-permute-done((bf16[512,1280]{1,0:T(8,128)(2,1)S(1)}, bf16[512,1280]{1,0:T(8,128)(2,1)S(1)}, u32[]{:S(2)}, u32[]{:S(2)}) %collective-permute-start.8) | collective-permute-done | bytes 1310752 | tf_op jit(solution)/shard_map/ppermute | solution.py:648
  103.0 1.4 slice.140
  105.8 1.7 %collective-permute-start.11 = (bf16[2,4,32,1280]{3,2,1,0:T(8,128)(2,1)S(1)}, bf16[2,4,32,1280]{3,2,1,0:T(8,128)(2,1)S(1)}, u32[]{:S(2)}, u32[]{:S(2)}) collective-permute-start(bf16[2,4,32,1280]{3,2,1,0:T(8,128)(2,1)S(1)} %pad_maximum_fusion.3), channel_id=1, source_target_pairs={{0,8},{1,25},{8,0},{9,17},{16,24},{17,9},{24,16},{25,1},{2,10},{3,... | collective-permute-start | bytes 1966088 | tf_op jit(solution)/shard_map/ppermute | solution.py:644
  112.7 1.7 %collective-permute-start.9 = (bf16[2,4,8,3200]{3,2,1,0:T(8,128)(2,1)S(1)}, bf16[2,4,8,3200]{3,2,1,0:T(8,128)(2,1)S(1)}, u32[]{:S(2)}, u32[]{:S(2)}) collective-permute-start(bf16[2,4,8,3200]{3,2,1,0:T(8,128)(2,1)S(1)} %pad_maximum_fusion.5), channel_id=1, source_target_pairs={{0,32},{1,97},{32,0},{33,65},{64,96},{65,33},{96,64},{97,1},{2,34}... | collective-permute-start | bytes 1228808 | tf_op jit(solution)/shard_map/ppermute | solution.py:644
  114.5 2.0 %collective-permute-done.11 = bf16[2,4,32,1280]{3,2,1,0:T(8,128)(2,1)S(1)} collective-permute-done((bf16[2,4,32,1280]{3,2,1,0:T(8,128)(2,1)S(1)}, bf16[2,4,32,1280]{3,2,1,0:T(8,128)(2,1)S(1)}, u32[]{:S(2)}, u32[]{:S(2)}) %collective-permute-start.11) | collective-permute-done | bytes 655392 | tf_op jit(solution)/shard_map/ppermute | solution.py:644
  116.5 2.9 %collective-permute-start.14 = (bf16[4,32,1280]{2,1,0:T(8,128)(2,1)S(1)}, bf16[4,32,1280]{2,1,0:T(8,128)(2,1)S(1)}, u32[]{:S(2)}, u32[]{:S(2)}) collective-permute-start(bf16[4,32,1280]{2,1,0:T(8,128)(2,1)S(1)} %fusion.3), channel_id=1, source_target_pairs={{0,24},{1,9},{8,16},{9,1},{16,8},{17,25},{24,0},{25,17},{2,26},{3,... | collective-permute-start | bytes 983048 | tf_op jit(solution)/shard_map/ppermute | solution.py:648
  119.5 3.1 %collective-permute-start.13 = (bf16[4,8,4096]{2,1,0:T(8,128)(2,1)S(1)}, bf16[4,8,4096]{2,1,0:T(8,128)(2,1)S(1)}, u32[]{:S(2)}, u32[]{:S(2)}) collective-permute-start(bf16[4,8,4096]{2,1,0:T(8,128)(2,1)S(1)} %fusion.4), channel_id=1, source_target_pairs={{0,96},{1,33},{32,64},{33,1},{64,32},{65,97},{96,0},{97,65},{2,98}... | collective-permute-start | bytes 786440 | tf_op jit(solution)/shard_map/ppermute | solution.py:648
  122.7 3.3 %collective-permute-done.9 = bf16[2,4,8,3200]{3,2,1,0:T(8,128)(2,1)S(1)} collective-permute-done((bf16[2,4,8,3200]{3,2,1,0:T(8,128)(2,1)S(1)}, bf16[2,4,8,3200]{3,2,1,0:T(8,128)(2,1)S(1)}, u32[]{:S(2)}, u32[]{:S(2)}) %collective-permute-start.9) | collective-permute-done | bytes 409632 | tf_op jit(solution)/shard_map/ppermute | solution.py:644
  126.0 3.1 %collective-permute-start.12 = (bf16[4,8,3200]{2,1,0:T(8,128)(2,1)S(1)}, bf16[4,8,3200]{2,1,0:T(8,128)(2,1)S(1)}, u32[]{:S(2)}, u32[]{:S(2)}) collective-permute-start(bf16[4,8,3200]{2,1,0:T(8,128)(2,1)S(1)} %fusion.5), channel_id=1, source_target_pairs={{0,96},{1,33},{32,64},{33,1},{64,32},{65,97},{96,0},{97,65},{2,98}... | collective-permute-start | bytes 614408 | tf_op jit(solution)/shard_map/ppermute | solution.py:648
  129.4 2.0 %collective-permute-start.17 = (bf16[2,32,1280]{2,1,0:T(8,128)(2,1)S(1)}, bf16[2,32,1280]{2,1,0:T(8,128)(2,1)S(1)}, u32[]{:S(2)}, u32[]{:S(2)}) collective-permute-start(bf16[2,32,1280]{2,1,0:T(8,128)(2,1)S(1)} %pad_maximum_fusion.9), channel_id=1, source_target_pairs={{0,2},{1,7},{2,0},{3,5},{4,6},{5,3},{6,4},{7,1},{8,10},{9,15},{10,... | collective-permute-start | bytes 491528 | tf_op jit(solution)/shard_map/ppermute | solution.py:644
  134.0 1.7 %collective-permute-done.17 = bf16[2,32,1280]{2,1,0:T(8,128)(2,1)S(1)} collective-permute-done((bf16[2,32,1280]{2,1,0:T(8,128)(2,1)S(1)}, bf16[2,32,1280]{2,1,0:T(8,128)(2,1)S(1)}, u32[]{:S(2)}, u32[]{:S(2)}) %collective-permute-start.17) | collective-permute-done | bytes 163872 | tf_op jit(solution)/shard_map/ppermute | solution.py:644
  135.8 4.7 %collective-permute-start.19 = (bf16[32,1280]{1,0:T(8,128)(2,1)S(1)}, bf16[32,1280]{1,0:T(8,128)(2,1)S(1)}, u32[]{:S(2)}, u32[]{:S(2)}) collective-permute-start(bf16[32,1280]{1,0:T(8,128)(2,1)S(1)} %fusion.12), channel_id=1, source_target_pairs={{0,6},{1,3},{2,4},{3,1},{4,2},{5,7},{6,0},{7,5},{8,14},{9,11},{10,... | collective-permute-start | bytes 245768 | tf_op jit(solution)/shard_map/ppermute | solution.py:648
  140.5 1.5 collective-permute-start.20
  142.0 2.2 %collective-permute-start.18 = (bf16[8,3200]{1,0:T(8,128)(2,1)S(1)}, bf16[8,3200]{1,0:T(8,128)(2,1)S(1)}, u32[]{:S(2)}, u32[]{:S(2)}) collective-permute-start(bf16[8,3200]{1,0:T(8,128)(2,1)S(1)} %fusion.14), channel_id=1, source_target_pairs={{0,24},{1,9},{8,16},{9,1},{16,8},{17,25},{24,0},{25,17},{2,26},{3,... | collective-permute-start | bytes 153608 | tf_op jit(solution)/shard_map/ppermute | solution.py:648
  144.2 1.8 %collective-permute-done.20 = bf16[8,4096]{1,0:T(8,128)(2,1)S(1)} collective-permute-done((bf16[8,4096]{1,0:T(8,128)(2,1)S(1)}, bf16[8,4096]{1,0:T(8,128)(2,1)S(1)}, u32[]{:S(2)}, u32[]{:S(2)}) %collective-permute-start.20) | collective-permute-done | bytes 65568 | tf_op jit(solution)/shard_map/ppermute | solution.py:648
  (91 shorter events, 16.6 us)
Async XLA Ops:
  36.1 4.8 %collective-permute-start = (bf16[4608,256]{1,0:T(8,128)(2,1)}, bf16[4608,256]{1,0:T(8,128)(2,1)S(1)}, u32[]{:S(2)}, u32[]{:S(2)}) collective-permute-start(bf16[4608,256]{1,0:T(8,128)(2,1)} %get-tuple-element.76), channel_id=1, source_target_pairs={{0,1},{1,0},{2,3},{3,2},{4,5},{5,4},{6,7},{7,6},{8,9},{9,8},{10,11... | collective-permute-start | bytes 7077896 | tf_op jit(solution)/shard_map/ppermute | solution.py:616
  41.0 1.4 copy-start.5
  42.4 9.8 %collective-permute-start.1 = (bf16[4608,256]{1,0:T(8,128)(2,1)}, bf16[4608,256]{1,0:T(8,128)(2,1)S(1)}, u32[]{:S(2)}, u32[]{:S(2)}) collective-permute-start(bf16[4608,256]{1,0:T(8,128)(2,1)} %get-tuple-element.77), channel_id=1, source_target_pairs={{0,1},{1,0},{2,3},{3,2},{4,5},{5,4},{6,7},{7,6},{8,9},{9,8},{10,11... | collective-permute-start | bytes 7077896 | tf_op jit(solution)/shard_map/ppermute | solution.py:616
  50.4 32.0 %collective-permute-start.5 = (bf16[2,512,1280]{2,1,0:T(8,128)(2,1)}, bf16[2,512,1280]{2,1,0:T(8,128)(2,1)}, u32[]{:S(2)}, u32[]{:S(2)}) collective-permute-start(bf16[2,512,1280]{2,1,0:T(8,128)(2,1)} %get-tuple-element.81.after), channel_id=1, source_target_pairs={{0,32},{1,97},{32,0},{33,65},{64,96},{65,33},{96,64},{97,1},{2,34}... | collective-permute-start | bytes 7864328 | tf_op jit(solution)/shard_map/ppermute | solution.py:644
  52.1 1.5 %copy-start.4 = (bf16[4608,256]{1,0:T(8,128)(2,1)}, bf16[4608,256]{1,0:T(8,128)(2,1)S(1)}, u32[]{:S(2)}) copy-start(bf16[4608,256]{1,0:T(8,128)(2,1)S(1)} %collective-permute-done.1.two) | copy-start | bytes 7077892
  52.1 10.5 %collective-permute-start.2 = (bf16[3840,256]{1,0:T(8,128)(2,1)}, bf16[3840,256]{1,0:T(8,128)(2,1)S(1)}, u32[]{:S(2)}, u32[]{:S(2)}) collective-permute-start(bf16[3840,256]{1,0:T(8,128)(2,1)} %get-tuple-element.78), channel_id=1, source_target_pairs={{0,1},{1,0},{2,3},{3,2},{4,5},{5,4},{6,7},{7,6},{8,9},{9,8},{10,11... | collective-permute-start | bytes 5898248 | tf_op jit(solution)/shard_map/ppermute | solution.py:616
  61.1 26.4 %collective-permute-start.4 = (bf16[2,128,4096]{2,1,0:T(8,128)(2,1)}, bf16[2,128,4096]{2,1,0:T(8,128)(2,1)}, u32[]{:S(2)}, u32[]{:S(2)}) collective-permute-start(bf16[2,128,4096]{2,1,0:T(8,128)(2,1)} %get-tuple-element.82.after), channel_id=1, source_target_pairs={{0,8},{1,25},{8,0},{9,17},{16,24},{17,9},{24,16},{25,1},{2,10},{3,... | collective-permute-start | bytes 6291464 | tf_op jit(solution)/shard_map/ppermute | solution.py:644
  62.7 1.3 copy-start.2
  63.9 18.5 %copy-start = (bf16[2,512,1280]{2,1,0:T(8,128)(2,1)S(1)}, bf16[2,512,1280]{2,1,0:T(8,128)(2,1)}, u32[]{:S(2)}) copy-start(bf16[2,512,1280]{2,1,0:T(8,128)(2,1)} %get-tuple-element.94) | copy-start | bytes 7864324
  70.5 21.5 %collective-permute-start.3 = (bf16[2,128,3200]{2,1,0:T(8,128)(2,1)}, bf16[2,128,3200]{2,1,0:T(8,128)(2,1)}, u32[]{:S(2)}, u32[]{:S(2)}) collective-permute-start(bf16[2,128,3200]{2,1,0:T(8,128)(2,1)} %get-tuple-element.83), channel_id=1, source_target_pairs={{0,2},{1,7},{2,0},{3,5},{4,6},{5,3},{6,4},{7,1},{8,10},{9,15},{10,... | collective-permute-start | bytes 4915208 | tf_op jit(solution)/shard_map/ppermute | solution.py:644
  72.5 15.1 %copy-start.1 = (bf16[2,128,4096]{2,1,0:T(8,128)(2,1)S(1)}, bf16[2,128,4096]{2,1,0:T(8,128)(2,1)}, u32[]{:S(2)}) copy-start(bf16[2,128,4096]{2,1,0:T(8,128)(2,1)} %get-tuple-element.97) | copy-start | bytes 6291460
  84.1 7.9 %copy-start.3 = (bf16[2,128,3200]{2,1,0:T(8,128)(2,1)S(1)}, bf16[2,128,3200]{2,1,0:T(8,128)(2,1)}, u32[]{:S(2)}) copy-start(bf16[2,128,3200]{2,1,0:T(8,128)(2,1)} %get-tuple-element.100) | copy-start | bytes 4915204
  84.1 18.9 %collective-permute-start.8 = (bf16[512,1280]{1,0:T(8,128)(2,1)S(1)}, bf16[512,1280]{1,0:T(8,128)(2,1)S(1)}, u32[]{:S(2)}, u32[]{:S(2)}) collective-permute-start(bf16[512,1280]{1,0:T(8,128)(2,1)S(1)} %fusion), channel_id=1, source_target_pairs={{0,96},{1,33},{32,64},{33,1},{64,32},{65,97},{96,0},{97,65},{2,98}... | collective-permute-start | bytes 3932168 | tf_op jit(solution)/shard_map/ppermute | solution.py:648
  89.0 18.4 %collective-permute-start.7 = (bf16[128,4096]{1,0:T(8,128)(2,1)S(1)}, bf16[128,4096]{1,0:T(8,128)(2,1)S(1)}, u32[]{:S(2)}, u32[]{:S(2)}) collective-permute-start(bf16[128,4096]{1,0:T(8,128)(2,1)S(1)} %fusion.1), channel_id=1, source_target_pairs={{0,24},{1,9},{8,16},{9,1},{16,8},{17,25},{24,0},{25,17},{2,26},{3,... | collective-permute-start | bytes 3145736 | tf_op jit(solution)/shard_map/ppermute | solution.py:648
  93.3 17.5 %collective-permute-start.6 = (bf16[128,3200]{1,0:T(8,128)(2,1)S(1)}, bf16[128,3200]{1,0:T(8,128)(2,1)S(1)}, u32[]{:S(2)}, u32[]{:S(2)}) collective-permute-start(bf16[128,3200]{1,0:T(8,128)(2,1)S(1)} %fusion.2), channel_id=1, source_target_pairs={{0,6},{1,3},{2,4},{3,1},{4,2},{5,7},{6,0},{7,5},{8,14},{9,11},{10,... | collective-permute-start | bytes 2457608 | tf_op jit(solution)/shard_map/ppermute | solution.py:648
  105.8 10.7 %collective-permute-start.11 = (bf16[2,4,32,1280]{3,2,1,0:T(8,128)(2,1)S(1)}, bf16[2,4,32,1280]{3,2,1,0:T(8,128)(2,1)S(1)}, u32[]{:S(2)}, u32[]{:S(2)}) collective-permute-start(bf16[2,4,32,1280]{3,2,1,0:T(8,128)(2,1)S(1)} %pad_maximum_fusion.3), channel_id=1, source_target_pairs={{0,8},{1,25},{8,0},{9,17},{16,24},{17,9},{24,16},{25,1},{2,10},{3,... | collective-permute-start | bytes 1966088 | tf_op jit(solution)/shard_map/ppermute | solution.py:644
  109.9 9.5 %collective-permute-start.10 = (bf16[2,4,8,4096]{3,2,1,0:T(8,128)(2,1)S(1)}, bf16[2,4,8,4096]{3,2,1,0:T(8,128)(2,1)S(1)}, u32[]{:S(2)}, u32[]{:S(2)}) collective-permute-start(bf16[2,4,8,4096]{3,2,1,0:T(8,128)(2,1)S(1)} %pad_maximum_fusion.4), channel_id=1, source_target_pairs={{0,32},{1,97},{32,0},{33,65},{64,96},{65,33},{96,64},{97,1},{2,34}... | collective-permute-start | bytes 1572872 | tf_op jit(solution)/shard_map/ppermute | solution.py:644
  112.7 13.2 %collective-permute-start.9 = (bf16[2,4,8,3200]{3,2,1,0:T(8,128)(2,1)S(1)}, bf16[2,4,8,3200]{3,2,1,0:T(8,128)(2,1)S(1)}, u32[]{:S(2)}, u32[]{:S(2)}) collective-permute-start(bf16[2,4,8,3200]{3,2,1,0:T(8,128)(2,1)S(1)} %pad_maximum_fusion.5), channel_id=1, source_target_pairs={{0,32},{1,97},{32,0},{33,65},{64,96},{65,33},{96,64},{97,1},{2,34}... | collective-permute-start | bytes 1228808 | tf_op jit(solution)/shard_map/ppermute | solution.py:644
  116.5 12.6 %collective-permute-start.14 = (bf16[4,32,1280]{2,1,0:T(8,128)(2,1)S(1)}, bf16[4,32,1280]{2,1,0:T(8,128)(2,1)S(1)}, u32[]{:S(2)}, u32[]{:S(2)}) collective-permute-start(bf16[4,32,1280]{2,1,0:T(8,128)(2,1)S(1)} %fusion.3), channel_id=1, source_target_pairs={{0,24},{1,9},{8,16},{9,1},{16,8},{17,25},{24,0},{25,17},{2,26},{3,... | collective-permute-start | bytes 983048 | tf_op jit(solution)/shard_map/ppermute | solution.py:648
  119.5 12.0 %collective-permute-start.13 = (bf16[4,8,4096]{2,1,0:T(8,128)(2,1)S(1)}, bf16[4,8,4096]{2,1,0:T(8,128)(2,1)S(1)}, u32[]{:S(2)}, u32[]{:S(2)}) collective-permute-start(bf16[4,8,4096]{2,1,0:T(8,128)(2,1)S(1)} %fusion.4), channel_id=1, source_target_pairs={{0,96},{1,33},{32,64},{33,1},{64,32},{65,97},{96,0},{97,65},{2,98}... | collective-permute-start | bytes 786440 | tf_op jit(solution)/shard_map/ppermute | solution.py:648
  126.0 7.0 %collective-permute-start.12 = (bf16[4,8,3200]{2,1,0:T(8,128)(2,1)S(1)}, bf16[4,8,3200]{2,1,0:T(8,128)(2,1)S(1)}, u32[]{:S(2)}, u32[]{:S(2)}) collective-permute-start(bf16[4,8,3200]{2,1,0:T(8,128)(2,1)S(1)} %fusion.5), channel_id=1, source_target_pairs={{0,96},{1,33},{32,64},{33,1},{64,32},{65,97},{96,0},{97,65},{2,98}... | collective-permute-start | bytes 614408 | tf_op jit(solution)/shard_map/ppermute | solution.py:648
  129.4 6.3 %collective-permute-start.17 = (bf16[2,32,1280]{2,1,0:T(8,128)(2,1)S(1)}, bf16[2,32,1280]{2,1,0:T(8,128)(2,1)S(1)}, u32[]{:S(2)}, u32[]{:S(2)}) collective-permute-start(bf16[2,32,1280]{2,1,0:T(8,128)(2,1)S(1)} %pad_maximum_fusion.9), channel_id=1, source_target_pairs={{0,2},{1,7},{2,0},{3,5},{4,6},{5,3},{6,4},{7,1},{8,10},{9,15},{10,... | collective-permute-start | bytes 491528 | tf_op jit(solution)/shard_map/ppermute | solution.py:644
  131.7 8.8 %collective-permute-start.16 = (bf16[2,8,4096]{2,1,0:T(8,128)(2,1)S(1)}, bf16[2,8,4096]{2,1,0:T(8,128)(2,1)S(1)}, u32[]{:S(2)}, u32[]{:S(2)}) collective-permute-start(bf16[2,8,4096]{2,1,0:T(8,128)(2,1)S(1)} %pad_maximum_fusion.10), channel_id=1, source_target_pairs={{0,2},{1,7},{2,0},{3,5},{4,6},{5,3},{6,4},{7,1},{8,10},{9,15},{10,... | collective-permute-start | bytes 393224 | tf_op jit(solution)/shard_map/ppermute | solution.py:644
  133.3 8.7 %collective-permute-start.15 = (bf16[2,8,3200]{2,1,0:T(8,128)(2,1)S(1)}, bf16[2,8,3200]{2,1,0:T(8,128)(2,1)S(1)}, u32[]{:S(2)}, u32[]{:S(2)}) collective-permute-start(bf16[2,8,3200]{2,1,0:T(8,128)(2,1)S(1)} %pad_maximum_fusion.11), channel_id=1, source_target_pairs={{0,8},{1,25},{8,0},{9,17},{16,24},{17,9},{24,16},{25,1},{2,10},{3,... | collective-permute-start | bytes 307208 | tf_op jit(solution)/shard_map/ppermute | solution.py:644
  135.8 10.3 %collective-permute-start.19 = (bf16[32,1280]{1,0:T(8,128)(2,1)S(1)}, bf16[32,1280]{1,0:T(8,128)(2,1)S(1)}, u32[]{:S(2)}, u32[]{:S(2)}) collective-permute-start(bf16[32,1280]{1,0:T(8,128)(2,1)S(1)} %fusion.12), channel_id=1, source_target_pairs={{0,6},{1,3},{2,4},{3,1},{4,2},{5,7},{6,0},{7,5},{8,14},{9,11},{10,... | collective-permute-start | bytes 245768 | tf_op jit(solution)/shard_map/ppermute | solution.py:648
  140.5 5.6 %collective-permute-start.20 = (bf16[8,4096]{1,0:T(8,128)(2,1)S(1)}, bf16[8,4096]{1,0:T(8,128)(2,1)S(1)}, u32[]{:S(2)}, u32[]{:S(2)}) collective-permute-start(bf16[8,4096]{1,0:T(8,128)(2,1)S(1)} %fusion.13), channel_id=1, source_target_pairs={{0,6},{1,3},{2,4},{3,1},{4,2},{5,7},{6,0},{7,5},{8,14},{9,11},{10,... | collective-permute-start | bytes 196616 | tf_op jit(solution)/shard_map/ppermute | solution.py:648
  142.0 6.0 %collective-permute-start.18 = (bf16[8,3200]{1,0:T(8,128)(2,1)S(1)}, bf16[8,3200]{1,0:T(8,128)(2,1)S(1)}, u32[]{:S(2)}, u32[]{:S(2)}) collective-permute-start(bf16[8,3200]{1,0:T(8,128)(2,1)S(1)} %fusion.14), channel_id=1, source_target_pairs={{0,24},{1,9},{8,16},{9,1},{16,8},{17,25},{24,0},{25,17},{2,26},{3,... | collective-permute-start | bytes 153608 | tf_op jit(solution)/shard_map/ppermute | solution.py:648
where the time goes:
time: 151 us; the launch traced here: 150 us
  Pallas kernels  56.5 us (37%)
  starting transfers between devices  41.7 us (28%)
  waiting for transfers between devices  30.6 us (20%)
  other arithmetic  10.5 us (7%)
  local copies, waits for them, and re-layouts  9.91 us (7%)
    pallas_call x1, Pallas kernels, layer(): call(layer_kernel, 'layer', 12 * T * D * (3 * D + FF), 40 * MIB, in_specs...  34.6 us
    ppermute x9, starting transfers between devices, chain(): got_2 = lax.ppermute(more, (axis, 'c'), pairs(3, 1))  27.6 us
    ppermute x9, waiting for transfers between devices, chain(): got = lax.ppermute(sent, (axis, 'c'), pairs(1, 3))  17.4 us
    pallas_call x2, Pallas kernels, wide_grads(): call(functools.partial(wide_kernel, axis, parts), name, 2 * T * D * D * p...  14 us
    ppermute x9, starting transfers between devices, chain(): got = lax.ppermute(sent, (axis, 'c'), pairs(1, 3))  12.3 us
    ppermute x9, waiting for transfers between devices, chain(): got_2 = lax.ppermute(more, (axis, 'c'), pairs(3, 1))  8.47 us
    pallas_call x1, Pallas kernels, down_grads(): call(down_grad_kernel, 'down_and_out_grad', 2 * T * D * (FF + D), 10 * MI...  7.88 us
    ppermute x3, waiting for transfers between devices, swap_cores(): return lax.ppermute(array, 'c', [(0, 1), (1, 0)])  4.74 us
  transfers between devices with their start and end apart: 21, of which 10 were waited for; matrix products, arithmetic and copies ran while one was open for 10% of the time, Pallas kernels for 15%

commit v1 on v0

v1 whole, which is shorter than its diff:
```python
import jax
import jax.numpy as jnp
import numpy as np
from jax import lax
from jax.experimental import pallas as pl
from jax.experimental.pallas import tpu as pltpu
from jax.sharding import Mesh
from jax.sharding import PartitionSpec as P

HD = 64
NEST = 4
AX = ("y", "x", "z", "c")

NEG = -1e30
EPS = 1e-05
F32 = jnp.float32
BF16 = jnp.bfloat16
T = 256
D = 1024
FF = 4096
GW = 256
GROUPS = D // GW
ACT, GB, GA, MERGED, FIRST = 0, 512, 768, 1024, 1152
GP, ZED, NORMED, SECOND = 0, 1024, 1152, 1280
GQKV, LINES, THIRD = 0, 768, 896
BITS = 9
MIB = 1024 * 1024


def nn(a, b):
    return lax.dot_general(a, b, (((1,), (0,)), ((), ())), preferred_element_type=F32)


def nt(a, b):
    return lax.dot_general(a, b, (((1,), (1,)), ((), ())), preferred_element_type=F32)


def tn(a, b):
    return lax.dot_general(a, b, (((0,), (0,)), ((), ())), preferred_element_type=F32)


def sds(shape, dtype):
    return jax.ShapeDtypeStruct(shape, dtype)


def smem():
    return pl.BlockSpec(memory_space=pltpu.SMEM)


def vmem():
    return pl.BlockSpec(memory_space=pltpu.VMEM)


def hbm():
    return pl.BlockSpec(memory_space=pltpu.HBM)


def call(kernel, name, flops, moved, room, anywhere=False, **kw):
    def in_hbm(spec):
        return spec.memory_space == pltpu.HBM

    kw["out_shape"] = [
        pltpu.HBM(s.shape, s.dtype) if in_hbm(spec) else s
        for s, spec in zip(kw["out_shape"], kw["out_specs"])
    ]
    run = pl.pallas_call(
        kernel,
        name=name,
        compiler_params=pltpu.CompilerParams(vmem_limit_bytes=room * MIB),
        cost_estimate=pl.CostEstimate(flops=flops, bytes_accessed=moved, transcendentals=0),
        **kw,
    )

    def placed(*args):
        return run(
            *(
                pltpu.with_memory_space_constraint(arg, pltpu.HBM)
                if in_hbm(spec) and not anywhere
                else arg
                for arg, spec in zip(args, kw["in_specs"])
            )
        )

    return placed


def first_halves():
    return lax.broadcasted_iota(jnp.int32, (T, 128), 1) % HD < HD // 2


def low_heads():
    return lax.broadcasted_iota(jnp.int32, (T, 128), 1) < HD


def turned(x, cosine, sine, first):
    parts = []
    for at in range(0, x.shape[1], 128):
        part = x[:, at : at + 128]
        other = jnp.where(first, pltpu.roll(part, 128 - HD // 2, 1), pltpu.roll(part, HD // 2, 1))
        parts.append(part * cosine + other * sine)
    return jnp.concatenate(parts, 1)


def doc_start(lengths, place):
    end_0 = lengths[0, 0]
    end_1 = end_0 + lengths[0, 1]
    return jnp.where(place >= end_1, end_1, jnp.where(place >= end_0, end_0, 0))


def of_doc(lengths, place, values):
    end_0 = lengths[0, 0]
    end_1 = end_0 + lengths[0, 1]
    return jnp.where(
        place >= end_1, values[0, 2], jnp.where(place >= end_0, values[0, 1], values[0, 0])
    )


def normalized(middle):
    shifted = middle - jnp.mean(middle, -1, keepdims=True)
    rstd = lax.rsqrt(jnp.mean(shifted * shifted, -1, keepdims=True) + EPS)
    return shifted * rstd, rstd


def load(src, dst, sem):
    copy = pltpu.make_async_copy(src, dst, sem)
    copy.start()
    return copy


def columns(j, size):
    if isinstance(j, int):
        return pl.ds(j * size, size)
    return pl.ds(pl.multiple_of(j * size, size), size)


def upright(row):
    return jnp.broadcast_to(row, (8, T)).T[:, :1]


def places():
    return lax.broadcasted_iota(jnp.int32, (T, 128), 0)


def rotary(lengths, inverse):
    phase = (places() - doc_start(lengths, places())).astype(F32) * inverse[...]
    sine = jnp.sin(phase)
    return jnp.cos(phase), jnp.where(first_halves(), -sine, sine)


def store_both(src, refs, at, sem):
    return [pltpu.make_async_copy(src, ref.at[at], sem.at[side]) for side, ref in enumerate(refs)]


def start(copies):
    for copy in copies:
        copy.start()


def wait(copies):
    for copy in copies:
        copy.wait()


def front_kernel(
    lengths,
    heads,
    order,
    norm_gain,
    inverse,
    ln_gain,
    ln_bias,
    router,
    bucket,
    tokens_hbm,
    cot_hbm,
    wqkv_hbm,
    wo_hbm,
    up_hbm,
    down_hbm,
    parts,
    first_mine,
    first_other,
    second_mine,
    second_other,
    qkv_out,
    grad_mid_out,
    mixed_out,
    tokens,
    cot,
    wqkv,
    wo,
    up,
    down,
    qkv,
    normed,
    merged,
    zed,
    gb,
    act,
    act_turned,
    gp,
    turned_f,
    left,
    middle,
    grad_mid,
    ga,
    mixed,
    bias,
    active,
    level,
    in_sem,
    ffn_sem,
    act_sem,
    gp_sem,
    left_sem,
    gb_sem,
    ga_sem,
    out_sem,
):
    core = order[0, 4]
    firsts, seconds = (first_mine, first_other), (second_mine, second_other)
    loads = [load(tokens_hbm, tokens, in_sem.at[0])]
    for n in range(3):
        loads.append(load(wqkv_hbm.at[:, n * D : (n + 1) * D], wqkv.at[n], in_sem.at[1 + n]))

    def ffn_loads(j):
        at = columns(j, D)
        return (
            pltpu.make_async_copy(up_hbm.at[:, at], up.at[:, at], ffn_sem.at[0, j]),
            pltpu.make_async_copy(down_hbm.at[at, :], down.at[at, :], ffn_sem.at[1, j]),
        )

    stores = []

    def store_left(n, value, axis, refs, at):
        turned_f[...] = value.astype(F32).T.reshape(turned_f.shape)
        for side, ref in enumerate(refs):
            half = core if side == 0 else 1 - core
            for i in range(4):
                if axis == 0:
                    rows = turned_f[i, :, :, half]
                elif axis == 1:
                    rows = turned_f[:, i, :, half]
                else:
                    rows = turned_f[:, :, i, half]
                left[side, n, :, pl.ds(T * i, T)] = rows.reshape(128, T).astype(BF16)
            dst = ref.at[pl.ds(at, 128), :]
            stores.append(load(left.at[side, n], dst, left_sem.at[side, n]))

    first = first_halves()
    low = low_heads()
    zero = jnp.zeros((T, 128), BF16)
    scale = HD**-0.5
    cosine, sine = rotary(lengths, inverse)
    row = lax.broadcasted_iota(jnp.int32, (T, T), 0)
    col = lax.broadcasted_iota(jnp.int32, (T, T), 1)
    bias[...] = jnp.where((col >= doc_start(lengths, row)) & (col <= row), 0.0, NEG)
    active[...] = of_doc(lengths, places(), heads)
    level[...] = upright(bucket[...])
    prob = upright(router[...])

    loads[0].wait()
    resid = tokens[...].astype(F32)
    rscale = lax.rsqrt(jnp.mean(resid * resid, -1, keepdims=True) + EPS)
    normed[...] = (resid * rscale * norm_gain[...]).astype(BF16)
    for n in range(3):
        loads[1 + n].wait()
        if n == 1:
            loads.append(load(cot_hbm, cot, in_sem.at[4]))
        if n == 2:
            loads.append(load(wo_hbm, wo, in_sem.at[5]))
            for copy in ffn_loads(0) + ffn_loads(1):
                copy.start()
        part = nn(normed[...], wqkv[n])
        qkv[n] = (turned(part, cosine, sine, first) if n < 2 else part).astype(BF16)
    stores.append(load(qkv, qkv_out, out_sem.at[0]))

    def attend(g, carry):
        for pair in range(2):
            lanes = pl.ds(pl.multiple_of(g * GW + 128 * pair, 128), 128)
            qp, kp, vp = qkv[0, :, lanes], qkv[1, :, lanes], qkv[2, :, lanes]
            out = jnp.zeros((T, 128), F32)
            for side in range(2):
                keep = low if side == 0 else ~low
                s = nt(qp, jnp.where(keep, kp, zero)) * scale + bias[...]
                e = jnp.exp(s - jnp.max(s, -1, keepdims=True))
                p = (e / jnp.sum(e, -1, keepdims=True)).astype(BF16)
                out = out + nn(p, jnp.where(keep, vp, zero))
            head = 4 * g + 2 * pair + jnp.where(low, 0, 1)
            merged[:, lanes] = jnp.where(head < active[...], out, 0.0).astype(BF16)

        @pl.when((g > 0) & (g < NEST - 1))
        def _():
            for copy in ffn_loads(g + 1):
                copy.start()

        return carry

    lax.fori_loop(0, GROUPS, attend, 0)
    loads[5].wait()
    middle[...] = tokens[...].astype(F32) + nn(merged[...], wo[...])
    normed_mid, _ = normalized(middle[...])
    zed[...] = (normed_mid * ln_gain[...] + ln_bias[...]).astype(BF16)
    loads[4].wait()
    gb[...] = (cot[...].astype(F32) * prob).astype(BF16)
    both_gb = store_both(gb, firsts, (pl.ds(GB, T), slice(None)), gb_sem)
    for copy in both_gb:
        copy.start()

    def act_stores(j):
        at = (pl.ds(ACT, 512), columns(j, T))
        return [
            pltpu.make_async_copy(act_turned.at[side, :, at[1]], ref.at[at], act_sem.at[side, j])
            for side, ref in enumerate(firsts)
        ]

    def gp_stores(j):
        rows = pl.ds(pl.multiple_of(GP + T * j, T), T)
        return store_both(gp.at[:, columns(j, D)], seconds, (rows, slice(None)), gp_sem.at[j])

    def hidden(j, carry):
        copy_up, copy_down = ffn_loads(j)
        at = columns(j, D)
        copy_up.wait()
        r = jnp.where(level[...] >= j, jnp.maximum(nn(zed[...], up[:, at]), 0.0), 0.0)
        a = (r * r).astype(BF16)
        act[:, at] = a
        by_core = a.T.reshape(16, 2, 32, T)
        low_rows, high_rows = by_core[:, 0].reshape(512, T), by_core[:, 1].reshape(512, T)
        act_turned[0, :, columns(j, T)] = jnp.where(core == 0, low_rows, high_rows)
        act_turned[1, :, columns(j, T)] = jnp.where(core == 0, high_rows, low_rows)
        for copy in act_stores(j):
            copy.start()
        copy_down.wait()
        gp[:, at] = (nt(gb[...], down[at, :]) * 2.0 * r).astype(BF16)
        for copy in gp_stores(j):
            copy.start()
        return carry

    lax.fori_loop(0, NEST, hidden, 0)
    store_left(0, zed[...], 1, seconds, ZED)
    store_left(1, normed[...], 2, seconds, NORMED)
    store_left(2, merged[...], 0, firsts, MERGED)

    branch = nn(act[...], down[...]).astype(BF16).astype(F32)
    mid = middle[...]
    mixed[...] = (mid + prob * branch).astype(BF16)
    stores.append(load(mixed, mixed_out, out_sem.at[1]))
    grad_zed = nt(gp[...], up[...]).astype(BF16).astype(F32)
    normed_mid, rstd = normalized(mid)
    parts[0:1, :] = jnp.sum(grad_zed * normed_mid, 0, keepdims=True)
    parts[1:2, :] = jnp.sum(grad_zed, 0, keepdims=True)
    grad_norm = grad_zed * ln_gain[...]
    grad = cot[...].astype(F32) + rstd * (
        grad_norm
        - jnp.mean(grad_norm, -1, keepdims=True)
        - normed_mid * jnp.mean(grad_norm * normed_mid, -1, keepdims=True)
    )
    ga[...] = grad.astype(BF16)
    both_ga = store_both(ga, firsts, (pl.ds(GA, T), slice(None)), ga_sem)
    for copy in both_ga:
        copy.start()
    grad_mid[...] = grad
    stores.append(load(grad_mid, grad_mid_out, out_sem.at[2]))
    for j in range(NEST):
        wait(act_stores(j) + gp_stores(j))
    wait(both_gb + both_ga + stores)


def front(lengths, heads, order, norm_gain, inverse, ln_gain, ln_bias, router, bucket, *arrays):
    firsts = sds((FIRST, D), BF16)
    seconds = sds((SECOND, D), BF16)
    row_b = sds((T, D), BF16)
    row_f = sds((T, D), F32)
    scratch = [
        row_b,
        row_b,
        sds((3, D, D), BF16),
        sds((D, D), BF16),
        sds((D, FF), BF16),
        sds((FF, D), BF16),
        sds((3, T, D), BF16),
        row_b,
        row_b,
        row_b,
        row_b,
        sds((T, FF), BF16),
        sds((2, 512, D), BF16),
        sds((T, FF), BF16),
        sds((4, 4, 4, 2, 8, T), F32),
        sds((2, 3, 128, D), BF16),
        row_f,
        row_f,
        row_b,
        row_b,
        sds((T, T), F32),
        sds((T, 128), jnp.int32),
        sds((T, 1), jnp.int32),
    ]
    semaphores = [(6,), (2, NEST), (2, NEST), (NEST, 2), (2, 3), (2,), (2,), (3,)]
    return call(
        front_kernel,
        "front",
        2 * T * D * (4 * D + 4 * FF),
        40 * MIB,
        58,
        in_specs=[smem()] * 3 + [vmem()] * 6 + [hbm()] * 6,
        out_specs=[vmem()] + [hbm()] * 7,
        out_shape=[sds((8, D), F32), firsts, firsts, seconds, seconds, sds((3, T, D), BF16)]
        + [row_f, row_b],
        scratch_shapes=[pltpu.VMEM(s.shape, s.dtype) for s in scratch]
        + [pltpu.SemaphoreType.DMA(s) for s in semaphores],
    )(lengths, heads, order, norm_gain, inverse, ln_gain, ln_bias, router, bucket, *arrays)


def back_kernel(
    lengths,
    heads,
    order,
    norm_gain,
    inverse,
    bucket,
    parts,
    first_mine,
    qkv_hbm,
    grad_mid_hbm,
    tokens_hbm,
    wqkv_hbm,
    wo_hbm,
    third_mine,
    third_other,
    input_grad_out,
    ga,
    qkv,
    grad_mid,
    tokens,
    wqkv,
    wo,
    gqkv,
    lines_f,
    lines,
    bias,
    active,
    in_sem,
    w_sem,
    group_sem,
    out_sem,
):
    core = order[0, 4]
    thirds = (third_mine, third_other)
    loads = [
        load(first_mine.at[pl.ds(GA, T), :], ga, in_sem.at[0]),
        load(wo_hbm.at[pl.ds(0, GW), :], wo.at[pl.ds(0, GW), :], in_sem.at[1]),
        load(qkv_hbm.at[:, :, pl.ds(0, GW)], qkv.at[:, :, pl.ds(0, GW)], in_sem.at[2]),
    ]
    others = pl.ds(GW, D - GW)
    more = [
        pltpu.make_async_copy(wo_hbm.at[others, :], wo.at[others, :], in_sem.at[5]),
        pltpu.make_async_copy(qkv_hbm.at[:, :, others], qkv.at[:, :, others], in_sem.at[6]),
    ]
    late = [
        pltpu.make_async_copy(tokens_hbm, tokens, in_sem.at[3]),
        pltpu.make_async_copy(grad_mid_hbm, grad_mid, in_sem.at[4]),
    ]
    for n in range(3):
        src = wqkv_hbm.at[:, n * D : (n + 1) * D]
        late.append(pltpu.make_async_copy(src, wqkv.at[n], w_sem.at[n]))

    first = first_halves()
    low = low_heads()
    zero = jnp.zeros((T, 128), BF16)
    scale = HD**-0.5
    cosine, sine = rotary(lengths, inverse)
    sine = -sine
    query = lax.broadcasted_iota(jnp.int32, (T, T), 1)
    key = lax.broadcasted_iota(jnp.int32, (T, T), 0)
    bias[...] = jnp.where((key >= doc_start(lengths, query)) & (key <= query), 0.0, NEG)
    active[...] = of_doc(lengths, places(), heads)
    wait(loads)
    for copy in more:
        copy.start()

    def group_stores(g):
        at = columns(g, GW)
        return [
            copy
            for n in range(3)
            for copy in store_both(
                gqkv.at[n, :, at], thirds, (pl.ds(GQKV + T * n, T), at), group_sem.at[n, g]
            )
        ]

    def attend_back(g, carry):
        @pl.when(g == 1)
        def _():
            wait(more)
            start(late)

        grad_merged = nt(ga[...], wo[columns(g, GW), :])
        for pair in range(2):
            lanes = pl.ds(pl.multiple_of(g * GW + 128 * pair, 128), 128)
            head = 4 * g + 2 * pair + jnp.where(low, 0, 1)
            gm = grad_merged[:, 128 * pair : 128 * pair + 128]
            gm = jnp.where(head < active[...], gm, 0.0).astype(BF16)
            qp, kp, vp = qkv[0, :, lanes], qkv[1, :, lanes], qkv[2, :, lanes]
            k_turned = kp.T
            grad_values = jnp.zeros((T, 128), F32)
            grad_keys = jnp.zeros((T, 128), F32)
            grad_query = []
            for side in range(2):
                keep = low if side == 0 else ~low
                q_head = jnp.where(keep, qp, zero)
                gm_head = jnp.where(keep, gm, zero)
                s = nt(kp, q_head) * scale + bias[...]
                e = jnp.exp(s - jnp.max(s, 0, keepdims=True))
                p = e / jnp.sum(e, 0, keepdims=True)
                grad_p = nt(vp, gm_head)
                grad_values = grad_values + nn(p.astype(BF16), gm_head)
                grad_s = (p * (grad_p - jnp.sum(p * grad_p, 0, keepdims=True))).astype(BF16)
                grad_keys = grad_keys + nn(grad_s, q_head)
                grad_query.append(nn(k_turned[HD * side : HD * side + HD], grad_s))
            grad_q = jnp.concatenate(grad_query, 0).T * scale
            gqkv[0, :, lanes] = turned(grad_q, cosine, sine, first).astype(BF16)
            gqkv[1, :, lanes] = turned(grad_keys * scale, cosine, sine, first).astype(BF16)
            gqkv[2, :, lanes] = grad_values.astype(BF16)
        for copy in group_stores(g):
            copy.start()
        return carry

    lax.fori_loop(0, GROUPS, attend_back, 0)

    wait(late)
    grad_normed = nt(gqkv[0], wqkv[0]) + nt(gqkv[1], wqkv[1]) + nt(gqkv[2], wqkv[2])
    resid = tokens[...].astype(F32)
    rscale = lax.rsqrt(jnp.mean(resid * resid, -1, keepdims=True) + EPS)
    unit = resid * rscale
    gain_part = jnp.sum(grad_normed * unit, 0, keepdims=True)
    grad_unit = grad_normed * norm_gain[...]
    grad_mid[...] += rscale * (
        grad_unit - unit * jnp.mean(grad_unit * unit, -1, keepdims=True)
    )
    stores = [load(grad_mid, input_grad_out, out_sem.at[0])]

    item = lax.broadcasted_iota(jnp.int32, (128, 1), 0)
    count = jnp.zeros((128, 1), jnp.int32)
    for n in range(NEST):
        total = jnp.sum((bucket[...] == n).astype(jnp.int32), 1, keepdims=True)
        at = item - 3 - BITS * n
        bit = lax.shift_right_logical(total, jnp.clip(at, 0, BITS - 1)) & 1
        count = jnp.where((at >= 0) & (at < BITS), bit, count)
    wide = jnp.where(item == 0, gain_part, jnp.where(item == 1, parts[0:1, :], parts[1:2, :]))
    lines_f[...] = jnp.where(item < 3, wide, count.astype(F32)).T.reshape(lines_f.shape)
    for side, ref in enumerate(thirds):
        half = core if side == 0 else 1 - core
        for i in range(4):
            part = lines_f[:, i, :, half].reshape(128, 128).astype(BF16)
            lines[side, :, pl.ds(128 * i, 128)] = part
        dst = ref.at[pl.ds(LINES, 128), pl.ds(0, 512)]
        stores.append(load(lines.at[side], dst, out_sem.at[1 + side]))
    for g in range(GROUPS):
        wait(group_stores(g))
    wait(stores)


def back(lengths, heads, order, norm_gain, inverse, bucket, parts, *arrays):
    thirds = sds((THIRD, D), BF16)
    scratch = [
        sds((T, D), BF16),
        sds((3, T, D), BF16),
        sds((T, D), F32),
        sds((T, D), BF16),
        sds((3, D, D), BF16),
        sds((D, D), BF16),
        sds((3, T, D), BF16),
        sds((4, 4, 4, 2, 8, 128), F32),
        sds((2, 128, 512), BF16),
        sds((T, T), F32),
        sds((T, 128), jnp.int32),
    ]
    return call(
        back_kernel,
        "back",
        2 * T * D * 4 * D + 10 * 16 * T * T * 256,
        18 * MIB,
        32,
        in_specs=[smem()] * 3 + [vmem()] * 4 + [hbm()] * 6,
        out_specs=[hbm()] * 3,
        out_shape=[thirds, thirds, sds((T, D), F32)],
        scratch_shapes=[pltpu.VMEM(s.shape, s.dtype) for s in scratch]
        + [pltpu.SemaphoreType.DMA(s) for s in [(7,), (3,), (3, GROUPS, 2), (3,)]],
    )(lengths, heads, order, norm_gain, inverse, bucket, parts, *arrays)


def load_left(refs, at, rows, order, axis, left, sem):
    return [
        pltpu.make_async_copy(
            ref.at[pl.ds(at, rows), columns(order[axis, i], T)],
            left.at[pl.ds(rows * i, rows), pl.ds(T * m, T)],
            sem.at[i, m],
        )
        for i in range(4)
        for m, ref in enumerate(refs)
    ]


def load_right(refs, at, right, sem):
    return [
        pltpu.make_async_copy(ref.at[pl.ds(at, T), :], right.at[pl.ds(T * m, T), :], sem.at[m])
        for m, ref in enumerate(refs)
    ]


def store_out(out, at, sent, kept, sem):
    return [
        load(out.at[pl.ds(2 * side, 2), :, at], ref.at[:, :, at], sem.at[side])
        for side, ref in enumerate((sent, kept))
    ]


def down_grad_kernel(
    order, one, two, sent, kept, act, merged, gb, ga, out, act_sem, merged_sem, gb_sem, ga_sem, sem
):
    refs = (one, two)
    gb_loads = load_right(refs, GB, gb, gb_sem)
    act_loads = load_left(refs, ACT, 512, order, 0, act, act_sem)
    ga_loads = load_right(refs, GA, ga, ga_sem)
    merged_loads = load_left(refs, MERGED, 128, order, 0, merged, merged_sem)
    stages = [gb_loads + act_loads[:2], act_loads[2:4], act_loads[4:6], act_loads[6:]]
    stages.append(ga_loads + merged_loads)
    stores = []
    start(stages[0] + stages[1])
    wide = pl.ds(0, D)
    for i in range(4):
        wait(stages[i])
        start(stages[i + 2] if i < 3 else [])
        out[i, :, wide] = nn(act[pl.ds(512 * i, 512), :], gb[...]).astype(BF16)
        dst = (sent, kept)[i // 2].at[i % 2, :, wide]
        stores.append(load(out.at[i, :, wide], dst, sem.at[0, i]))
    wait(stages[4])
    part = nn(merged[...], ga[...])
    more = pl.ds(D, T)
    for i in range(4):
        rows = part[128 * i : 128 * i + 128].reshape(16, 8, D)
        quarters = [rows[:, :, T * q : T * q + T] for q in range(4)]
        out[i, :, more] = jnp.concatenate(quarters, 1).reshape(512, T).astype(BF16)
    stores += store_out(out, more, sent, kept, sem.at[1])
    wait(stores)


def down_grads(order, one, two):
    part = sds((2, 512, D + T), BF16)
    return call(
        down_grad_kernel,
        "down_and_out_grad",
        2 * T * D * (FF + D),
        10 * MIB,
        24,
        True,
        in_specs=[smem()] + [hbm()] * 2,
        out_specs=[hbm()] * 2,
        out_shape=[part, part],
        scratch_shapes=[
            pltpu.VMEM((FF // 2, 2 * T), BF16),
            pltpu.VMEM((512, 2 * T), BF16),
            pltpu.VMEM((2 * T, D), BF16),
            pltpu.VMEM((2 * T, D), BF16),
            pltpu.VMEM((4, 512, D + T), BF16),
            pltpu.SemaphoreType.DMA((4, 2)),
            pltpu.SemaphoreType.DMA((4, 2)),
            pltpu.SemaphoreType.DMA((2,)),
            pltpu.SemaphoreType.DMA((2,)),
            pltpu.SemaphoreType.DMA((2, 4)),
        ],
    )(order, one, two)


def up_and_qkv_kernel(
    order,
    one,
    two,
    three,
    four,
    after,
    up_sent,
    up_kept,
    qkv_sent,
    qkv_kept,
    zed,
    normed,
    gp,
    gqkv,
    lines,
    up_out,
    qkv_out,
    zed_sem,
    normed_sem,
    gp_sem,
    gqkv_sem,
    line_sem,
    up_sem,
    qkv_sem,
):
    refs = (one, two)
    late = (three, four)
    zed_loads = load_left(refs, ZED, 128, order, 1, zed, zed_sem)
    gp_loads = [load_right(refs, GP + T * n, gp.at[n], gp_sem.at[n]) for n in range(4)]
    line_loads = [
        pltpu.make_async_copy(
            ref.at[pl.ds(LINES, 128), columns(order[1, i], 128)],
            lines.at[i, m],
            line_sem.at[i, m],
        )
        for i in range(4)
        for m, ref in enumerate(late)
    ]
    normed_loads = load_left(refs, NORMED, 128, order, 2, normed, normed_sem)
    gqkv_loads = [load_right(late, GQKV + T * n, gqkv.at[n], gqkv_sem.at[n]) for n in range(3)]
    stages = [zed_loads + gp_loads[0], *gp_loads[1:], normed_loads + gqkv_loads[0]]
    stages += [gqkv_loads[1], gqkv_loads[2] + line_loads, []]
    stores = []
    start(stages[0] + stages[1])
    for n in range(4):
        wait(stages[n])
        start(stages[n + 2])
        at = pl.ds(n * D, D)
        up_out[:, :, at] = nn(zed[...], gp[n]).astype(BF16).reshape(4, 128, D)
        stores += store_out(up_out, at, up_sent, up_kept, up_sem.at[n])
    for n in range(3):
        wait(stages[4 + n])
        start(stages[6] if n == 0 else [])
        at = pl.ds(n * D, D)
        qkv_out[:, :, at] = nn(normed[...], gqkv[n]).astype(BF16).reshape(4, 128, D)
        stores += store_out(qkv_out, at, qkv_sent, qkv_kept, qkv_sem.at[n])
    at = pl.ds(FF, 128)
    up_out[:, :, at] = (lines[:, 0].astype(F32) + lines[:, 1].astype(F32)).astype(BF16)
    stores += store_out(up_out, at, up_sent, up_kept, up_sem.at[4])
    wait(stores)


def up_and_qkv_grads(order, one, two, three, four, after):
    up = sds((2, 128, FF + 128), BF16)
    qkv = sds((2, 128, 3 * D), BF16)
    return call(
        up_and_qkv_kernel,
        "up_and_qkv_grad",
        2 * T * D * (FF + 3 * D),
        16 * MIB,
        28,
        True,
        in_specs=[smem()] + [hbm()] * 5,
        out_specs=[hbm()] * 4,
        out_shape=[up, up, qkv, qkv],
        scratch_shapes=[
            pltpu.VMEM((512, 2 * T), BF16),
            pltpu.VMEM((512, 2 * T), BF16),
            pltpu.VMEM((4, 2 * T, D), BF16),
            pltpu.VMEM((3, 2 * T, D), BF16),
            pltpu.VMEM((4, 2, 128, 128), BF16),
            pltpu.VMEM((4, 128, FF + 128), BF16),
            pltpu.VMEM((4, 128, 3 * D), BF16),
            pltpu.SemaphoreType.DMA((4, 2)),
            pltpu.SemaphoreType.DMA((4, 2)),
            pltpu.SemaphoreType.DMA((4, 2)),
            pltpu.SemaphoreType.DMA((3, 2)),
            pltpu.SemaphoreType.DMA((4, 2)),
            pltpu.SemaphoreType.DMA((5, 2)),
            pltpu.SemaphoreType.DMA((3, 2)),
        ],
    )(order, one, two, three, four, after)


def swap_cores(array):
    return lax.ppermute(array, "c", [(0, 1), (1, 0)])


def pairs(mask_0, mask_1):
    perm = []
    for p in range(4):
        perm.append((2 * p, 2 * (p ^ mask_0)))
        perm.append((2 * p + 1, 2 * (p ^ mask_1) + 1))
    return perm


def block_order(axis):
    p = lax.axis_index(axis)
    core = lax.axis_index("c")
    return [p ^ (1 + 2 * core), p ^ 2, p, p ^ (3 - 2 * core)]


def ordered(token, *arrays):
    return lax.optimization_barrier((*arrays, token))[:-1]


def chain(sent, kept, axes, shape, finish):
    left = [axis for axis in ("y", "x", "z") if axis != axes[0]]
    for axis in axes:
        got = lax.ppermute(sent, (axis, "c"), pairs(1, 3))
        token = yield sent
        got, kept = ordered(token, got, kept)
        more = (got[1].astype(F32) + kept[1].astype(F32)).astype(BF16)
        got_2 = lax.ppermute(more, (axis, "c"), pairs(3, 1))
        token = yield more
        got, kept, got_2 = ordered(token, got, kept, got_2)
        terms = [got.reshape(2, *shape), kept.reshape(2, *shape), got_2.reshape(1, *shape)]
        if not left:
            finish(*terms)
            return
        following = axes[axes.index(axis) + 1]
        dim = left.index(following)
        left.pop(dim)
        shape = shape[:dim] + shape[dim + 1 :]

        def block(at):
            total = 0.0
            for term in terms:
                start = [0] * term.ndim
                start[1 + dim] = at
                sizes = (1,) + term.shape[1 : 1 + dim] + (1,) + term.shape[2 + dim :]
                total = total + lax.dynamic_slice(term, start, sizes).astype(F32)
            return total.reshape(shape)

        first, across, own, second = [block(at) for at in block_order(following)]
        sent = jnp.stack([first, across]).astype(BF16)
        kept = jnp.stack([own, second])


def total(terms, *at):
    return sum(term[(0, *at)].astype(F32) for term in terms)


def take_turns(token, turns, **chains):
    for steps in chains.values():
        next(steps)
    for turn in turns:
        token = next_step(chains[turn], token)


def next_step(steps, token):
    try:
        return steps.send(token)
    except StopIteration:
        return token


def body(
    tokens,
    norm_gain,
    qkv_weight,
    out_weight,
    ln_gain,
    ln_bias,
    up_weight,
    down_weight,
    buckets,
    router_prob,
    heads_active,
    doc_lengths,
    cotangent,
):
    core = lax.axis_index("c")
    orders = jnp.stack([jnp.stack(block_order(axis) + [core]) for axis in ("y", "x", "z")])
    orders = orders.astype(jnp.int32)
    norm_gain, ln_gain, ln_bias = [v.reshape(1, D) for v in (norm_gain, ln_gain, ln_bias)]
    router = router_prob.reshape(1, T)
    levels = buckets.reshape(1, T)
    inverse = np.tile(10000.0 ** (-2.0 * np.arange(HD // 2) / HD), 4).reshape(1, 128)
    inverse = jnp.asarray(inverse, F32)

    parts, first, first_other, second, second_other, qkv, grad_mid, mixed = front(
        doc_lengths,
        heads_active,
        orders,
        norm_gain,
        inverse,
        ln_gain,
        ln_bias,
        router,
        levels,
        tokens,
        cotangent,
        qkv_weight,
        out_weight,
        up_weight,
        down_weight,
    )
    first_2, second_2 = swap_cores(first_other), swap_cores(second_other)
    third, third_other, input_grad = back(
        doc_lengths,
        heads_active,
        orders,
        norm_gain,
        inverse,
        levels,
        parts,
        first,
        qkv,
        grad_mid,
        tokens,
        qkv_weight,
        out_weight,
    )
    third_2 = swap_cores(third_other)
    first_2, _ = lax.optimization_barrier((first_2, third))
    down_sent, down_kept = down_grads(orders, first, first_2)
    up_sent, up_kept, qkv_sent, qkv_kept = up_and_qkv_grads(
        orders, second, second_2, third, third_2, down_sent
    )

    every = slice(None)
    grads = {}

    def down_done(*terms):
        grads["down"] = total(terms, every, slice(0, D))
        out = total(terms, every, slice(D, D + T))
        grads["out"] = out.reshape(4, 8, T).transpose(1, 0, 2).reshape(8, D)

    def up_done(*terms):
        grads["up"] = total(terms, every, slice(0, FF))
        line = total(terms, every, slice(FF, FF + 128))
        grads["gains"] = [line[:, n] for n in range(3)]
        bits = line[0, 3 : 3 + BITS * NEST].astype(jnp.int32).reshape(NEST, BITS)
        grads["counts"] = jnp.sum(bits << jnp.arange(BITS, dtype=jnp.int32)[None, :], 1)

    def qkv_done(*terms):
        grads["qkv"] = total(terms)

    take_turns(
        qkv_sent,
        "dquqduqdqudqudqudu",
        d=chain(down_sent, down_kept, "yxz", (4, 4, 32, D + T), down_done),
        u=chain(up_sent, up_kept, "xyz", (4, 4, 8, FF + 128), up_done),
        q=chain(qkv_sent, qkv_kept, "zyx", (4, 4, 8, 3 * D), qkv_done),
    )
    gain_grad, ln_gain_grad, ln_bias_grad = grads["gains"]
    return (
        mixed,
        input_grad,
        gain_grad,
        grads["qkv"],
        grads["out"],
        ln_gain_grad,
        ln_bias_grad,
        grads["up"],
        grads["down"],
        grads["counts"],
    )


def solution(mesh):
    finer = Mesh(mesh.devices.reshape(4, 4, 4, 2), AX)
    rows = P(AX, None)
    return jax.shard_map(
        body,
        mesh=finer,
        in_specs=(rows, P(), P(), P(), P(), P(), P(), P(), rows, P(AX), rows, rows, rows),
        out_specs=(rows, rows, P(AX), rows, rows, P(AX), P(AX), rows, rows, P()),
        check_vma=False,
    )
```

time: 151 us -> 145 us (0.960)
  waiting for transfers between devices: 30.6 us -> 44.8 us
  starting transfers between devices: 41.7 us -> 28.7 us
  local copies, waits for them, and re-layouts: 9.91 us -> 3.61 us
  Pallas kernels: 56.5 us -> 52.2 us
  other arithmetic: 10.5 us -> 14.5 us
    ppermute x9, waiting for transfers between devices: 8.47 us -> 21.7 us  [chain(): got_2 = lax.ppermute(more, (axis, 'c'), pairs(3, 1))]
    ppermute x9, starting transfers between devices: 27.6 us -> 20.2 us  [chain(): got_2 = lax.ppermute(more, (axis, 'c'), pairs(3, 1))]
    slice x13 -> x1, local copies, waits for them, and re-layouts: 6.9 us -> 0.73 us  [up_done(): grads['gains'] = [line[:, n] for n in range(3)]]
    ppermute x9, waiting for transfers between devices: 17.4 us -> 23.1 us  [chain(): got = lax.ppermute(sent, (axis, 'c'), pairs(1, 3))]
    another operation x6 -> x12, other arithmetic: 0.28 us -> 5.54 us  [chain(): kept = jnp.stack([own, second])]
    ppermute x3, waiting for transfers between devices: 4.74 us -> 0.01 us  [swap_cores(): return lax.ppermute(array, 'c', [(0, 1), (1, 0)])]
    ppermute x9, starting transfers between devices: 12.3 us -> 7.62 us  [chain(): got = lax.ppermute(sent, (axis, 'c'), pairs(1, 3))]
    pallas_call x4, Pallas kernels: 56.5 us -> 52.2 us  [placed(): run(*(pltpu.with_memory_space_constraint(arg, pltpu.HBM) if in_hbm(spec)...]
  transfers between devices with their start and end apart: 21 -> 21, of which waited for: 10 -> 11; matrix products, arithmetic and copies ran while one was open for 10% -> 9% of each run, Pallas kernels for 15% -> 19%
where the time goes in v1:
time: 145 us
  Pallas kernels  52.2 us (36%)
  waiting for transfers between devices  44.8 us (31%)
  starting transfers between devices  28.7 us (20%)
  other arithmetic  14.5 us (10%)
  local copies, waits for them, and re-layouts  3.61 us (2%)
    pallas_call x4, Pallas kernels, placed(): run(*(pltpu.with_memory_space_constraint(arg, pltpu.HBM) if in_hbm(spec)...  52.2 us
    ppermute x9, waiting for transfers between devices, chain(): got = lax.ppermute(sent, (axis, 'c'), pairs(1, 3))  23.1 us
    ppermute x9, waiting for transfers between devices, chain(): got_2 = lax.ppermute(more, (axis, 'c'), pairs(3, 1))  21.7 us
    ppermute x9, starting transfers between devices, chain(): got_2 = lax.ppermute(more, (axis, 'c'), pairs(3, 1))  20.2 us
    ppermute x9, starting transfers between devices, chain(): got = lax.ppermute(sent, (axis, 'c'), pairs(1, 3))  7.62 us
    another operation x12, other arithmetic, chain(): kept = jnp.stack([own, second])  5.54 us
    convert_element_type x9, other arithmetic, chain(): more = (got[1].astype(F32) + kept[1].astype(F32)).astype(BF16)  4.75 us
  transfers between devices with their start and end apart: 21, of which 11 were waited for; matrix products, arithmetic and copies ran while one was open for 9% of the time, Pallas kernels for 19%

profile of v1, /device:TPU:0, one launch (start us, length us, event | category | flops | bytes accessed | tf_op | source)
XLA Modules:
  0.0 144.8 jit_solution(17954395087352983265)
XLA Ops:
  1.6 24.2 %front.1 = (f32[8,1024]{1,0:T(8,128)}, bf16[1152,1024]{1,0:T(8,128)(2,1)}, bf16[1152,1024]{1,0:T(8,128)(2,1)}, bf16[1280,1024]{1,0:T(8,128)(2,1)}, bf16[1280,102...) custom-call(s32[1,3]{1,0:T(1,128)} %lengths.3, s32[1,3]{1,0:T(1,128)} %heads.3, ...), custom_call_target="tpu_custom_call" | custom-call | flops 10737418240 | bytes 41943040 | tf_op jit(solution)/shard_map/front/pallas_call | solution.py:75
  26.4 0.7 copy-done.10
  27.1 14.0 %back.1 = (bf16[896,1024]{1,0:T(8,128)(2,1)}, bf16[896,1024]{1,0:T(8,128)(2,1)}, f32[256,1024]{1,0:T(8,128)}) custom-call(s32[1,3]{1,0:T(1,128)S(1)} %copy-done.4, s32[1,3]{1,0:T(1,128)S(1)} %copy-done.5, s32[3,5]{1,0:T(4,128)S(1)} %copy-done, f32[1,1024]{1,0:T(1,128)S(1)} %bitcast.148, f32[1,128]{1,0:T(1,128)S(1)} %copy-done.6, s32[1,256]{1,0:T(1,128)S(1)} %bitcast.150, ...), custom_call_target="tpu_custom_call" | custom-call | flops 4831838208 | bytes 18874368 | tf_op jit(solution)/shard_map/back/pallas_call | solution.py:75
  41.5 6.0 %down_and_out_grad.1 = (bf16[2,512,1280]{2,1,0:T(8,128)(2,1)}, bf16[2,512,1280]{2,1,0:T(8,128)(2,1)}) custom-call(s32[3,5]{1,0:T(4,128)S(1)} %copy-done, bf16[1152,1024]{1,0:T(8,128)(2,1)S(1)} %copy-done.9, bf16[1152,1024]{1,0:T(8,128)(2,1)S(1)} %collective-permute-done.2.two), custom_call_target="tpu_custom_call" | custom-call | flops 2684354560 | bytes 10485760 | tf_op jit(solution)/shard_map/down_and_out_grad/pallas_call | solution.py:75
  47.5 1.7 %collective-permute-start.5 = (bf16[2,512,1280]{2,1,0:T(8,128)(2,1)}, bf16[2,512,1280]{2,1,0:T(8,128)(2,1)}, u32[]{:S(2)}, u32[]{:S(2)}) collective-permute-start(bf16[2,512,1280]{2,1,0:T(8,128)(2,1)} %get-tuple-element.85.after), channel_id=1, source_target_pairs={{0,32},{1,97},{32,0},{33,65},{64,96},{65,33},{96,64},{97,1},{2,34}... | collective-permute-start | bytes 7864328 | tf_op jit(solution)/shard_map/ppermute | solution.py:797
  49.3 1.7 %copy-done.1 = bf16[2,512,1280]{2,1,0:T(8,128)(2,1)S(1)} copy-done((bf16[2,512,1280]{2,1,0:T(8,128)(2,1)S(1)}, bf16[2,512,1280]{2,1,0:T(8,128)(2,1)}, u32[]{:S(2)}) %copy-start.1) | copy-done | bytes 2621464
  51.0 8.0 %up_and_qkv_grad.1 = (bf16[2,128,4224]{2,1,0:T(8,128)(2,1)}, bf16[2,128,4224]{2,1,0:T(8,128)(2,1)}, bf16[2,128,3072]{2,1,0:T(8,128)(2,1)}, bf16[2,128,3072]{2,1,0:T(8,128)(2,1)}) custom-call(s32[3,5]{1,0:T(4,128)S(1)} %copy-done, bf16[1280,1024]{1,0:T(8,128)(2,1)S(1)} %copy-done.7, bf16[1280,1024]{1,0:T(8,128)(2,1)S(1)} %collective-permute-done.two, ...), custom_call_target="tpu_custom_call" | custom-call | flops 3758096384 | bytes 16777216 | tf_op jit(solution)/shard_map/up_and_qkv_grad/pallas_call | solution.py:75
  59.0 2.0 %collective-permute-start.4 = (bf16[2,128,3072]{2,1,0:T(8,128)(2,1)}, bf16[2,128,3072]{2,1,0:T(8,128)(2,1)}, u32[]{:S(2)}, u32[]{:S(2)}) collective-permute-start(bf16[2,128,3072]{2,1,0:T(8,128)(2,1)} %get-tuple-element.88), channel_id=1, source_target_pairs={{0,2},{1,7},{2,0},{3,5},{4,6},{5,3},{6,4},{7,1},{8,10},{9,15},{10,... | collective-permute-start | bytes 4718600 | tf_op jit(solution)/shard_map/ppermute | solution.py:797
  61.0 1.5 %collective-permute-start.3 = (bf16[2,128,4224]{2,1,0:T(8,128)(2,1)}, bf16[2,128,4224]{2,1,0:T(8,128)(2,1)}, u32[]{:S(2)}, u32[]{:S(2)}) collective-permute-start(bf16[2,128,4224]{2,1,0:T(8,128)(2,1)} %get-tuple-element.86), channel_id=1, source_target_pairs={{0,8},{1,25},{8,0},{9,17},{16,24},{17,9},{24,16},{25,1},{2,10},{3,... | collective-permute-start | bytes 6488072 | tf_op jit(solution)/shard_map/ppermute | solution.py:797
  62.5 17.1 %collective-permute-done.5 = bf16[2,512,1280]{2,1,0:T(8,128)(2,1)} collective-permute-done((bf16[2,512,1280]{2,1,0:T(8,128)(2,1)}, bf16[2,512,1280]{2,1,0:T(8,128)(2,1)}, u32[]{:S(2)}, u32[]{:S(2)}) %collective-permute-start.5) | collective-permute-done | bytes 2621472 | tf_op jit(solution)/shard_map/ppermute | solution.py:797
  79.6 1.7 %fusion = bf16[512,1280]{1,0:T(8,128)(2,1)S(1)} fusion(bf16[2,512,1280]{2,1,0:T(8,128)(2,1)S(1)} %copy-done.11, bf16[2,512,1280]{2,1,0:T(8,128)(2,1)} %collective-permute-done.5), kind=kLoop, calls=%fused_computation.3 | loop fusion | flops 2621440 | bytes 3932160 | tf_op jit(solution)/shard_map/convert_element_type | solution.py:800
  81.3 3.2 %collective-permute-start.7 = (bf16[512,1280]{1,0:T(8,128)(2,1)S(1)}, bf16[512,1280]{1,0:T(8,128)(2,1)S(1)}, u32[]{:S(2)}, u32[]{:S(2)}) collective-permute-start(bf16[512,1280]{1,0:T(8,128)(2,1)S(1)} %fusion), channel_id=1, source_target_pairs={{0,96},{1,33},{32,64},{33,1},{64,32},{65,97},{96,0},{97,65},{2,98}... | collective-permute-start | bytes 3932168 | tf_op jit(solution)/shard_map/ppermute | solution.py:801
  84.5 1.3 fusion.2
  85.8 4.1 %collective-permute-start.8 = (bf16[128,3072]{1,0:T(8,128)(2,1)S(1)}, bf16[128,3072]{1,0:T(8,128)(2,1)S(1)}, u32[]{:S(2)}, u32[]{:S(2)}) collective-permute-start(bf16[128,3072]{1,0:T(8,128)(2,1)S(1)} %fusion.2), channel_id=1, source_target_pairs={{0,6},{1,3},{2,4},{3,1},{4,2},{5,7},{6,0},{7,5},{8,14},{9,11},{10,... | collective-permute-start | bytes 2359304 | tf_op jit(solution)/shard_map/ppermute | solution.py:801
  90.0 1.5 %fusion.1 = bf16[128,4224]{1,0:T(8,128)(2,1)S(1)} fusion(bf16[2,128,4224]{2,1,0:T(8,128)(2,1)S(1)} %copy-done.12, bf16[2,128,4224]{2,1,0:T(8,128)(2,1)} %collective-permute-done.3), kind=kLoop, calls=%fused_computation.5 | loop fusion | flops 2162688 | bytes 3244032 | tf_op jit(solution)/shard_map/convert_element_type | solution.py:800
  91.5 2.8 %collective-permute-start.6 = (bf16[128,4224]{1,0:T(8,128)(2,1)S(1)}, bf16[128,4224]{1,0:T(8,128)(2,1)S(1)}, u32[]{:S(2)}, u32[]{:S(2)}) collective-permute-start(bf16[128,4224]{1,0:T(8,128)(2,1)S(1)} %fusion.1), channel_id=1, source_target_pairs={{0,24},{1,9},{8,16},{9,1},{16,8},{17,25},{24,0},{25,17},{2,26},{3,... | collective-permute-start | bytes 3244040 | tf_op jit(solution)/shard_map/ppermute | solution.py:801
  94.3 5.6 %collective-permute-done.8 = bf16[128,3072]{1,0:T(8,128)(2,1)S(1)} collective-permute-done((bf16[128,3072]{1,0:T(8,128)(2,1)S(1)}, bf16[128,3072]{1,0:T(8,128)(2,1)S(1)}, u32[]{:S(2)}, u32[]{:S(2)}) %collective-permute-start.8) | collective-permute-done | bytes 786464 | tf_op jit(solution)/shard_map/ppermute | solution.py:801
  99.9 1.5 %add_bitcast_fusion.5 = (f32[1,4,8,3072]{3,2,1,0:T(8,128)S(1)}, f32[1,4,8,3072]{3,2,1,0:T(8,128)S(1)}, bf16[1,4,8,3072]{3,2,1,0:T(8,128)(2,1)S(1)}, bf16[1,4,8,3072]{3,2,1,0:T(8,128)(2,1)S(1)}) fusion(bf16[1,4,4,8,3072]{4,3,2,1,0:T(8,128)(2,1)S(1)} %bitcast.156, s32[]{:T(128)S(6)} %select_n.28, bf16[2,4,4,8,3072]{4,3,2,1,0:T(8,128)(2,1)S(1)} %bitcast.153, ...), kind=kLoop, calls=%fused_computation.24 | loop fusion | flops 2162688 | bytes 3538960 | tf_op jit(solution)/shard_map/stack;reshape | solution.py:824
  101.8 1.8 %add_bitcast_fusion.1 = (f32[1,4,32,1280]{3,2,1,0:T(8,128)S(1)}, f32[1,4,32,1280]{3,2,1,0:T(8,128)S(1)}, bf16[1,4,32,1280]{3,2,1,0:T(8,128)(2,1)S(1)}, bf16[1,4,32,1280]{3,2,1,0:T(8,128)(2,1)S(1)}) fusion(bf16[1,4,4,32,1280]{4,3,2,1,0:T(8,128)(2,1)S(1)} %bitcast.154, s32[]{:T(128)S(6)} %select_n.30, bf16[2,4,4,32,1280]{4,3,2,1,0:T(8,128)(2,1)S(1)} %bitcast.151, ...), kind=kLoop, calls=%fused_computation.12 | loop fusion | flops 3604480 | bytes 5898256 | tf_op jit(solution)/shard_map/stack;reshape | solution.py:824
  103.7 1.6 %collective-permute-start.12 = (bf16[2,4,32,1280]{3,2,1,0:T(8,128)(2,1)S(1)}, bf16[2,4,32,1280]{3,2,1,0:T(8,128)(2,1)S(1)}, u32[]{:S(2)}, u32[]{:S(2)}) collective-permute-start(bf16[2,4,32,1280]{3,2,1,0:T(8,128)(2,1)S(1)} %pad_maximum_fusion.3), channel_id=1, source_target_pairs={{0,8},{1,25},{8,0},{9,17},{16,24},{17,9},{24,16},{25,1},{2,10},{3,... | collective-permute-start | bytes 1966088 | tf_op jit(solution)/shard_map/ppermute | solution.py:797
  105.3 5.5 %collective-permute-done.6 = bf16[128,4224]{1,0:T(8,128)(2,1)S(1)} collective-permute-done((bf16[128,4224]{1,0:T(8,128)(2,1)S(1)}, bf16[128,4224]{1,0:T(8,128)(2,1)S(1)}, u32[]{:S(2)}, u32[]{:S(2)}) %collective-permute-start.6) | collective-permute-done | bytes 1081376 | tf_op jit(solution)/shard_map/ppermute | solution.py:801
  110.8 1.6 %add_bitcast_fusion.3 = (f32[1,4,8,4224]{3,2,1,0:T(8,128)S(1)}, f32[1,4,8,4224]{3,2,1,0:T(8,128)S(1)}, bf16[1,4,8,4224]{3,2,1,0:T(8,128)(2,1)S(1)}, bf16[1,4,8,4224]{3,2,1,0:T(8,128)(2,1)S(1)}) fusion(bf16[1,4,4,8,4224]{4,3,2,1,0:T(8,128)(2,1)S(1)} %bitcast.155, s32[]{:T(128)S(6)} %select_n.28, bf16[2,4,4,8,4224]{4,3,2,1,0:T(8,128)(2,1)S(1)} %bitcast.152, ...), kind=kLoop, calls=%fused_computation.18 | loop fusion | flops 2973696 | bytes 4866064 | tf_op jit(solution)/shard_map/stack;reshape | solution.py:824
  113.3 1.1 collective-permute-done.12
  114.4 2.8 %collective-permute-start.15 = (bf16[4,32,1280]{2,1,0:T(8,128)(2,1)S(1)}, bf16[4,32,1280]{2,1,0:T(8,128)(2,1)S(1)}, u32[]{:S(2)}, u32[]{:S(2)}) collective-permute-start(bf16[4,32,1280]{2,1,0:T(8,128)(2,1)S(1)} %fusion.5), channel_id=1, source_target_pairs={{0,24},{1,9},{8,16},{9,1},{16,8},{17,25},{24,0},{25,17},{2,26},{3,... | collective-permute-start | bytes 983048 | tf_op jit(solution)/shard_map/ppermute | solution.py:801
  117.3 3.6 %collective-permute-done.11 = bf16[4,8,3072]{2,1,0:T(8,128)(2,1)S(1)} collective-permute-done((bf16[4,8,3072]{2,1,0:T(8,128)(2,1)S(1)}, bf16[4,8,3072]{2,1,0:T(8,128)(2,1)S(1)}, u32[]{:S(2)}, u32[]{:S(2)}) %collective-permute-start.11) | collective-permute-done | bytes 196640 | tf_op jit(solution)/shard_map/ppermute | solution.py:801
  122.6 1.1 collective-permute-done.15
  123.9 2.1 %collective-permute-done.14 = bf16[2,8,3072]{2,1,0:T(8,128)(2,1)S(1)} collective-permute-done((bf16[2,8,3072]{2,1,0:T(8,128)(2,1)S(1)}, bf16[2,8,3072]{2,1,0:T(8,128)(2,1)S(1)}, u32[]{:S(2)}, u32[]{:S(2)}) %collective-permute-start.14) | collective-permute-done | bytes 98336 | tf_op jit(solution)/shard_map/ppermute | solution.py:797
  126.1 2.7 %collective-permute-start.19 = (bf16[8,3072]{1,0:T(8,128)(2,1)S(1)}, bf16[8,3072]{1,0:T(8,128)(2,1)S(1)}, u32[]{:S(2)}, u32[]{:S(2)}) collective-permute-start(bf16[8,3072]{1,0:T(8,128)(2,1)S(1)} %fusion.30), channel_id=1, source_target_pairs={{0,24},{1,9},{8,16},{9,1},{16,8},{17,25},{24,0},{25,17},{2,26},{3,... | collective-permute-start | bytes 147464 | tf_op jit(solution)/shard_map/ppermute | solution.py:801
  128.8 1.0 collective-permute-done.13
  130.1 3.4 %collective-permute-start.20 = (bf16[32,1280]{1,0:T(8,128)(2,1)S(1)}, bf16[32,1280]{1,0:T(8,128)(2,1)S(1)}, u32[]{:S(2)}, u32[]{:S(2)}) collective-permute-start(bf16[32,1280]{1,0:T(8,128)(2,1)S(1)} %fusion.24), channel_id=1, source_target_pairs={{0,6},{1,3},{2,4},{3,1},{4,2},{5,7},{6,0},{7,5},{8,14},{9,11},{10,... | collective-permute-start | bytes 245768 | tf_op jit(solution)/shard_map/ppermute | solution.py:801
  133.5 2.2 %collective-permute-done.16 = bf16[2,8,4224]{2,1,0:T(8,128)(2,1)S(1)} collective-permute-done((bf16[2,8,4224]{2,1,0:T(8,128)(2,1)S(1)}, bf16[2,8,4224]{2,1,0:T(8,128)(2,1)S(1)}, u32[]{:S(2)}, u32[]{:S(2)}) %collective-permute-start.16) | collective-permute-done | bytes 135200 | tf_op jit(solution)/shard_map/ppermute | solution.py:797
  136.5 4.8 %collective-permute-done.18 = bf16[8,4224]{1,0:T(8,128)(2,1)S(1)} collective-permute-done((bf16[8,4224]{1,0:T(8,128)(2,1)S(1)}, bf16[8,4224]{1,0:T(8,128)(2,1)S(1)}, u32[]{:S(2)}, u32[]{:S(2)}) %collective-permute-start.18) | collective-permute-done | bytes 67616 | tf_op jit(solution)/shard_map/ppermute | solution.py:801
  (82 shorter events, 9.6 us)
Async XLA Ops:
  1.5 24.8 %copy-start = (s32[3,5]{1,0:T(4,128)S(1)}, s32[3,5]{1,0:T(4,128)}, u32[]{:S(2)}) copy-start(s32[3,5]{1,0:T(4,128)} %pad_add_fusion.order) | copy-start | bytes 184
  1.5 24.8 %copy-start.2 = (f32[1024]{0:T(1024)S(1)}, f32[1024]{0:T(1024)}, u32[]{:S(2)}) copy-start(f32[1024]{0:T(1024)} %param.15) | copy-start | bytes 12292
  1.5 24.8 %copy-start.3 = (s32[256,1]{0,1:T(1,128)S(1)}, s32[256,1]{0,1:T(1,128)}, u32[]{:S(2)}) copy-start(s32[256,1]{0,1:T(1,128)} %param.22) | copy-start | bytes 3076
  1.5 24.8 %copy-start.4 = (s32[1,3]{1,0:T(1,128)S(1)}, s32[1,3]{1,0:T(1,128)}, u32[]{:S(2)}) copy-start(s32[1,3]{1,0:T(1,128)} %lengths.3) | copy-start | bytes 40
  1.5 24.8 %copy-start.5 = (s32[1,3]{1,0:T(1,128)S(1)}, s32[1,3]{1,0:T(1,128)}, u32[]{:S(2)}) copy-start(s32[1,3]{1,0:T(1,128)} %heads.3) | copy-start | bytes 40
  1.5 24.8 %copy-start.6 = (f32[1,128]{1,0:T(1,128)S(1)}, f32[1,128]{1,0:T(1,128)}, u32[]{:S(2)}) copy-start(f32[1,128]{1,0:T(1,128)} %constant.27.clone.inverse) | copy-start | bytes 1540
  25.7 15.8 %collective-permute-start.2 = (bf16[1152,1024]{1,0:T(8,128)(2,1)}, bf16[1152,1024]{1,0:T(8,128)(2,1)S(1)}, u32[]{:S(2)}, u32[]{:S(2)}) collective-permute-start(bf16[1152,1024]{1,0:T(8,128)(2,1)} %get-tuple-element.83), channel_id=1, source_target_pairs={{0,1},{1,0},{2,3},{3,2},{4,5},{5,4},{6,7},{7,6},{8,9},{9,8},{10,11... | collective-permute-start | bytes 7077896 | tf_op jit(solution)/shard_map/ppermute | solution.py:773
  25.8 23.4 %collective-permute-start = (bf16[1280,1024]{1,0:T(8,128)(2,1)}, bf16[1280,1024]{1,0:T(8,128)(2,1)S(1)}, u32[]{:S(2)}, u32[]{:S(2)}) collective-permute-start(bf16[1280,1024]{1,0:T(8,128)(2,1)} %get-tuple-element.80), channel_id=1, source_target_pairs={{0,1},{1,0},{2,3},{3,2},{4,5},{5,4},{6,7},{7,6},{8,9},{9,8},{10,11... | collective-permute-start | bytes 7864328 | tf_op jit(solution)/shard_map/ppermute | solution.py:773
  27.1 14.4 %copy-start.9 = (bf16[1152,1024]{1,0:T(8,128)(2,1)S(1)}, bf16[1152,1024]{1,0:T(8,128)(2,1)}, u32[]{:S(2)}) copy-start(bf16[1152,1024]{1,0:T(8,128)(2,1)} %get-tuple-element.75.first_mine.one) | copy-start | bytes 7077892
  41.1 8.1 %collective-permute-start.1 = (bf16[896,1024]{1,0:T(8,128)(2,1)}, bf16[896,1024]{1,0:T(8,128)(2,1)S(1)}, u32[]{:S(2)}, u32[]{:S(2)}) collective-permute-start(bf16[896,1024]{1,0:T(8,128)(2,1)} %get-tuple-element.82), channel_id=1, source_target_pairs={{0,1},{1,0},{2,3},{3,2},{4,5},{5,4},{6,7},{7,6},{8,9},{9,8},{10,11... | collective-permute-start | bytes 5505032 | tf_op jit(solution)/shard_map/ppermute | solution.py:773
  41.5 7.8 %copy-start.7 = (bf16[1280,1024]{1,0:T(8,128)(2,1)S(1)}, bf16[1280,1024]{1,0:T(8,128)(2,1)}, u32[]{:S(2)}) copy-start(bf16[1280,1024]{1,0:T(8,128)(2,1)} %get-tuple-element.79.one) | copy-start | bytes 7864324
  41.5 7.8 %copy-start.8 = (bf16[896,1024]{1,0:T(8,128)(2,1)S(1)}, bf16[896,1024]{1,0:T(8,128)(2,1)}, u32[]{:S(2)}) copy-start(bf16[896,1024]{1,0:T(8,128)(2,1)} %get-tuple-element.81.three) | copy-start | bytes 5505028
  47.5 32.0 %collective-permute-start.5 = (bf16[2,512,1280]{2,1,0:T(8,128)(2,1)}, bf16[2,512,1280]{2,1,0:T(8,128)(2,1)}, u32[]{:S(2)}, u32[]{:S(2)}) collective-permute-start(bf16[2,512,1280]{2,1,0:T(8,128)(2,1)} %get-tuple-element.85.after), channel_id=1, source_target_pairs={{0,32},{1,97},{32,0},{33,65},{64,96},{65,33},{96,64},{97,1},{2,34}... | collective-permute-start | bytes 7864328 | tf_op jit(solution)/shard_map/ppermute | solution.py:797
  51.0 28.5 %copy-start.11 = (bf16[2,512,1280]{2,1,0:T(8,128)(2,1)S(1)}, bf16[2,512,1280]{2,1,0:T(8,128)(2,1)}, u32[]{:S(2)}) copy-start(bf16[2,512,1280]{2,1,0:T(8,128)(2,1)} %get-tuple-element.101) | copy-start | bytes 7864324
  59.0 25.5 %collective-permute-start.4 = (bf16[2,128,3072]{2,1,0:T(8,128)(2,1)}, bf16[2,128,3072]{2,1,0:T(8,128)(2,1)}, u32[]{:S(2)}, u32[]{:S(2)}) collective-permute-start(bf16[2,128,3072]{2,1,0:T(8,128)(2,1)} %get-tuple-element.88), channel_id=1, source_target_pairs={{0,2},{1,7},{2,0},{3,5},{4,6},{5,3},{6,4},{7,1},{8,10},{9,15},{10,... | collective-permute-start | bytes 4718600 | tf_op jit(solution)/shard_map/ppermute | solution.py:797
  61.0 29.0 %collective-permute-start.3 = (bf16[2,128,4224]{2,1,0:T(8,128)(2,1)}, bf16[2,128,4224]{2,1,0:T(8,128)(2,1)}, u32[]{:S(2)}, u32[]{:S(2)}) collective-permute-start(bf16[2,128,4224]{2,1,0:T(8,128)(2,1)} %get-tuple-element.86), channel_id=1, source_target_pairs={{0,8},{1,25},{8,0},{9,17},{16,24},{17,9},{24,16},{25,1},{2,10},{3,... | collective-permute-start | bytes 6488072 | tf_op jit(solution)/shard_map/ppermute | solution.py:797
  81.3 8.6 %copy-start.12 = (bf16[2,128,4224]{2,1,0:T(8,128)(2,1)S(1)}, bf16[2,128,4224]{2,1,0:T(8,128)(2,1)}, u32[]{:S(2)}) copy-start(bf16[2,128,4224]{2,1,0:T(8,128)(2,1)} %get-tuple-element.104) | copy-start | bytes 6488068
  81.3 20.5 %collective-permute-start.7 = (bf16[512,1280]{1,0:T(8,128)(2,1)S(1)}, bf16[512,1280]{1,0:T(8,128)(2,1)S(1)}, u32[]{:S(2)}, u32[]{:S(2)}) collective-permute-start(bf16[512,1280]{1,0:T(8,128)(2,1)S(1)} %fusion), channel_id=1, source_target_pairs={{0,96},{1,33},{32,64},{33,1},{64,32},{65,97},{96,0},{97,65},{2,98}... | collective-permute-start | bytes 3932168 | tf_op jit(solution)/shard_map/ppermute | solution.py:801
  85.8 14.1 %collective-permute-start.8 = (bf16[128,3072]{1,0:T(8,128)(2,1)S(1)}, bf16[128,3072]{1,0:T(8,128)(2,1)S(1)}, u32[]{:S(2)}, u32[]{:S(2)}) collective-permute-start(bf16[128,3072]{1,0:T(8,128)(2,1)S(1)} %fusion.2), channel_id=1, source_target_pairs={{0,6},{1,3},{2,4},{3,1},{4,2},{5,7},{6,0},{7,5},{8,14},{9,11},{10,... | collective-permute-start | bytes 2359304 | tf_op jit(solution)/shard_map/ppermute | solution.py:801
  91.5 19.3 %collective-permute-start.6 = (bf16[128,4224]{1,0:T(8,128)(2,1)S(1)}, bf16[128,4224]{1,0:T(8,128)(2,1)S(1)}, u32[]{:S(2)}, u32[]{:S(2)}) collective-permute-start(bf16[128,4224]{1,0:T(8,128)(2,1)S(1)} %fusion.1), channel_id=1, source_target_pairs={{0,24},{1,9},{8,16},{9,1},{16,8},{17,25},{24,0},{25,17},{2,26},{3,... | collective-permute-start | bytes 3244040 | tf_op jit(solution)/shard_map/ppermute | solution.py:801
  101.5 11.1 %collective-permute-start.10 = (bf16[2,4,8,3072]{3,2,1,0:T(8,128)(2,1)S(1)}, bf16[2,4,8,3072]{3,2,1,0:T(8,128)(2,1)S(1)}, u32[]{:S(2)}, u32[]{:S(2)}) collective-permute-start(bf16[2,4,8,3072]{3,2,1,0:T(8,128)(2,1)S(1)} %pad_maximum_fusion.5), channel_id=1, source_target_pairs={{0,32},{1,97},{32,0},{33,65},{64,96},{65,33},{96,64},{97,1},{2,34}... | collective-permute-start | bytes 1179656 | tf_op jit(solution)/shard_map/ppermute | solution.py:797
  103.7 10.7 %collective-permute-start.12 = (bf16[2,4,32,1280]{3,2,1,0:T(8,128)(2,1)S(1)}, bf16[2,4,32,1280]{3,2,1,0:T(8,128)(2,1)S(1)}, u32[]{:S(2)}, u32[]{:S(2)}) collective-permute-start(bf16[2,4,32,1280]{3,2,1,0:T(8,128)(2,1)S(1)} %pad_maximum_fusion.3), channel_id=1, source_target_pairs={{0,8},{1,25},{8,0},{9,17},{16,24},{17,9},{24,16},{25,1},{2,10},{3,... | collective-permute-start | bytes 1966088 | tf_op jit(solution)/shard_map/ppermute | solution.py:797
  112.5 9.4 %collective-permute-start.9 = (bf16[2,4,8,4224]{3,2,1,0:T(8,128)(2,1)S(1)}, bf16[2,4,8,4224]{3,2,1,0:T(8,128)(2,1)S(1)}, u32[]{:S(2)}, u32[]{:S(2)}) collective-permute-start(bf16[2,4,8,4224]{3,2,1,0:T(8,128)(2,1)S(1)} %pad_maximum_fusion.4), channel_id=1, source_target_pairs={{0,32},{1,97},{32,0},{33,65},{64,96},{65,33},{96,64},{97,1},{2,34}... | collective-permute-start | bytes 1622024 | tf_op jit(solution)/shard_map/ppermute | solution.py:797
  112.6 8.3 %collective-permute-start.11 = (bf16[4,8,3072]{2,1,0:T(8,128)(2,1)S(1)}, bf16[4,8,3072]{2,1,0:T(8,128)(2,1)S(1)}, u32[]{:S(2)}, u32[]{:S(2)}) collective-permute-start(bf16[4,8,3072]{2,1,0:T(8,128)(2,1)S(1)} %fusion.11), channel_id=1, source_target_pairs={{0,96},{1,33},{32,64},{33,1},{64,32},{65,97},{96,0},{97,65},{2,98}... | collective-permute-start | bytes 589832 | tf_op jit(solution)/shard_map/ppermute | solution.py:801
  114.4 9.3 %collective-permute-start.15 = (bf16[4,32,1280]{2,1,0:T(8,128)(2,1)S(1)}, bf16[4,32,1280]{2,1,0:T(8,128)(2,1)S(1)}, u32[]{:S(2)}, u32[]{:S(2)}) collective-permute-start(bf16[4,32,1280]{2,1,0:T(8,128)(2,1)S(1)} %fusion.5), channel_id=1, source_target_pairs={{0,24},{1,9},{8,16},{9,1},{16,8},{17,25},{24,0},{25,17},{2,26},{3,... | collective-permute-start | bytes 983048 | tf_op jit(solution)/shard_map/ppermute | solution.py:801
  121.0 5.1 %collective-permute-start.14 = (bf16[2,8,3072]{2,1,0:T(8,128)(2,1)S(1)}, bf16[2,8,3072]{2,1,0:T(8,128)(2,1)S(1)}, u32[]{:S(2)}, u32[]{:S(2)}) collective-permute-start(bf16[2,8,3072]{2,1,0:T(8,128)(2,1)S(1)} %pad_maximum_fusion.11), channel_id=1, source_target_pairs={{0,8},{1,25},{8,0},{9,17},{16,24},{17,9},{24,16},{25,1},{2,10},{3,... | collective-permute-start | bytes 294920 | tf_op jit(solution)/shard_map/ppermute | solution.py:797
  122.0 7.8 %collective-permute-start.13 = (bf16[4,8,4224]{2,1,0:T(8,128)(2,1)S(1)}, bf16[4,8,4224]{2,1,0:T(8,128)(2,1)S(1)}, u32[]{:S(2)}, u32[]{:S(2)}) collective-permute-start(bf16[4,8,4224]{2,1,0:T(8,128)(2,1)S(1)} %fusion.8), channel_id=1, source_target_pairs={{0,96},{1,33},{32,64},{33,1},{64,32},{65,97},{96,0},{97,65},{2,98}... | collective-permute-start | bytes 811016 | tf_op jit(solution)/shard_map/ppermute | solution.py:801
  123.9 6.2 %collective-permute-start.17 = (bf16[2,32,1280]{2,1,0:T(8,128)(2,1)S(1)}, bf16[2,32,1280]{2,1,0:T(8,128)(2,1)S(1)}, u32[]{:S(2)}, u32[]{:S(2)}) collective-permute-start(bf16[2,32,1280]{2,1,0:T(8,128)(2,1)S(1)} %pad_maximum_fusion.9), channel_id=1, source_target_pairs={{0,2},{1,7},{2,0},{3,5},{4,6},{5,3},{6,4},{7,1},{8,10},{9,15},{10,... | collective-permute-start | bytes 491528 | tf_op jit(solution)/shard_map/ppermute | solution.py:797
  126.1 7.4 %collective-permute-start.19 = (bf16[8,3072]{1,0:T(8,128)(2,1)S(1)}, bf16[8,3072]{1,0:T(8,128)(2,1)S(1)}, u32[]{:S(2)}, u32[]{:S(2)}) collective-permute-start(bf16[8,3072]{1,0:T(8,128)(2,1)S(1)} %fusion.30), channel_id=1, source_target_pairs={{0,24},{1,9},{8,16},{9,1},{16,8},{17,25},{24,0},{25,17},{2,26},{3,... | collective-permute-start | bytes 147464 | tf_op jit(solution)/shard_map/ppermute | solution.py:801
  129.9 5.8 %collective-permute-start.16 = (bf16[2,8,4224]{2,1,0:T(8,128)(2,1)S(1)}, bf16[2,8,4224]{2,1,0:T(8,128)(2,1)S(1)}, u32[]{:S(2)}, u32[]{:S(2)}) collective-permute-start(bf16[2,8,4224]{2,1,0:T(8,128)(2,1)S(1)} %pad_maximum_fusion.10), channel_id=1, source_target_pairs={{0,2},{1,7},{2,0},{3,5},{4,6},{5,3},{6,4},{7,1},{8,10},{9,15},{10,... | collective-permute-start | bytes 405512 | tf_op jit(solution)/shard_map/ppermute | solution.py:797
  130.1 13.4 %collective-permute-start.20 = (bf16[32,1280]{1,0:T(8,128)(2,1)S(1)}, bf16[32,1280]{1,0:T(8,128)(2,1)S(1)}, u32[]{:S(2)}, u32[]{:S(2)}) collective-permute-start(bf16[32,1280]{1,0:T(8,128)(2,1)S(1)} %fusion.24), channel_id=1, source_target_pairs={{0,6},{1,3},{2,4},{3,1},{4,2},{5,7},{6,0},{7,5},{8,14},{9,11},{10,... | collective-permute-start | bytes 245768 | tf_op jit(solution)/shard_map/ppermute | solution.py:801
  135.7 5.6 %collective-permute-start.18 = (bf16[8,4224]{1,0:T(8,128)(2,1)S(1)}, bf16[8,4224]{1,0:T(8,128)(2,1)S(1)}, u32[]{:S(2)}, u32[]{:S(2)}) collective-permute-start(bf16[8,4224]{1,0:T(8,128)(2,1)S(1)} %fusion.27), channel_id=1, source_target_pairs={{0,6},{1,3},{2,4},{3,1},{4,2},{5,7},{6,0},{7,5},{8,14},{9,11},{10,... | collective-permute-start | bytes 202760 | tf_op jit(solution)/shard_map/ppermute | solution.py:801
  (3 other events, 7.4 us)

commit v2 on v1

--- a/solution.py
+++ b/solution.py
@@ -20,9 +20,10 @@
 FF = 4096
 GW = 256
 GROUPS = D // GW
-ACT, GB, GA, MERGED, FIRST = 0, 512, 768, 1024, 1152
-GP, ZED, NORMED, SECOND = 0, 1024, 1152, 1280
-GQKV, LINES, THIRD = 0, 768, 896
+HEADS = GW // HD
+ACT, MERGED, FIRST_OWN, GB, GA, FIRST = 0, 512, 640, 640, 896, 1152
+ZED, NORMED, SECOND_OWN, GP, SECOND = 0, 128, 256, 256, 1280
+LINES, THIRD_OWN, GQKV, THIRD = 0, 128, 128, 896
 BITS = 9
 MIB = 1024 * 1024
 
@@ -55,7 +56,7 @@
     return pl.BlockSpec(memory_space=pltpu.HBM)
 
 
-def call(kernel, name, flops, moved, room, anywhere=False, **kw):
+def call(kernel, name, flops, moved, room, anywhere=(), **kw):
     def in_hbm(spec):
         return spec.memory_space == pltpu.HBM
 
@@ -75,9 +76,9 @@
         return run(
             *(
                 pltpu.with_memory_space_constraint(arg, pltpu.HBM)
-                if in_hbm(spec) and not anywhere
+                if in_hbm(spec) and n not in anywhere
                 else arg
-                for arg, spec in zip(args, kw["in_specs"])
+                for n, (arg, spec) in enumerate(zip(args, kw["in_specs"]))
             )
         )
 
@@ -88,8 +89,15 @@
     return lax.broadcasted_iota(jnp.int32, (T, 128), 1) % HD < HD // 2
 
 
-def low_heads():
-    return lax.broadcasted_iota(jnp.int32, (T, 128), 1) < HD
+def head_of(g):
+    return HEADS * g + lax.broadcasted_iota(jnp.int32, (T, GW), 1) // HD
+
+
+def by_head(x):
+    lane = lax.broadcasted_iota(jnp.int32, (T, GW), 1)
+    zero = jnp.zeros((T, GW), x.dtype)
+    own = [(lane >= HD * h) & (lane < HD * h + HD) for h in range(HEADS)]
+    return jnp.concatenate([jnp.where(keep, x, zero) for keep in own], 0)
 
 
 def turned(x, cosine, sine, first):
@@ -101,18 +109,19 @@
     return jnp.concatenate(parts, 1)
 
 
+def doc_ends(lengths):
+    return lengths[0, 0], lengths[0, 0] + lengths[0, 1]
+
+
 def doc_start(lengths, place):
-    end_0 = lengths[0, 0]
-    end_1 = end_0 + lengths[0, 1]
+    end_0, end_1 = doc_ends(lengths)
     return jnp.where(place >= end_1, end_1, jnp.where(place >= end_0, end_0, 0))
 
 
 def of_doc(lengths, place, values):
-    end_0 = lengths[0, 0]
-    end_1 = end_0 + lengths[0, 1]
-    return jnp.where(
-        place >= end_1, values[0, 2], jnp.where(place >= end_0, values[0, 1], values[0, 0])
-    )
+    end_0, end_1 = doc_ends(lengths)
+    late = jnp.where(place >= end_1, values[0, 2], values[0, 1])
+    return jnp.where(place >= end_0, late, values[0, 0])
 
 
 def normalized(middle):
@@ -121,6 +130,12 @@
     return shifted * rstd, rstd
 
 
+def block_order(axis):
+    p = lax.axis_index(axis)
+    core = lax.axis_index("c")
+    return [p ^ (1 + 2 * core), p ^ 2, p, p ^ (3 - 2 * core)]
+
+
 def load(src, dst, sem):
     copy = pltpu.make_async_copy(src, dst, sem)
     copy.start()
@@ -147,10 +162,6 @@
     return jnp.cos(phase), jnp.where(first_halves(), -sine, sine)
 
 
-def store_both(src, refs, at, sem):
-    return [pltpu.make_async_copy(src, ref.at[at], sem.at[side]) for side, ref in enumerate(refs)]
-
-
 def start(copies):
     for copy in copies:
         copy.start()
@@ -164,7 +175,6 @@
 def front_kernel(
     lengths,
     heads,
-    order,
     norm_gain,
     inverse,
     ln_gain,
@@ -177,14 +187,14 @@
     wo_hbm,
     up_hbm,
     down_hbm,
-    parts,
+    parts_out,
     first_mine,
     first_other,
     second_mine,
     second_other,
     qkv_out,
-    grad_mid_out,
     mixed_out,
+    parts,
     tokens,
     cot,
     wqkv,
@@ -202,7 +212,6 @@
     turned_f,
     left,
     middle,
-    grad_mid,
     ga,
     mixed,
     bias,
@@ -213,15 +222,15 @@
     act_sem,
     gp_sem,
     left_sem,
-    gb_sem,
-    ga_sem,
     out_sem,
 ):
-    core = order[0, 4]
+    core = lax.axis_index("c")
     firsts, seconds = (first_mine, first_other), (second_mine, second_other)
     loads = [load(tokens_hbm, tokens, in_sem.at[0])]
     for n in range(3):
-        loads.append(load(wqkv_hbm.at[:, n * D : (n + 1) * D], wqkv.at[n], in_sem.at[1 + n]))
+        src = wqkv_hbm.at[:, n * D : (n + 1) * D]
+        loads.append(pltpu.make_async_copy(src, wqkv.at[n], in_sem.at[1 + n]))
+    loads[1].start()
 
     def ffn_loads(j):
         at = columns(j, D)
@@ -248,18 +257,17 @@
             stores.append(load(left.at[side, n], dst, left_sem.at[side, n]))
 
     first = first_halves()
-    low = low_heads()
-    zero = jnp.zeros((T, 128), BF16)
-    scale = HD**-0.5
+    scale = jnp.asarray(HD**-0.5, BF16)
     cosine, sine = rotary(lengths, inverse)
     row = lax.broadcasted_iota(jnp.int32, (T, T), 0)
     col = lax.broadcasted_iota(jnp.int32, (T, T), 1)
     bias[...] = jnp.where((col >= doc_start(lengths, row)) & (col <= row), 0.0, NEG)
-    active[...] = of_doc(lengths, places(), heads)
+    active[...] = of_doc(lengths, lax.broadcasted_iota(jnp.int32, (T, GW), 0), heads)
     level[...] = upright(bucket[...])
     prob = upright(router[...])
 
     loads[0].wait()
+    start(loads[2:4])
     resid = tokens[...].astype(F32)
     rscale = lax.rsqrt(jnp.mean(resid * resid, -1, keepdims=True) + EPS)
     normed[...] = (resid * rscale * norm_gain[...]).astype(BF16)
@@ -276,18 +284,16 @@
     stores.append(load(qkv, qkv_out, out_sem.at[0]))
 
     def attend(g, carry):
-        for pair in range(2):
-            lanes = pl.ds(pl.multiple_of(g * GW + 128 * pair, 128), 128)
-            qp, kp, vp = qkv[0, :, lanes], qkv[1, :, lanes], qkv[2, :, lanes]
-            out = jnp.zeros((T, 128), F32)
-            for side in range(2):
-                keep = low if side == 0 else ~low
-                s = nt(qp, jnp.where(keep, kp, zero)) * scale + bias[...]
-                e = jnp.exp(s - jnp.max(s, -1, keepdims=True))
-                p = (e / jnp.sum(e, -1, keepdims=True)).astype(BF16)
-                out = out + nn(p, jnp.where(keep, vp, zero))
-            head = 4 * g + 2 * pair + jnp.where(low, 0, 1)
-            merged[:, lanes] = jnp.where(head < active[...], out, 0.0).astype(BF16)
+        at = columns(g, GW)
+        keys, values = by_head(qkv[1, :, at]), by_head(qkv[2, :, at])
+        s = nt(qkv[0, :, at] * scale, keys)
+        parts = []
+        for h in range(HEADS):
+            one = s[:, T * h : T * h + T] + bias[...]
+            e = jnp.exp(one - jnp.max(one, -1, keepdims=True))
+            parts.append((e / jnp.sum(e, -1, keepdims=True)).astype(BF16))
+        out = nn(jnp.concatenate(parts, 1), values)
+        merged[:, at] = jnp.where(head_of(g) < active[...], out, 0.0).astype(BF16)
 
         @pl.when((g > 0) & (g < NEST - 1))
         def _():
@@ -303,9 +309,7 @@
     zed[...] = (normed_mid * ln_gain[...] + ln_bias[...]).astype(BF16)
     loads[4].wait()
     gb[...] = (cot[...].astype(F32) * prob).astype(BF16)
-    both_gb = store_both(gb, firsts, (pl.ds(GB, T), slice(None)), gb_sem)
-    for copy in both_gb:
-        copy.start()
+    stores.append(load(gb, first_other.at[pl.ds(GB, T), :], out_sem.at[2]))
 
     def act_stores(j):
         at = (pl.ds(ACT, 512), columns(j, T))
@@ -314,9 +318,9 @@
             for side, ref in enumerate(firsts)
         ]
 
-    def gp_stores(j):
+    def gp_store(j):
         rows = pl.ds(pl.multiple_of(GP + T * j, T), T)
-        return store_both(gp.at[:, columns(j, D)], seconds, (rows, slice(None)), gp_sem.at[j])
+        return pltpu.make_async_copy(gp.at[:, columns(j, D)], second_other.at[rows, :], gp_sem.at[j])
 
     def hidden(j, carry):
         copy_up, copy_down = ffn_loads(j)
@@ -333,8 +337,7 @@
             copy.start()
         copy_down.wait()
         gp[:, at] = (nt(gb[...], down[at, :]) * 2.0 * r).astype(BF16)
-        for copy in gp_stores(j):
-            copy.start()
+        gp_store(j).start()
         return carry
 
     lax.fori_loop(0, NEST, hidden, 0)
@@ -357,22 +360,17 @@
         - normed_mid * jnp.mean(grad_norm * normed_mid, -1, keepdims=True)
     )
     ga[...] = grad.astype(BF16)
-    both_ga = store_both(ga, firsts, (pl.ds(GA, T), slice(None)), ga_sem)
-    for copy in both_ga:
-        copy.start()
-    grad_mid[...] = grad
-    stores.append(load(grad_mid, grad_mid_out, out_sem.at[2]))
+    stores.append(load(parts, parts_out, out_sem.at[3]))
+    stores.append(load(ga, first_other.at[pl.ds(GA, T), :], out_sem.at[4]))
     for j in range(NEST):
-        wait(act_stores(j) + gp_stores(j))
-    wait(both_gb + both_ga + stores)
-
-
-def front(lengths, heads, order, norm_gain, inverse, ln_gain, ln_bias, router, bucket, *arrays):
-    firsts = sds((FIRST, D), BF16)
-    seconds = sds((SECOND, D), BF16)
+        wait(act_stores(j) + [gp_store(j)])
+    wait(stores)
+
+
+def front(lengths, heads, norm_gain, inverse, ln_gain, ln_bias, router, bucket, *arrays):
     row_b = sds((T, D), BF16)
-    row_f = sds((T, D), F32)
     scratch = [
+        sds((8, D), F32),
         row_b,
         row_b,
         sds((3, D, D), BF16),
@@ -389,50 +387,55 @@
         sds((T, FF), BF16),
         sds((4, 4, 4, 2, 8, T), F32),
         sds((2, 3, 128, D), BF16),
-        row_f,
-        row_f,
+        sds((T, D), F32),
         row_b,
         row_b,
         sds((T, T), F32),
-        sds((T, 128), jnp.int32),
+        sds((T, GW), jnp.int32),
         sds((T, 1), jnp.int32),
     ]
-    semaphores = [(6,), (2, NEST), (2, NEST), (NEST, 2), (2, 3), (2,), (2,), (3,)]
+    semaphores = [(6,), (2, NEST), (2, NEST), (NEST,), (2, 3), (5,)]
     return call(
         front_kernel,
         "front",
         2 * T * D * (4 * D + 4 * FF),
         40 * MIB,
         58,
-        in_specs=[smem()] * 3 + [vmem()] * 6 + [hbm()] * 6,
-        out_specs=[vmem()] + [hbm()] * 7,
-        out_shape=[sds((8, D), F32), firsts, firsts, seconds, seconds, sds((3, T, D), BF16)]
-        + [row_f, row_b],
+        in_specs=[smem()] * 2 + [vmem()] * 6 + [hbm()] * 6,
+        out_specs=[hbm()] * 7,
+        out_shape=[
+            sds((8, D), F32),
+            sds((FIRST_OWN, D), BF16),
+            sds((FIRST, D), BF16),
+            sds((SECOND_OWN, D), BF16),
+            sds((SECOND, D), BF16),
+            sds((3, T, D), BF16),
+            row_b,
+        ],
         scratch_shapes=[pltpu.VMEM(s.shape, s.dtype) for s in scratch]
         + [pltpu.SemaphoreType.DMA(s) for s in semaphores],
-    )(lengths, heads, order, norm_gain, inverse, ln_gain, ln_bias, router, bucket, *arrays)
+    )(lengths, heads, norm_gain, inverse, ln_gain, ln_bias, router, bucket, *arrays)
 
 
 def back_kernel(
     lengths,
     heads,
-    order,
     norm_gain,
     inverse,
     bucket,
-    parts,
-    first_mine,
+    parts_hbm,
+    first_other,
     qkv_hbm,
-    grad_mid_hbm,
     tokens_hbm,
     wqkv_hbm,
     wo_hbm,
     third_mine,
     third_other,
     input_grad_out,
+    parts,
     ga,
     qkv,
-    grad_mid,
+    input_grad,
     tokens,
     wqkv,
     wo,
@@ -446,10 +449,10 @@
     group_sem,
     out_sem,
 ):
-    core = order[0, 4]
+    core = lax.axis_index("c")
     thirds = (third_mine, third_other)
     loads = [
-        load(first_mine.at[pl.ds(GA, T), :], ga, in_sem.at[0]),
+        load(first_other.at[pl.ds(GA, T), :], ga, in_sem.at[0]),
         load(wo_hbm.at[pl.ds(0, GW), :], wo.at[pl.ds(0, GW), :], in_sem.at[1]),
         load(qkv_hbm.at[:, :, pl.ds(0, GW)], qkv.at[:, :, pl.ds(0, GW)], in_sem.at[2]),
     ]
@@ -460,22 +463,20 @@
     ]
     late = [
         pltpu.make_async_copy(tokens_hbm, tokens, in_sem.at[3]),
-        pltpu.make_async_copy(grad_mid_hbm, grad_mid, in_sem.at[4]),
+        pltpu.make_async_copy(parts_hbm, parts, in_sem.at[7]),
     ]
     for n in range(3):
         src = wqkv_hbm.at[:, n * D : (n + 1) * D]
         late.append(pltpu.make_async_copy(src, wqkv.at[n], w_sem.at[n]))
 
     first = first_halves()
-    low = low_heads()
-    zero = jnp.zeros((T, 128), BF16)
-    scale = HD**-0.5
+    scale = jnp.asarray(HD**-0.5, BF16)
     cosine, sine = rotary(lengths, inverse)
     sine = -sine
     query = lax.broadcasted_iota(jnp.int32, (T, T), 1)
     key = lax.broadcasted_iota(jnp.int32, (T, T), 0)
     bias[...] = jnp.where((key >= doc_start(lengths, query)) & (key <= query), 0.0, NEG)
-    active[...] = of_doc(lengths, places(), heads)
+    active[...] = of_doc(lengths, lax.broadcasted_iota(jnp.int32, (T, GW), 0), heads)
     wait(loads)
     for copy in more:
         copy.start()
@@ -483,11 +484,10 @@
     def group_stores(g):
         at = columns(g, GW)
         return [
-            copy
+            pltpu.make_async_copy(
+                gqkv.at[n, :, at], third_other.at[pl.ds(GQKV + T * n, T), at], group_sem.at[n, g]
+            )
             for n in range(3)
-            for copy in store_both(
-                gqkv.at[n, :, at], thirds, (pl.ds(GQKV + T * n, T), at), group_sem.at[n, g]
-            )
         ]
 
     def attend_back(g, carry):
@@ -496,33 +496,31 @@
             wait(more)
             start(late)
 
-        grad_merged = nt(ga[...], wo[columns(g, GW), :])
-        for pair in range(2):
-            lanes = pl.ds(pl.multiple_of(g * GW + 128 * pair, 128), 128)
-            head = 4 * g + 2 * pair + jnp.where(low, 0, 1)
-            gm = grad_merged[:, 128 * pair : 128 * pair + 128]
-            gm = jnp.where(head < active[...], gm, 0.0).astype(BF16)
-            qp, kp, vp = qkv[0, :, lanes], qkv[1, :, lanes], qkv[2, :, lanes]
-            k_turned = kp.T
-            grad_values = jnp.zeros((T, 128), F32)
-            grad_keys = jnp.zeros((T, 128), F32)
-            grad_query = []
-            for side in range(2):
-                keep = low if side == 0 else ~low
-                q_head = jnp.where(keep, qp, zero)
-                gm_head = jnp.where(keep, gm, zero)
-                s = nt(kp, q_head) * scale + bias[...]
-                e = jnp.exp(s - jnp.max(s, 0, keepdims=True))
-                p = e / jnp.sum(e, 0, keepdims=True)
-                grad_p = nt(vp, gm_head)
-                grad_values = grad_values + nn(p.astype(BF16), gm_head)
-                grad_s = (p * (grad_p - jnp.sum(p * grad_p, 0, keepdims=True))).astype(BF16)
-                grad_keys = grad_keys + nn(grad_s, q_head)
-                grad_query.append(nn(k_turned[HD * side : HD * side + HD], grad_s))
-            grad_q = jnp.concatenate(grad_query, 0).T * scale
-            gqkv[0, :, lanes] = turned(grad_q, cosine, sine, first).astype(BF16)
-            gqkv[1, :, lanes] = turned(grad_keys * scale, cosine, sine, first).astype(BF16)
-            gqkv[2, :, lanes] = grad_values.astype(BF16)
+        at = columns(g, GW)
+        gm = nt(ga[...], wo[at, :])
+        gm = jnp.where(head_of(g) < active[...], gm, 0.0).astype(BF16)
+        gms, queries = by_head(gm), by_head(qkv[0, :, at] * scale)
+        k = qkv[1, :, at]
+        s = nt(k, queries)
+        grad_p = nt(qkv[2, :, at], gms)
+        parts_p, parts_s = [], []
+        for h in range(HEADS):
+            one = s[:, T * h : T * h + T] + bias[...]
+            e = jnp.exp(one - jnp.max(one, 0, keepdims=True))
+            p = e / jnp.sum(e, 0, keepdims=True)
+            grad = grad_p[:, T * h : T * h + T]
+            parts_p.append(p.astype(BF16))
+            grad = p * (grad - jnp.sum(p * grad, 0, keepdims=True))
+            parts_s.append(grad.astype(BF16))
+        grad_s = jnp.concatenate(parts_s, 1)
+        grad_v = nn(jnp.concatenate(parts_p, 1), gms)
+        grad_k = nn(grad_s, queries)
+        wide = nn((k * scale).T, grad_s)
+        grad_q = [wide[HD * h : HD * h + HD, T * h : T * h + T] for h in range(HEADS)]
+        grad_q = jnp.concatenate(grad_q, 0).T
+        gqkv[0, :, at] = turned(grad_q, cosine, sine, first).astype(BF16)
+        gqkv[1, :, at] = turned(grad_k, cosine, sine, first).astype(BF16)
+        gqkv[2, :, at] = grad_v.astype(BF16)
         for copy in group_stores(g):
             copy.start()
         return carry
@@ -536,10 +534,10 @@
     unit = resid * rscale
     gain_part = jnp.sum(grad_normed * unit, 0, keepdims=True)
     grad_unit = grad_normed * norm_gain[...]
-    grad_mid[...] += rscale * (
+    input_grad[...] = ga[...].astype(F32) + rscale * (
         grad_unit - unit * jnp.mean(grad_unit * unit, -1, keepdims=True)
     )
-    stores = [load(grad_mid, input_grad_out, out_sem.at[0])]
+    stores = [load(input_grad, input_grad_out, out_sem.at[0])]
 
     item = lax.broadcasted_iota(jnp.int32, (128, 1), 0)
     count = jnp.zeros((128, 1), jnp.int32)
@@ -562,9 +560,9 @@
     wait(stores)
 
 
-def back(lengths, heads, order, norm_gain, inverse, bucket, parts, *arrays):
-    thirds = sds((THIRD, D), BF16)
+def back(lengths, heads, norm_gain, inverse, bucket, parts, *arrays):
     scratch = [
+        sds((8, D), F32),
         sds((T, D), BF16),
         sds((3, T, D), BF16),
         sds((T, D), F32),
@@ -575,7 +573,7 @@
         sds((4, 4, 4, 2, 8, 128), F32),
         sds((2, 128, 512), BF16),
         sds((T, T), F32),
-        sds((T, 128), jnp.int32),
+        sds((T, GW), jnp.int32),
     ]
     return call(
         back_kernel,
@@ -583,22 +581,22 @@
         2 * T * D * 4 * D + 10 * 16 * T * T * 256,
         18 * MIB,
         32,
-        in_specs=[smem()] * 3 + [vmem()] * 4 + [hbm()] * 6,
+        in_specs=[smem()] * 2 + [vmem()] * 3 + [hbm()] * 6,
         out_specs=[hbm()] * 3,
-        out_shape=[thirds, thirds, sds((T, D), F32)],
+        out_shape=[sds((THIRD_OWN, D), BF16), sds((THIRD, D), BF16), sds((T, D), F32)],
         scratch_shapes=[pltpu.VMEM(s.shape, s.dtype) for s in scratch]
-        + [pltpu.SemaphoreType.DMA(s) for s in [(7,), (3,), (3, GROUPS, 2), (3,)]],
-    )(lengths, heads, order, norm_gain, inverse, bucket, parts, *arrays)
-
-
-def load_left(refs, at, rows, order, axis, left, sem):
+        + [pltpu.SemaphoreType.DMA(s) for s in [(8,), (3,), (3, GROUPS), (3,)]],
+    )(lengths, heads, norm_gain, inverse, bucket, parts, *arrays)
+
+
+def load_left(refs, at, rows, axis, left, sem):
     return [
         pltpu.make_async_copy(
-            ref.at[pl.ds(at, rows), columns(order[axis, i], T)],
+            ref.at[pl.ds(at, rows), columns(block, T)],
             left.at[pl.ds(rows * i, rows), pl.ds(T * m, T)],
             sem.at[i, m],
         )
-        for i in range(4)
+        for i, block in enumerate(block_order(axis))
         for m, ref in enumerate(refs)
     ]
 
@@ -618,13 +616,13 @@
 
 
 def down_grad_kernel(
-    order, one, two, sent, kept, act, merged, gb, ga, out, act_sem, merged_sem, gb_sem, ga_sem, sem
+    own, one, two, sent, kept, act, merged, gb, ga, out, act_sem, merged_sem, gb_sem, ga_sem, sem
 ):
-    refs = (one, two)
+    refs, split = (one, two), (own, two)
     gb_loads = load_right(refs, GB, gb, gb_sem)
-    act_loads = load_left(refs, ACT, 512, order, 0, act, act_sem)
+    act_loads = load_left(split, ACT, 512, "y", act, act_sem)
     ga_loads = load_right(refs, GA, ga, ga_sem)
-    merged_loads = load_left(refs, MERGED, 128, order, 0, merged, merged_sem)
+    merged_loads = load_left(split, MERGED, 128, "y", merged, merged_sem)
     stages = [gb_loads + act_loads[:2], act_loads[2:4], act_loads[4:6], act_loads[6:]]
     stages.append(ga_loads + merged_loads)
     stores = []
@@ -647,7 +645,7 @@
     wait(stores)
 
 
-def down_grads(order, one, two):
+def down_grads(own, one, two):
     part = sds((2, 512, D + T), BF16)
     return call(
         down_grad_kernel,
@@ -655,8 +653,8 @@
         2 * T * D * (FF + D),
         10 * MIB,
         24,
-        True,
-        in_specs=[smem()] + [hbm()] * 2,
+        (2,),
+        in_specs=[hbm()] * 3,
         out_specs=[hbm()] * 2,
         out_shape=[part, part],
         scratch_shapes=[
@@ -671,13 +669,14 @@
             pltpu.SemaphoreType.DMA((2,)),
             pltpu.SemaphoreType.DMA((2, 4)),
         ],
-    )(order, one, two)
+    )(own, one, two)
 
 
 def up_and_qkv_kernel(
-    order,
+    own,
     one,
     two,
+    late_own,
     three,
     four,
     after,
@@ -700,20 +699,20 @@
     up_sem,
     qkv_sem,
 ):
-    refs = (one, two)
+    refs, split = (one, two), (own, two)
     late = (three, four)
-    zed_loads = load_left(refs, ZED, 128, order, 1, zed, zed_sem)
+    zed_loads = load_left(split, ZED, 128, "x", zed, zed_sem)
     gp_loads = [load_right(refs, GP + T * n, gp.at[n], gp_sem.at[n]) for n in range(4)]
     line_loads = [
         pltpu.make_async_copy(
-            ref.at[pl.ds(LINES, 128), columns(order[1, i], 128)],
+            ref.at[pl.ds(LINES, 128), columns(block, 128)],
             lines.at[i, m],
             line_sem.at[i, m],
         )
-        for i in range(4)
-        for m, ref in enumerate(late)
+        for i, block in enumerate(block_order("x"))
+        for m, ref in enumerate((late_own, four))
     ]
-    normed_loads = load_left(refs, NORMED, 128, order, 2, normed, normed_sem)
+    normed_loads = load_left(split, NORMED, 128, "z", normed, normed_sem)
     gqkv_loads = [load_right(late, GQKV + T * n, gqkv.at[n], gqkv_sem.at[n]) for n in range(3)]
     stages = [zed_loads + gp_loads[0], *gp_loads[1:], normed_loads + gqkv_loads[0]]
     stages += [gqkv_loads[1], gqkv_loads[2] + line_loads, []]
@@ -737,7 +736,7 @@
     wait(stores)
 
 
-def up_and_qkv_grads(order, one, two, three, four, after):
+def up_and_qkv_grads(own, one, two, late_own, three, four, after):
     up = sds((2, 128, FF + 128), BF16)
     qkv = sds((2, 128, 3 * D), BF16)
     return call(
@@ -746,8 +745,8 @@
         2 * T * D * (FF + 3 * D),
         16 * MIB,
         28,
-        True,
-        in_specs=[smem()] + [hbm()] * 5,
+        (2, 5),
+        in_specs=[hbm()] * 7,
         out_specs=[hbm()] * 4,
         out_shape=[up, up, qkv, qkv],
         scratch_shapes=[
@@ -766,7 +765,7 @@
             pltpu.SemaphoreType.DMA((5, 2)),
             pltpu.SemaphoreType.DMA((3, 2)),
         ],
-    )(order, one, two, three, four, after)
+    )(own, one, two, late_own, three, four, after)
 
 
 def swap_cores(array):
@@ -779,12 +778,6 @@
         perm.append((2 * p, 2 * (p ^ mask_0)))
         perm.append((2 * p + 1, 2 * (p ^ mask_1) + 1))
     return perm
-
-
-def block_order(axis):
-    p = lax.axis_index(axis)
-    core = lax.axis_index("c")
-    return [p ^ (1 + 2 * core), p ^ 2, p, p ^ (3 - 2 * core)]
 
 
 def ordered(token, *arrays):
@@ -803,8 +796,7 @@
         got, kept, got_2 = ordered(token, got, kept, got_2)
         terms = [got.reshape(2, *shape), kept.reshape(2, *shape), got_2.reshape(1, *shape)]
         if not left:
-            finish(*terms)
-            return
+            return finish(*terms)
         following = axes[axes.index(axis) + 1]
         dim = left.index(following)
         left.pop(dim)
@@ -838,8 +830,8 @@
 def next_step(steps, token):
     try:
         return steps.send(token)
-    except StopIteration:
-        return token
+    except StopIteration as end:
+        return end.value
 
 
 def body(
@@ -857,19 +849,15 @@
     doc_lengths,
     cotangent,
 ):
-    core = lax.axis_index("c")
-    orders = jnp.stack([jnp.stack(block_order(axis) + [core]) for axis in ("y", "x", "z")])
-    orders = orders.astype(jnp.int32)
     norm_gain, ln_gain, ln_bias = [v.reshape(1, D) for v in (norm_gain, ln_gain, ln_bias)]
     router = router_prob.reshape(1, T)
     levels = buckets.reshape(1, T)
     inverse = np.tile(10000.0 ** (-2.0 * np.arange(HD // 2) / HD), 4).reshape(1, 128)
     inverse = jnp.asarray(inverse, F32)
 
-    parts, first, first_other, second, second_other, qkv, grad_mid, mixed = front(
+    parts, first, first_other, second, second_other, qkv, mixed = front(
         doc_lengths,
         heads_active,
-        orders,
         norm_gain,
         inverse,
         ln_gain,
@@ -887,23 +875,21 @@
     third, third_other, input_grad = back(
         doc_lengths,
         heads_active,
-        orders,
         norm_gain,
         inverse,
         levels,
         parts,
-        first,
+        first_other,
         qkv,
-        grad_mid,
         tokens,
         qkv_weight,
         out_weight,
     )
     third_2 = swap_cores(third_other)
     first_2, _ = lax.optimization_barrier((first_2, third))
-    down_sent, down_kept = down_grads(orders, first, first_2)
+    down_sent, down_kept = down_grads(first, first_other, first_2)
     up_sent, up_kept, qkv_sent, qkv_kept = up_and_qkv_grads(
-        orders, second, second_2, third, third_2, down_sent
+        second, second_other, second_2, third, third_other, third_2, down_sent
     )
 
     every = slice(None)
@@ -913,6 +899,8 @@
         grads["down"] = total(terms, every, slice(0, D))
         out = total(terms, every, slice(D, D + T))
         grads["out"] = out.reshape(4, 8, T).transpose(1, 0, 2).reshape(8, D)
+        grads["down"], grads["out"] = lax.optimization_barrier((grads["down"], grads["out"]))
+        return grads["out"]
 
     def up_done(*terms):
         grads["up"] = total(terms, every, slice(0, FF))
@@ -920,13 +908,17 @@
         grads["gains"] = [line[:, n] for n in range(3)]
         bits = line[0, 3 : 3 + BITS * NEST].astype(jnp.int32).reshape(NEST, BITS)
         grads["counts"] = jnp.sum(bits << jnp.arange(BITS, dtype=jnp.int32)[None, :], 1)
+        done = (grads["up"], grads["counts"], *grads["gains"])
+        grads["up"], grads["counts"], *grads["gains"] = lax.optimization_barrier(done)
+        return grads["up"]
 
     def qkv_done(*terms):
         grads["qkv"] = total(terms)
+        return grads["qkv"]
 
     take_turns(
         qkv_sent,
-        "dquqduqdqudqudqudu",
+        "dquqduqduqdudquduq",
         d=chain(down_sent, down_kept, "yxz", (4, 4, 32, D + T), down_done),
         u=chain(up_sent, up_kept, "xyz", (4, 4, 8, FF + 128), up_done),
         q=chain(qkv_sent, qkv_kept, "zyx", (4, 4, 8, 3 * D), qkv_done),

time: 145 us -> 142 us (0.979)
  waiting for transfers between devices: 44.8 us -> 48.6 us
  local copies, waits for them, and re-layouts: 3.61 us -> 0.85 us
  Pallas kernels: 52.2 us -> 50.1 us
    ppermute x9, waiting for transfers between devices: 23.1 us -> 27.7 us  [chain(): got = lax.ppermute(sent, (axis, 'c'), pairs(1, 3))]
    unnamed x28 -> x16, local copies, waits for them, and re-layouts: 2.55 us -> 0.04 us
    pallas_call x4, Pallas kernels: 52.2 us -> 50.1 us  [placed(): run(*(pltpu.with_memory_space_constraint(arg, pltpu.HBM) if in_hbm(spec)...]
  transfers between devices with their start and end apart: 21 -> 21, of which waited for: 11 -> 8; matrix products, arithmetic and copies ran while one was open for 9% -> 10% of each run, Pallas kernels for 19% -> 19%
where the time goes in v2:
time: 142 us
  Pallas kernels  50.1 us (35%)
  waiting for transfers between devices  48.6 us (34%)
  starting transfers between devices  27.4 us (19%)
  other arithmetic  13.9 us (10%)
    pallas_call x4, Pallas kernels, placed(): run(*(pltpu.with_memory_space_constraint(arg, pltpu.HBM) if in_hbm(spec)...  50.1 us
    ppermute x9, waiting for transfers between devices, chain(): got = lax.ppermute(sent, (axis, 'c'), pairs(1, 3))  27.7 us
    ppermute x9, waiting for transfers between devices, chain(): got_2 = lax.ppermute(more, (axis, 'c'), pairs(3, 1))  20.9 us
    ppermute x9, starting transfers between devices, chain(): got_2 = lax.ppermute(more, (axis, 'c'), pairs(3, 1))  18.8 us
    ppermute x9, starting transfers between devices, chain(): got = lax.ppermute(sent, (axis, 'c'), pairs(1, 3))  7.65 us
    another operation x12, other arithmetic, chain(): kept = jnp.stack([own, second])  5.57 us
    convert_element_type x9, other arithmetic, chain(): more = (got[1].astype(F32) + kept[1].astype(F32)).astype(BF16)  4.74 us
  transfers between devices with their start and end apart: 21, of which 8 were waited for; matrix products, arithmetic and copies ran while one was open for 10% of the time, Pallas kernels for 19%

profile of v2, /device:TPU:0, one launch (start us, length us, event | category | flops | bytes accessed | tf_op | source)
XLA Modules:
  0.0 141.9 jit_solution(2681578752903376750)
XLA Ops:
  0.7 23.8 %front.1 = (f32[8,1024]{1,0:T(8,128)}, bf16[640,1024]{1,0:T(8,128)(2,1)}, bf16[1152,1024]{1,0:T(8,128)(2,1)}, bf16[256,1024]{1,0:T(8,128)(2,1)}, bf16[1280,1024]...) custom-call(s32[1,3]{1,0:T(1,128)} %lengths.3, s32[1,3]{1,0:T(1,128)} %heads.3, ...), custom_call_target="tpu_custom_call" | custom-call | flops 10737418240 | bytes 41943040 | tf_op jit(solution)/shard_map/front/pallas_call | solution.py:76
  25.1 12.0 %back.1 = (bf16[128,1024]{1,0:T(8,128)(2,1)}, bf16[896,1024]{1,0:T(8,128)(2,1)}, f32[256,1024]{1,0:T(8,128)}) custom-call(s32[1,3]{1,0:T(1,128)S(1)} %copy-done.2, s32[1,3]{1,0:T(1,128)S(1)} %copy-done.3, f32[1,1024]{1,0:T(1,128)S(1)} %bitcast.132, f32[1,128]{1,0:T(1,128)S(1)} %copy-done.4, s32[1,256]{1,0:T(1,128)S(1)} %bitcast.134, ...), custom_call_target="tpu_custom_call" | custom-call | flops 4831838208 | bytes 18874368 | tf_op jit(solution)/shard_map/back/pallas_call | solution.py:76
  37.5 6.2 %down_and_out_grad.1 = (bf16[2,512,1280]{2,1,0:T(8,128)(2,1)}, bf16[2,512,1280]{2,1,0:T(8,128)(2,1)}) custom-call(bf16[640,1024]{1,0:T(8,128)(2,1)} %get-tuple-element.88.own, bf16[1152,1024]{1,0:T(8,128)(2,1)} %get-tuple-element.81.first_other.one, bf16[1152,1024]{1,0:T(8,128)(2,1)S(1)} %collective-permute-done.2.two), custom_call_target="tpu_custom_call" | custom-call | flops 2684354560 | bytes 10485760 | tf_op jit(solution)/shard_map/down_and_out_grad/pallas_call | solution.py:76
  43.6 1.7 %collective-permute-start.5 = (bf16[2,512,1280]{2,1,0:T(8,128)(2,1)}, bf16[2,512,1280]{2,1,0:T(8,128)(2,1)}, u32[]{:S(2)}, u32[]{:S(2)}) collective-permute-start(bf16[2,512,1280]{2,1,0:T(8,128)(2,1)} %get-tuple-element.90.after), channel_id=1, source_target_pairs={{0,32},{1,97},{32,0},{33,65},{64,96},{65,33},{96,64},{97,1},{2,34}... | collective-permute-start | bytes 7864328 | tf_op jit(solution)/shard_map/ppermute | solution.py:790
  45.4 8.2 %up_and_qkv_grad.1 = (bf16[2,128,4224]{2,1,0:T(8,128)(2,1)}, bf16[2,128,4224]{2,1,0:T(8,128)(2,1)}, bf16[2,128,3072]{2,1,0:T(8,128)(2,1)}, bf16[2,128,3072]{2,1,0:T(8,128)(2,1)}) custom-call(bf16[256,1024]{1,0:T(8,128)(2,1)} %get-tuple-element.84.own, bf16[1280,1024]{1,0:T(8,128)(2,1)} %get-tuple-element.85.one, ...), custom_call_target="tpu_custom_call" | custom-call | flops 3758096384 | bytes 16777216 | tf_op jit(solution)/shard_map/up_and_qkv_grad/pallas_call | solution.py:76
  53.6 2.0 %collective-permute-start.4 = (bf16[2,128,3072]{2,1,0:T(8,128)(2,1)}, bf16[2,128,3072]{2,1,0:T(8,128)(2,1)}, u32[]{:S(2)}, u32[]{:S(2)}) collective-permute-start(bf16[2,128,3072]{2,1,0:T(8,128)(2,1)} %get-tuple-element.93), channel_id=1, source_target_pairs={{0,2},{1,7},{2,0},{3,5},{4,6},{5,3},{6,4},{7,1},{8,10},{9,15},{10,... | collective-permute-start | bytes 4718600 | tf_op jit(solution)/shard_map/ppermute | solution.py:790
  55.6 1.5 %collective-permute-start.3 = (bf16[2,128,4224]{2,1,0:T(8,128)(2,1)}, bf16[2,128,4224]{2,1,0:T(8,128)(2,1)}, u32[]{:S(2)}, u32[]{:S(2)}) collective-permute-start(bf16[2,128,4224]{2,1,0:T(8,128)(2,1)} %get-tuple-element.91), channel_id=1, source_target_pairs={{0,8},{1,25},{8,0},{9,17},{16,24},{17,9},{24,16},{25,1},{2,10},{3,... | collective-permute-start | bytes 6488072 | tf_op jit(solution)/shard_map/ppermute | solution.py:790
  57.1 18.6 %collective-permute-done.5 = bf16[2,512,1280]{2,1,0:T(8,128)(2,1)} collective-permute-done((bf16[2,512,1280]{2,1,0:T(8,128)(2,1)}, bf16[2,512,1280]{2,1,0:T(8,128)(2,1)}, u32[]{:S(2)}, u32[]{:S(2)}) %collective-permute-start.5) | collective-permute-done | bytes 2621472 | tf_op jit(solution)/shard_map/ppermute | solution.py:790
  75.7 1.7 %fusion = bf16[512,1280]{1,0:T(8,128)(2,1)S(1)} fusion(bf16[2,512,1280]{2,1,0:T(8,128)(2,1)S(1)} %copy-done.5, bf16[2,512,1280]{2,1,0:T(8,128)(2,1)} %collective-permute-done.5), kind=kLoop, calls=%fused_computation.3 | loop fusion | flops 2621440 | bytes 3932160 | tf_op jit(solution)/shard_map/convert_element_type | solution.py:793
  77.4 3.4 %collective-permute-start.7 = (bf16[512,1280]{1,0:T(8,128)(2,1)S(1)}, bf16[512,1280]{1,0:T(8,128)(2,1)S(1)}, u32[]{:S(2)}, u32[]{:S(2)}) collective-permute-start(bf16[512,1280]{1,0:T(8,128)(2,1)S(1)} %fusion), channel_id=1, source_target_pairs={{0,96},{1,33},{32,64},{33,1},{64,32},{65,97},{96,0},{97,65},{2,98}... | collective-permute-start | bytes 3932168 | tf_op jit(solution)/shard_map/ppermute | solution.py:794
  80.8 1.3 fusion.2
  82.2 4.1 %collective-permute-start.8 = (bf16[128,3072]{1,0:T(8,128)(2,1)S(1)}, bf16[128,3072]{1,0:T(8,128)(2,1)S(1)}, u32[]{:S(2)}, u32[]{:S(2)}) collective-permute-start(bf16[128,3072]{1,0:T(8,128)(2,1)S(1)} %fusion.2), channel_id=1, source_target_pairs={{0,6},{1,3},{2,4},{3,1},{4,2},{5,7},{6,0},{7,5},{8,14},{9,11},{10,... | collective-permute-start | bytes 2359304 | tf_op jit(solution)/shard_map/ppermute | solution.py:794
  86.3 1.5 %fusion.1 = bf16[128,4224]{1,0:T(8,128)(2,1)S(1)} fusion(bf16[2,128,4224]{2,1,0:T(8,128)(2,1)S(1)} %copy-done.6, bf16[2,128,4224]{2,1,0:T(8,128)(2,1)} %collective-permute-done.3), kind=kLoop, calls=%fused_computation.5 | loop fusion | flops 2162688 | bytes 3244032 | tf_op jit(solution)/shard_map/convert_element_type | solution.py:793
  87.8 2.8 %collective-permute-start.6 = (bf16[128,4224]{1,0:T(8,128)(2,1)S(1)}, bf16[128,4224]{1,0:T(8,128)(2,1)S(1)}, u32[]{:S(2)}, u32[]{:S(2)}) collective-permute-start(bf16[128,4224]{1,0:T(8,128)(2,1)S(1)} %fusion.1), channel_id=1, source_target_pairs={{0,24},{1,9},{8,16},{9,1},{16,8},{17,25},{24,0},{25,17},{2,26},{3,... | collective-permute-start | bytes 3244040 | tf_op jit(solution)/shard_map/ppermute | solution.py:794
  90.6 5.6 %collective-permute-done.8 = bf16[128,3072]{1,0:T(8,128)(2,1)S(1)} collective-permute-done((bf16[128,3072]{1,0:T(8,128)(2,1)S(1)}, bf16[128,3072]{1,0:T(8,128)(2,1)S(1)}, u32[]{:S(2)}, u32[]{:S(2)}) %collective-permute-start.8) | collective-permute-done | bytes 786464 | tf_op jit(solution)/shard_map/ppermute | solution.py:794
  96.2 1.5 %add_bitcast_fusion.5 = (f32[1,4,8,3072]{3,2,1,0:T(8,128)S(1)}, f32[1,4,8,3072]{3,2,1,0:T(8,128)S(1)}, bf16[1,4,8,3072]{3,2,1,0:T(8,128)(2,1)S(1)}, bf16[1,4,8,3072]{3,2,1,0:T(8,128)(2,1)S(1)}) fusion(bf16[1,4,4,8,3072]{4,3,2,1,0:T(8,128)(2,1)S(1)} %bitcast.140, s32[]{:T(128)S(6)} %select_n.28, bf16[2,4,4,8,3072]{4,3,2,1,0:T(8,128)(2,1)S(1)} %bitcast.137, ...), kind=kLoop, calls=%fused_computation.24 | loop fusion | flops 2162688 | bytes 3538960 | tf_op jit(solution)/shard_map/stack;reshape | solution.py:816
  98.1 1.8 %add_bitcast_fusion.1 = (f32[1,4,32,1280]{3,2,1,0:T(8,128)S(1)}, f32[1,4,32,1280]{3,2,1,0:T(8,128)S(1)}, bf16[1,4,32,1280]{3,2,1,0:T(8,128)(2,1)S(1)}, bf16[1,4,32,1280]{3,2,1,0:T(8,128)(2,1)S(1)}) fusion(bf16[1,4,4,32,1280]{4,3,2,1,0:T(8,128)(2,1)S(1)} %bitcast.138, s32[]{:T(128)S(6)} %select_n.30, bf16[2,4,4,32,1280]{4,3,2,1,0:T(8,128)(2,1)S(1)} %bitcast.135, ...), kind=kLoop, calls=%fused_computation.12 | loop fusion | flops 3604480 | bytes 5898256 | tf_op jit(solution)/shard_map/stack;reshape | solution.py:816
  100.0 1.6 %collective-permute-start.10 = (bf16[2,4,32,1280]{3,2,1,0:T(8,128)(2,1)S(1)}, bf16[2,4,32,1280]{3,2,1,0:T(8,128)(2,1)S(1)}, u32[]{:S(2)}, u32[]{:S(2)}) collective-permute-start(bf16[2,4,32,1280]{3,2,1,0:T(8,128)(2,1)S(1)} %pad_maximum_fusion.3), channel_id=1, source_target_pairs={{0,8},{1,25},{8,0},{9,17},{16,24},{17,9},{24,16},{25,1},{2,10},{3,... | collective-permute-start | bytes 1966088 | tf_op jit(solution)/shard_map/ppermute | solution.py:790
  101.6 5.5 %collective-permute-done.6 = bf16[128,4224]{1,0:T(8,128)(2,1)S(1)} collective-permute-done((bf16[128,4224]{1,0:T(8,128)(2,1)S(1)}, bf16[128,4224]{1,0:T(8,128)(2,1)S(1)}, u32[]{:S(2)}, u32[]{:S(2)}) %collective-permute-start.6) | collective-permute-done | bytes 1081376 | tf_op jit(solution)/shard_map/ppermute | solution.py:794
  107.1 1.6 %add_bitcast_fusion.3 = (f32[1,4,8,4224]{3,2,1,0:T(8,128)S(1)}, f32[1,4,8,4224]{3,2,1,0:T(8,128)S(1)}, bf16[1,4,8,4224]{3,2,1,0:T(8,128)(2,1)S(1)}, bf16[1,4,8,4224]{3,2,1,0:T(8,128)(2,1)S(1)}) fusion(bf16[1,4,4,8,4224]{4,3,2,1,0:T(8,128)(2,1)S(1)} %bitcast.139, s32[]{:T(128)S(6)} %select_n.28, bf16[2,4,4,8,4224]{4,3,2,1,0:T(8,128)(2,1)S(1)} %bitcast.136, ...), kind=kLoop, calls=%fused_computation.18 | loop fusion | flops 2973696 | bytes 4866064 | tf_op jit(solution)/shard_map/stack;reshape | solution.py:816
  109.2 1.5 %collective-permute-done.10 = bf16[2,4,32,1280]{3,2,1,0:T(8,128)(2,1)S(1)} collective-permute-done((bf16[2,4,32,1280]{3,2,1,0:T(8,128)(2,1)S(1)}, bf16[2,4,32,1280]{3,2,1,0:T(8,128)(2,1)S(1)}, u32[]{:S(2)}, u32[]{:S(2)}) %collective-permute-start.10) | collective-permute-done | bytes 655392 | tf_op jit(solution)/shard_map/ppermute | solution.py:790
  110.8 2.8 %collective-permute-start.13 = (bf16[4,32,1280]{2,1,0:T(8,128)(2,1)S(1)}, bf16[4,32,1280]{2,1,0:T(8,128)(2,1)S(1)}, u32[]{:S(2)}, u32[]{:S(2)}) collective-permute-start(bf16[4,32,1280]{2,1,0:T(8,128)(2,1)S(1)} %fusion.5), channel_id=1, source_target_pairs={{0,24},{1,9},{8,16},{9,1},{16,8},{17,25},{24,0},{25,17},{2,26},{3,... | collective-permute-start | bytes 983048 | tf_op jit(solution)/shard_map/ppermute | solution.py:794
  113.6 6.8 %collective-permute-done.9 = bf16[2,4,8,4224]{3,2,1,0:T(8,128)(2,1)S(1)} collective-permute-done((bf16[2,4,8,4224]{3,2,1,0:T(8,128)(2,1)S(1)}, bf16[2,4,8,4224]{3,2,1,0:T(8,128)(2,1)S(1)}, u32[]{:S(2)}, u32[]{:S(2)}) %collective-permute-start.9) | collective-permute-done | bytes 540704 | tf_op jit(solution)/shard_map/ppermute | solution.py:790
  121.3 6.9 %collective-permute-done.12 = bf16[4,8,4224]{2,1,0:T(8,128)(2,1)S(1)} collective-permute-done((bf16[4,8,4224]{2,1,0:T(8,128)(2,1)S(1)}, bf16[4,8,4224]{2,1,0:T(8,128)(2,1)S(1)}, u32[]{:S(2)}, u32[]{:S(2)}) %collective-permute-start.12) | collective-permute-done | bytes 270368 | tf_op jit(solution)/shard_map/ppermute | solution.py:794
  128.5 1.0 collective-permute-start.19
  129.6 3.1 %collective-permute-start.20 = (bf16[8,3072]{1,0:T(8,128)(2,1)S(1)}, bf16[8,3072]{1,0:T(8,128)(2,1)S(1)}, u32[]{:S(2)}, u32[]{:S(2)}) collective-permute-start(bf16[8,3072]{1,0:T(8,128)(2,1)S(1)} %fusion.30), channel_id=1, source_target_pairs={{0,24},{1,9},{8,16},{9,1},{16,8},{17,25},{24,0},{25,17},{2,26},{3,... | collective-permute-start | bytes 147464 | tf_op jit(solution)/shard_map/ppermute | solution.py:794
  132.7 0.8 collective-permute-done.15
  133.5 1.4 collective-permute-start.18
  134.8 0.7 add_bitcast_fusion.7
  136.1 2.9 %collective-permute-done.18 = bf16[8,4224]{1,0:T(8,128)(2,1)S(1)} collective-permute-done((bf16[8,4224]{1,0:T(8,128)(2,1)S(1)}, bf16[8,4224]{1,0:T(8,128)(2,1)S(1)}, u32[]{:S(2)}, u32[]{:S(2)}) %collective-permute-start.18) | collective-permute-done | bytes 67616 | tf_op jit(solution)/shard_map/ppermute | solution.py:794
  139.0 0.7 add_bitcast_fusion.6
  139.8 0.7 slice_reduce_fusion
  (66 shorter events, 5.1 us)
Async XLA Ops:
  0.6 24.4 %copy-start = (f32[1024]{0:T(1024)S(1)}, f32[1024]{0:T(1024)}, u32[]{:S(2)}) copy-start(f32[1024]{0:T(1024)} %param.15) | copy-start | bytes 12292
  0.7 24.4 %copy-start.1 = (s32[256,1]{0,1:T(1,128)S(1)}, s32[256,1]{0,1:T(1,128)}, u32[]{:S(2)}) copy-start(s32[256,1]{0,1:T(1,128)} %param.22) | copy-start | bytes 3076
  0.7 24.4 %copy-start.2 = (s32[1,3]{1,0:T(1,128)S(1)}, s32[1,3]{1,0:T(1,128)}, u32[]{:S(2)}) copy-start(s32[1,3]{1,0:T(1,128)} %lengths.3) | copy-start | bytes 40
  0.7 24.4 %copy-start.3 = (s32[1,3]{1,0:T(1,128)S(1)}, s32[1,3]{1,0:T(1,128)}, u32[]{:S(2)}) copy-start(s32[1,3]{1,0:T(1,128)} %heads.3) | copy-start | bytes 40
  0.7 24.4 %copy-start.4 = (f32[1,128]{1,0:T(1,128)S(1)}, f32[1,128]{1,0:T(1,128)}, u32[]{:S(2)}) copy-start(f32[1,128]{1,0:T(1,128)} %constant.27.clone.inverse) | copy-start | bytes 1540
  24.5 13.0 %collective-permute-start.2 = (bf16[1152,1024]{1,0:T(8,128)(2,1)}, bf16[1152,1024]{1,0:T(8,128)(2,1)S(1)}, u32[]{:S(2)}, u32[]{:S(2)}) collective-permute-start(bf16[1152,1024]{1,0:T(8,128)(2,1)} %get-tuple-element.81.first_other.one), channel_id=1, source_target_pairs={{0,1},{1,0},{2,3},{3,2},{4,5},{5,4},{6,7},{7,6},{8,9},{9,8},{10,11... | collective-permute-start | bytes 7077896 | tf_op jit(solution)/shard_map/ppermute | solution.py:772
  24.6 20.8 %collective-permute-start = (bf16[1280,1024]{1,0:T(8,128)(2,1)}, bf16[1280,1024]{1,0:T(8,128)(2,1)S(1)}, u32[]{:S(2)}, u32[]{:S(2)}) collective-permute-start(bf16[1280,1024]{1,0:T(8,128)(2,1)} %get-tuple-element.85.one), channel_id=1, source_target_pairs={{0,1},{1,0},{2,3},{3,2},{4,5},{5,4},{6,7},{7,6},{8,9},{9,8},{10,11... | collective-permute-start | bytes 7864328 | tf_op jit(solution)/shard_map/ppermute | solution.py:772
  37.1 8.3 %collective-permute-start.1 = (bf16[896,1024]{1,0:T(8,128)(2,1)}, bf16[896,1024]{1,0:T(8,128)(2,1)S(1)}, u32[]{:S(2)}, u32[]{:S(2)}) collective-permute-start(bf16[896,1024]{1,0:T(8,128)(2,1)} %get-tuple-element.87.three), channel_id=1, source_target_pairs={{0,1},{1,0},{2,3},{3,2},{4,5},{5,4},{6,7},{7,6},{8,9},{9,8},{10,11... | collective-permute-start | bytes 5505032 | tf_op jit(solution)/shard_map/ppermute | solution.py:772
  43.6 32.0 %collective-permute-start.5 = (bf16[2,512,1280]{2,1,0:T(8,128)(2,1)}, bf16[2,512,1280]{2,1,0:T(8,128)(2,1)}, u32[]{:S(2)}, u32[]{:S(2)}) collective-permute-start(bf16[2,512,1280]{2,1,0:T(8,128)(2,1)} %get-tuple-element.90.after), channel_id=1, source_target_pairs={{0,32},{1,97},{32,0},{33,65},{64,96},{65,33},{96,64},{97,1},{2,34}... | collective-permute-start | bytes 7864328 | tf_op jit(solution)/shard_map/ppermute | solution.py:790
  45.4 30.3 %copy-start.5 = (bf16[2,512,1280]{2,1,0:T(8,128)(2,1)S(1)}, bf16[2,512,1280]{2,1,0:T(8,128)(2,1)}, u32[]{:S(2)}) copy-start(bf16[2,512,1280]{2,1,0:T(8,128)(2,1)} %get-tuple-element.106) | copy-start | bytes 7864324
  53.6 27.3 %collective-permute-start.4 = (bf16[2,128,3072]{2,1,0:T(8,128)(2,1)}, bf16[2,128,3072]{2,1,0:T(8,128)(2,1)}, u32[]{:S(2)}, u32[]{:S(2)}) collective-permute-start(bf16[2,128,3072]{2,1,0:T(8,128)(2,1)} %get-tuple-element.93), channel_id=1, source_target_pairs={{0,2},{1,7},{2,0},{3,5},{4,6},{5,3},{6,4},{7,1},{8,10},{9,15},{10,... | collective-permute-start | bytes 4718600 | tf_op jit(solution)/shard_map/ppermute | solution.py:790
  55.6 30.7 %collective-permute-start.3 = (bf16[2,128,4224]{2,1,0:T(8,128)(2,1)}, bf16[2,128,4224]{2,1,0:T(8,128)(2,1)}, u32[]{:S(2)}, u32[]{:S(2)}) collective-permute-start(bf16[2,128,4224]{2,1,0:T(8,128)(2,1)} %get-tuple-element.91), channel_id=1, source_target_pairs={{0,8},{1,25},{8,0},{9,17},{16,24},{17,9},{24,16},{25,1},{2,10},{3,... | collective-permute-start | bytes 6488072 | tf_op jit(solution)/shard_map/ppermute | solution.py:790
  75.7 5.2 %copy-start.7 = (bf16[2,128,3072]{2,1,0:T(8,128)(2,1)S(1)}, bf16[2,128,3072]{2,1,0:T(8,128)(2,1)}, u32[]{:S(2)}) copy-start(bf16[2,128,3072]{2,1,0:T(8,128)(2,1)} %get-tuple-element.103) | copy-start | bytes 4718596
  77.4 8.9 %copy-start.6 = (bf16[2,128,4224]{2,1,0:T(8,128)(2,1)S(1)}, bf16[2,128,4224]{2,1,0:T(8,128)(2,1)}, u32[]{:S(2)}) copy-start(bf16[2,128,4224]{2,1,0:T(8,128)(2,1)} %get-tuple-element.109) | copy-start | bytes 6488068
  77.4 20.7 %collective-permute-start.7 = (bf16[512,1280]{1,0:T(8,128)(2,1)S(1)}, bf16[512,1280]{1,0:T(8,128)(2,1)S(1)}, u32[]{:S(2)}, u32[]{:S(2)}) collective-permute-start(bf16[512,1280]{1,0:T(8,128)(2,1)S(1)} %fusion), channel_id=1, source_target_pairs={{0,96},{1,33},{32,64},{33,1},{64,32},{65,97},{96,0},{97,65},{2,98}... | collective-permute-start | bytes 3932168 | tf_op jit(solution)/shard_map/ppermute | solution.py:794
  82.2 14.1 %collective-permute-start.8 = (bf16[128,3072]{1,0:T(8,128)(2,1)S(1)}, bf16[128,3072]{1,0:T(8,128)(2,1)S(1)}, u32[]{:S(2)}, u32[]{:S(2)}) collective-permute-start(bf16[128,3072]{1,0:T(8,128)(2,1)S(1)} %fusion.2), channel_id=1, source_target_pairs={{0,6},{1,3},{2,4},{3,1},{4,2},{5,7},{6,0},{7,5},{8,14},{9,11},{10,... | collective-permute-start | bytes 2359304 | tf_op jit(solution)/shard_map/ppermute | solution.py:794
  87.8 19.3 %collective-permute-start.6 = (bf16[128,4224]{1,0:T(8,128)(2,1)S(1)}, bf16[128,4224]{1,0:T(8,128)(2,1)S(1)}, u32[]{:S(2)}, u32[]{:S(2)}) collective-permute-start(bf16[128,4224]{1,0:T(8,128)(2,1)S(1)} %fusion.1), channel_id=1, source_target_pairs={{0,24},{1,9},{8,16},{9,1},{16,8},{17,25},{24,0},{25,17},{2,26},{3,... | collective-permute-start | bytes 3244040 | tf_op jit(solution)/shard_map/ppermute | solution.py:794
  97.8 11.0 %collective-permute-start.11 = (bf16[2,4,8,3072]{3,2,1,0:T(8,128)(2,1)S(1)}, bf16[2,4,8,3072]{3,2,1,0:T(8,128)(2,1)S(1)}, u32[]{:S(2)}, u32[]{:S(2)}) collective-permute-start(bf16[2,4,8,3072]{3,2,1,0:T(8,128)(2,1)S(1)} %pad_maximum_fusion.5), channel_id=1, source_target_pairs={{0,32},{1,97},{32,0},{33,65},{64,96},{65,33},{96,64},{97,1},{2,34}... | collective-permute-start | bytes 1179656 | tf_op jit(solution)/shard_map/ppermute | solution.py:790
  100.0 10.7 %collective-permute-start.10 = (bf16[2,4,32,1280]{3,2,1,0:T(8,128)(2,1)S(1)}, bf16[2,4,32,1280]{3,2,1,0:T(8,128)(2,1)S(1)}, u32[]{:S(2)}, u32[]{:S(2)}) collective-permute-start(bf16[2,4,32,1280]{3,2,1,0:T(8,128)(2,1)S(1)} %pad_maximum_fusion.3), channel_id=1, source_target_pairs={{0,8},{1,25},{8,0},{9,17},{16,24},{17,9},{24,16},{25,1},{2,10},{3,... | collective-permute-start | bytes 1966088 | tf_op jit(solution)/shard_map/ppermute | solution.py:790
  108.7 11.7 %collective-permute-start.9 = (bf16[2,4,8,4224]{3,2,1,0:T(8,128)(2,1)S(1)}, bf16[2,4,8,4224]{3,2,1,0:T(8,128)(2,1)S(1)}, u32[]{:S(2)}, u32[]{:S(2)}) collective-permute-start(bf16[2,4,8,4224]{3,2,1,0:T(8,128)(2,1)S(1)} %pad_maximum_fusion.4), channel_id=1, source_target_pairs={{0,32},{1,97},{32,0},{33,65},{64,96},{65,33},{96,64},{97,1},{2,34}... | collective-permute-start | bytes 1622024 | tf_op jit(solution)/shard_map/ppermute | solution.py:790
  108.9 11.7 %collective-permute-start.14 = (bf16[4,8,3072]{2,1,0:T(8,128)(2,1)S(1)}, bf16[4,8,3072]{2,1,0:T(8,128)(2,1)S(1)}, u32[]{:S(2)}, u32[]{:S(2)}) collective-permute-start(bf16[4,8,3072]{2,1,0:T(8,128)(2,1)S(1)} %fusion.11), channel_id=1, source_target_pairs={{0,96},{1,33},{32,64},{33,1},{64,32},{65,97},{96,0},{97,65},{2,98}... | collective-permute-start | bytes 589832 | tf_op jit(solution)/shard_map/ppermute | solution.py:794
  110.8 10.3 %collective-permute-start.13 = (bf16[4,32,1280]{2,1,0:T(8,128)(2,1)S(1)}, bf16[4,32,1280]{2,1,0:T(8,128)(2,1)S(1)}, u32[]{:S(2)}, u32[]{:S(2)}) collective-permute-start(bf16[4,32,1280]{2,1,0:T(8,128)(2,1)S(1)} %fusion.5), channel_id=1, source_target_pairs={{0,24},{1,9},{8,16},{9,1},{16,8},{17,25},{24,0},{25,17},{2,26},{3,... | collective-permute-start | bytes 983048 | tf_op jit(solution)/shard_map/ppermute | solution.py:794
  120.4 7.8 %collective-permute-start.12 = (bf16[4,8,4224]{2,1,0:T(8,128)(2,1)S(1)}, bf16[4,8,4224]{2,1,0:T(8,128)(2,1)S(1)}, u32[]{:S(2)}, u32[]{:S(2)}) collective-permute-start(bf16[4,8,4224]{2,1,0:T(8,128)(2,1)S(1)} %fusion.8), channel_id=1, source_target_pairs={{0,96},{1,33},{32,64},{33,1},{64,32},{65,97},{96,0},{97,65},{2,98}... | collective-permute-start | bytes 811016 | tf_op jit(solution)/shard_map/ppermute | solution.py:794
  120.7 8.9 %collective-permute-start.16 = (bf16[2,8,3072]{2,1,0:T(8,128)(2,1)S(1)}, bf16[2,8,3072]{2,1,0:T(8,128)(2,1)S(1)}, u32[]{:S(2)}, u32[]{:S(2)}) collective-permute-start(bf16[2,8,3072]{2,1,0:T(8,128)(2,1)S(1)} %pad_maximum_fusion.11), channel_id=1, source_target_pairs={{0,8},{1,25},{8,0},{9,17},{16,24},{17,9},{24,16},{25,1},{2,10},{3,... | collective-permute-start | bytes 294920 | tf_op jit(solution)/shard_map/ppermute | solution.py:790
  121.2 7.3 %collective-permute-start.17 = (bf16[2,32,1280]{2,1,0:T(8,128)(2,1)S(1)}, bf16[2,32,1280]{2,1,0:T(8,128)(2,1)S(1)}, u32[]{:S(2)}, u32[]{:S(2)}) collective-permute-start(bf16[2,32,1280]{2,1,0:T(8,128)(2,1)S(1)} %pad_maximum_fusion.9), channel_id=1, source_target_pairs={{0,2},{1,7},{2,0},{3,5},{4,6},{5,3},{6,4},{7,1},{8,10},{9,15},{10,... | collective-permute-start | bytes 491528 | tf_op jit(solution)/shard_map/ppermute | solution.py:790
  128.3 5.1 %collective-permute-start.15 = (bf16[2,8,4224]{2,1,0:T(8,128)(2,1)S(1)}, bf16[2,8,4224]{2,1,0:T(8,128)(2,1)S(1)}, u32[]{:S(2)}, u32[]{:S(2)}) collective-permute-start(bf16[2,8,4224]{2,1,0:T(8,128)(2,1)S(1)} %pad_maximum_fusion.10), channel_id=1, source_target_pairs={{0,2},{1,7},{2,0},{3,5},{4,6},{5,3},{6,4},{7,1},{8,10},{9,15},{10,... | collective-permute-start | bytes 405512 | tf_op jit(solution)/shard_map/ppermute | solution.py:790
  128.5 6.3 %collective-permute-start.19 = (bf16[32,1280]{1,0:T(8,128)(2,1)S(1)}, bf16[32,1280]{1,0:T(8,128)(2,1)S(1)}, u32[]{:S(2)}, u32[]{:S(2)}) collective-permute-start(bf16[32,1280]{1,0:T(8,128)(2,1)S(1)} %fusion.24), channel_id=1, source_target_pairs={{0,6},{1,3},{2,4},{3,1},{4,2},{5,7},{6,0},{7,5},{8,14},{9,11},{10,... | collective-permute-start | bytes 245768 | tf_op jit(solution)/shard_map/ppermute | solution.py:794
  129.6 11.7 %collective-permute-start.20 = (bf16[8,3072]{1,0:T(8,128)(2,1)S(1)}, bf16[8,3072]{1,0:T(8,128)(2,1)S(1)}, u32[]{:S(2)}, u32[]{:S(2)}) collective-permute-start(bf16[8,3072]{1,0:T(8,128)(2,1)S(1)} %fusion.30), channel_id=1, source_target_pairs={{0,24},{1,9},{8,16},{9,1},{16,8},{17,25},{24,0},{25,17},{2,26},{3,... | collective-permute-start | bytes 147464 | tf_op jit(solution)/shard_map/ppermute | solution.py:794
  133.5 5.6 %collective-permute-start.18 = (bf16[8,4224]{1,0:T(8,128)(2,1)S(1)}, bf16[8,4224]{1,0:T(8,128)(2,1)S(1)}, u32[]{:S(2)}, u32[]{:S(2)}) collective-permute-start(bf16[8,4224]{1,0:T(8,128)(2,1)S(1)} %fusion.27), channel_id=1, source_target_pairs={{0,6},{1,3},{2,4},{3,1},{4,2},{5,7},{6,0},{7,5},{8,14},{9,11},{10,... | collective-permute-start | bytes 202760 | tf_op jit(solution)/shard_map/ppermute | solution.py:794

commit v3 on v2

--- a/solution.py
+++ b/solution.py
@@ -24,6 +24,7 @@
 ACT, MERGED, FIRST_OWN, GB, GA, FIRST = 0, 512, 640, 640, 896, 1152
 ZED, NORMED, SECOND_OWN, GP, SECOND = 0, 128, 256, 256, 1280
 LINES, THIRD_OWN, GQKV, THIRD = 0, 128, 128, 896
+TURNS = "dquqduqduqduqdudqu"
 BITS = 9
 MIB = 1024 * 1024
 
@@ -193,7 +194,8 @@
     second_mine,
     second_other,
     qkv_out,
-    mixed_out,
+    act_out,
+    middle_out,
     parts,
     tokens,
     cot,
@@ -213,7 +215,6 @@
     left,
     middle,
     ga,
-    mixed,
     bias,
     active,
     level,
@@ -305,6 +306,7 @@
     lax.fori_loop(0, GROUPS, attend, 0)
     loads[5].wait()
     middle[...] = tokens[...].astype(F32) + nn(merged[...], wo[...])
+    stores.append(load(middle, middle_out, out_sem.at[1]))
     normed_mid, _ = normalized(middle[...])
     zed[...] = (normed_mid * ln_gain[...] + ln_bias[...]).astype(BF16)
     loads[4].wait()
@@ -317,6 +319,10 @@
             pltpu.make_async_copy(act_turned.at[side, :, at[1]], ref.at[at], act_sem.at[side, j])
             for side, ref in enumerate(firsts)
         ]
+
+    def act_store(j):
+        at = columns(j, D)
+        return pltpu.make_async_copy(act.at[:, at], act_out.at[:, at], act_sem.at[2, j])
 
     def gp_store(j):
         rows = pl.ds(pl.multiple_of(GP + T * j, T), T)
@@ -331,6 +337,7 @@
         act[:, at] = a
         by_core = a.T.reshape(16, 2, 32, T)
         low_rows, high_rows = by_core[:, 0].reshape(512, T), by_core[:, 1].reshape(512, T)
+        act_store(j).start()
         act_turned[0, :, columns(j, T)] = jnp.where(core == 0, low_rows, high_rows)
         act_turned[1, :, columns(j, T)] = jnp.where(core == 0, high_rows, low_rows)
         for copy in act_stores(j):
@@ -345,12 +352,8 @@
     store_left(1, normed[...], 2, seconds, NORMED)
     store_left(2, merged[...], 0, firsts, MERGED)
 
-    branch = nn(act[...], down[...]).astype(BF16).astype(F32)
-    mid = middle[...]
-    mixed[...] = (mid + prob * branch).astype(BF16)
-    stores.append(load(mixed, mixed_out, out_sem.at[1]))
     grad_zed = nt(gp[...], up[...]).astype(BF16).astype(F32)
-    normed_mid, rstd = normalized(mid)
+    normed_mid, rstd = normalized(middle[...])
     parts[0:1, :] = jnp.sum(grad_zed * normed_mid, 0, keepdims=True)
     parts[1:2, :] = jnp.sum(grad_zed, 0, keepdims=True)
     grad_norm = grad_zed * ln_gain[...]
@@ -363,7 +366,7 @@
     stores.append(load(parts, parts_out, out_sem.at[3]))
     stores.append(load(ga, first_other.at[pl.ds(GA, T), :], out_sem.at[4]))
     for j in range(NEST):
-        wait(act_stores(j) + [gp_store(j)])
+        wait(act_stores(j) + [act_store(j), gp_store(j)])
     wait(stores)
 
 
@@ -389,20 +392,19 @@
         sds((2, 3, 128, D), BF16),
         sds((T, D), F32),
         row_b,
-        row_b,
         sds((T, T), F32),
         sds((T, GW), jnp.int32),
         sds((T, 1), jnp.int32),
     ]
-    semaphores = [(6,), (2, NEST), (2, NEST), (NEST,), (2, 3), (5,)]
+    semaphores = [(6,), (2, NEST), (3, NEST), (NEST,), (2, 3), (5,)]
     return call(
         front_kernel,
         "front",
-        2 * T * D * (4 * D + 4 * FF),
+        2 * T * D * (4 * D + 3 * FF),
         40 * MIB,
         58,
         in_specs=[smem()] * 2 + [vmem()] * 6 + [hbm()] * 6,
-        out_specs=[hbm()] * 7,
+        out_specs=[hbm()] * 8,
         out_shape=[
             sds((8, D), F32),
             sds((FIRST_OWN, D), BF16),
@@ -410,7 +412,8 @@
             sds((SECOND_OWN, D), BF16),
             sds((SECOND, D), BF16),
             sds((3, T, D), BF16),
-            row_b,
+            sds((T, FF), BF16),
+            sds((T, D), F32),
         ],
         scratch_shapes=[pltpu.VMEM(s.shape, s.dtype) for s in scratch]
         + [pltpu.SemaphoreType.DMA(s) for s in semaphores],
@@ -551,7 +554,7 @@
     for side, ref in enumerate(thirds):
         half = core if side == 0 else 1 - core
         for i in range(4):
-            part = lines_f[:, i, :, half].reshape(128, 128).astype(BF16)
+            part = lines_f[:, :, i, half].reshape(128, 128).astype(BF16)
             lines[side, :, pl.ds(128 * i, 128)] = part
         dst = ref.at[pl.ds(LINES, 128), pl.ds(0, 512)]
         stores.append(load(lines.at[side], dst, out_sem.at[1 + side]))
@@ -587,6 +590,50 @@
         scratch_shapes=[pltpu.VMEM(s.shape, s.dtype) for s in scratch]
         + [pltpu.SemaphoreType.DMA(s) for s in [(8,), (3,), (3, GROUPS), (3,)]],
     )(lengths, heads, norm_gain, inverse, bucket, parts, *arrays)
+
+
+def mixed_kernel(
+    router, middle_hbm, act_hbm, down_hbm, after, mixed_out, middle, act, down, mixed, sem, ffn_sem
+):
+    loads = [load(middle_hbm, middle, sem.at[0])]
+    stages = []
+    for j in range(NEST):
+        at = pl.ds(j * D, D)
+        stages.append(
+            [
+                pltpu.make_async_copy(act_hbm.at[:, at], act.at[:, at], ffn_sem.at[0, j]),
+                pltpu.make_async_copy(down_hbm.at[at, :], down.at[at, :], ffn_sem.at[1, j]),
+            ]
+        )
+        start(stages[j])
+    for stage in stages:
+        wait(stage)
+    branch = nn(act[...], down[...]).astype(BF16).astype(F32)
+    wait(loads)
+    mixed[...] = (middle[...] + upright(router[...]) * branch).astype(BF16)
+    load(mixed, mixed_out, sem.at[1]).wait()
+
+
+def mixed_output(router, middle, act, down, after):
+    (mixed,) = call(
+        mixed_kernel,
+        "mixed_output",
+        2 * T * D * FF,
+        12 * MIB,
+        24,
+        in_specs=[vmem()] + [hbm()] * 4,
+        out_specs=[hbm()],
+        out_shape=[sds((T, D), BF16)],
+        scratch_shapes=[
+            pltpu.VMEM((T, D), F32),
+            pltpu.VMEM((T, FF), BF16),
+            pltpu.VMEM((FF, D), BF16),
+            pltpu.VMEM((T, D), BF16),
+            pltpu.SemaphoreType.DMA((2,)),
+            pltpu.SemaphoreType.DMA((2, NEST)),
+        ],
+    )(router, middle, act, down, after)
+    return mixed
 
 
 def load_left(refs, at, rows, axis, left, sem):
@@ -709,7 +756,7 @@
             lines.at[i, m],
             line_sem.at[i, m],
         )
-        for i, block in enumerate(block_order("x"))
+        for i, block in enumerate(block_order("z"))
         for m, ref in enumerate((late_own, four))
     ]
     normed_loads = load_left(split, NORMED, 128, "z", normed, normed_sem)
@@ -730,15 +777,15 @@
         at = pl.ds(n * D, D)
         qkv_out[:, :, at] = nn(normed[...], gqkv[n]).astype(BF16).reshape(4, 128, D)
         stores += store_out(qkv_out, at, qkv_sent, qkv_kept, qkv_sem.at[n])
-    at = pl.ds(FF, 128)
-    up_out[:, :, at] = (lines[:, 0].astype(F32) + lines[:, 1].astype(F32)).astype(BF16)
-    stores += store_out(up_out, at, up_sent, up_kept, up_sem.at[4])
+    at = pl.ds(3 * D, 128)
+    qkv_out[:, :, at] = (lines[:, 0].astype(F32) + lines[:, 1].astype(F32)).astype(BF16)
+    stores += store_out(qkv_out, at, qkv_sent, qkv_kept, qkv_sem.at[3])
     wait(stores)
 
 
 def up_and_qkv_grads(own, one, two, late_own, three, four, after):
-    up = sds((2, 128, FF + 128), BF16)
-    qkv = sds((2, 128, 3 * D), BF16)
+    up = sds((2, 128, FF), BF16)
+    qkv = sds((2, 128, 3 * D + 128), BF16)
     return call(
         up_and_qkv_kernel,
         "up_and_qkv_grad",
@@ -755,15 +802,15 @@
             pltpu.VMEM((4, 2 * T, D), BF16),
             pltpu.VMEM((3, 2 * T, D), BF16),
             pltpu.VMEM((4, 2, 128, 128), BF16),
-            pltpu.VMEM((4, 128, FF + 128), BF16),
-            pltpu.VMEM((4, 128, 3 * D), BF16),
+            pltpu.VMEM((4, 128, FF), BF16),
+            pltpu.VMEM((4, 128, 3 * D + 128), BF16),
             pltpu.SemaphoreType.DMA((4, 2)),
             pltpu.SemaphoreType.DMA((4, 2)),
             pltpu.SemaphoreType.DMA((4, 2)),
             pltpu.SemaphoreType.DMA((3, 2)),
             pltpu.SemaphoreType.DMA((4, 2)),
-            pltpu.SemaphoreType.DMA((5, 2)),
-            pltpu.SemaphoreType.DMA((3, 2)),
+            pltpu.SemaphoreType.DMA((4, 2)),
+            pltpu.SemaphoreType.DMA((4, 2)),
         ],
     )(own, one, two, late_own, three, four, after)
 
@@ -855,7 +902,7 @@
     inverse = np.tile(10000.0 ** (-2.0 * np.arange(HD // 2) / HD), 4).reshape(1, 128)
     inverse = jnp.asarray(inverse, F32)
 
-    parts, first, first_other, second, second_other, qkv, mixed = front(
+    parts, first, first_other, second, second_other, qkv, act, middle = front(
         doc_lengths,
         heads_active,
         norm_gain,
@@ -892,6 +939,8 @@
         second, second_other, second_2, third, third_other, third_2, down_sent
     )
 
+    mixed = mixed_output(router, middle, act, down_weight, qkv_sent)
+
     every = slice(None)
     grads = {}
 
@@ -903,25 +952,25 @@
         return grads["out"]
 
     def up_done(*terms):
-        grads["up"] = total(terms, every, slice(0, FF))
-        line = total(terms, every, slice(FF, FF + 128))
+        grads["up"] = total(terms)
+        return grads["up"]
+
+    def qkv_done(*terms):
+        grads["qkv"] = total(terms, every, slice(0, 3 * D))
+        line = total(terms, every, slice(3 * D, 3 * D + 128))
         grads["gains"] = [line[:, n] for n in range(3)]
         bits = line[0, 3 : 3 + BITS * NEST].astype(jnp.int32).reshape(NEST, BITS)
         grads["counts"] = jnp.sum(bits << jnp.arange(BITS, dtype=jnp.int32)[None, :], 1)
-        done = (grads["up"], grads["counts"], *grads["gains"])
-        grads["up"], grads["counts"], *grads["gains"] = lax.optimization_barrier(done)
-        return grads["up"]
-
-    def qkv_done(*terms):
-        grads["qkv"] = total(terms)
+        done = (grads["qkv"], grads["counts"], *grads["gains"])
+        grads["qkv"], grads["counts"], *grads["gains"] = lax.optimization_barrier(done)
         return grads["qkv"]
 
     take_turns(
-        qkv_sent,
-        "dquqduqduqdudquduq",
+        mixed,
+        TURNS,
         d=chain(down_sent, down_kept, "yxz", (4, 4, 32, D + T), down_done),
-        u=chain(up_sent, up_kept, "xyz", (4, 4, 8, FF + 128), up_done),
-        q=chain(qkv_sent, qkv_kept, "zyx", (4, 4, 8, 3 * D), qkv_done),
+        u=chain(up_sent, up_kept, "xyz", (4, 4, 8, FF), up_done),
+        q=chain(qkv_sent, qkv_kept, "zyx", (4, 4, 8, 3 * D + 128), qkv_done),
     )
     gain_grad, ln_gain_grad, ln_bias_grad = grads["gains"]
     return (

time: 142 us -> 138 us (0.972)
  waiting for transfers between devices: 48.6 us -> 41.9 us
  Pallas kernels: 50.1 us -> 55.9 us
  other arithmetic: 13.9 us -> 11.3 us
    ppermute x9, waiting for transfers between devices: 27.7 us -> 20.1 us  [chain(): got = lax.ppermute(sent, (axis, 'c'), pairs(1, 3))]
    pallas_call x4 -> x5, Pallas kernels: 50.1 us -> 55.9 us  [placed(): run(*(pltpu.with_memory_space_constraint(arg, pltpu.HBM) if in_hbm(spec)...]
  transfers between devices with their start and end apart: 21 -> 21, of which waited for: 8 -> 8; matrix products, arithmetic and copies ran while one was open for 10% -> 8% of each run, Pallas kernels for 19% -> 25%
where the time goes in v3:
time: 138 us; the launch traced here: 137 us
  Pallas kernels  55.9 us (41%)
  waiting for transfers between devices  41.9 us (30%)
  starting transfers between devices  26.3 us (19%)
  other arithmetic  11.3 us (8%)
    pallas_call x5, Pallas kernels, placed(): run(*(pltpu.with_memory_space_constraint(arg, pltpu.HBM) if in_hbm(spec)...  55.9 us
    ppermute x9, waiting for transfers between devices, chain(): got_2 = lax.ppermute(more, (axis, 'c'), pairs(3, 1))  21.7 us
    ppermute x9, waiting for transfers between devices, chain(): got = lax.ppermute(sent, (axis, 'c'), pairs(1, 3))  20.1 us
    ppermute x9, starting transfers between devices, chain(): got_2 = lax.ppermute(more, (axis, 'c'), pairs(3, 1))  17.7 us
    ppermute x9, starting transfers between devices, chain(): got = lax.ppermute(sent, (axis, 'c'), pairs(1, 3))  7.63 us
    another operation x12, other arithmetic, chain(): kept = jnp.stack([own, second])  4.32 us
    convert_element_type x9, other arithmetic, chain(): more = (got[1].astype(F32) + kept[1].astype(F32)).astype(BF16)  3.41 us
  transfers between devices with their start and end apart: 21, of which 8 were waited for; matrix products, arithmetic and copies ran while one was open for 8% of the time, Pallas kernels for 25%

profile of v3, /device:TPU:0, one launch (start us, length us, event | category | flops | bytes accessed | tf_op | source)
XLA Modules:
  0.0 137.2 jit_solution(16814503574492210028)
XLA Ops:
  0.7 21.6 %front.1 = (f32[8,1024]{1,0:T(8,128)}, bf16[640,1024]{1,0:T(8,128)(2,1)}, bf16[1152,1024]{1,0:T(8,128)(2,1)}, bf16[256,1024]{1,0:T(8,128)(2,1)}, bf16[1280,1024]...) custom-call(s32[1,3]{1,0:T(1,128)} %lengths.3, s32[1,3]{1,0:T(1,128)} %heads.3, ...), custom_call_target="tpu_custom_call" | custom-call | flops 8589934592 | bytes 41943040 | tf_op jit(solution)/shard_map/front/pallas_call | solution.py:77
  23.0 12.0 %back.1 = (bf16[128,1024]{1,0:T(8,128)(2,1)}, bf16[896,1024]{1,0:T(8,128)(2,1)}, f32[256,1024]{1,0:T(8,128)}) custom-call(s32[1,3]{1,0:T(1,128)S(1)} %copy-done.3, s32[1,3]{1,0:T(1,128)S(1)} %copy-done.4, f32[1,1024]{1,0:T(1,128)S(1)} %bitcast.134, f32[1,128]{1,0:T(1,128)S(1)} %copy-done.5, s32[1,256]{1,0:T(1,128)S(1)} %bitcast.136, ...), custom_call_target="tpu_custom_call" | custom-call | flops 4831838208 | bytes 18874368 | tf_op jit(solution)/shard_map/back/pallas_call | solution.py:77
  35.3 6.2 %down_and_out_grad.1 = (bf16[2,512,1280]{2,1,0:T(8,128)(2,1)}, bf16[2,512,1280]{2,1,0:T(8,128)(2,1)}) custom-call(bf16[640,1024]{1,0:T(8,128)(2,1)} %get-tuple-element.89.own, bf16[1152,1024]{1,0:T(8,128)(2,1)} %get-tuple-element.85.first_other.one, bf16[1152,1024]{1,0:T(8,128)(2,1)S(1)} %collective-permute-done.2.two), custom_call_target="tpu_custom_call" | custom-call | flops 2684354560 | bytes 10485760 | tf_op jit(solution)/shard_map/down_and_out_grad/pallas_call | solution.py:77
  41.5 1.7 %collective-permute-start.4 = (bf16[2,512,1280]{2,1,0:T(8,128)(2,1)}, bf16[2,512,1280]{2,1,0:T(8,128)(2,1)S(1)}, u32[]{:S(2)}, u32[]{:S(2)}) collective-permute-start(bf16[2,512,1280]{2,1,0:T(8,128)(2,1)} %get-tuple-element.91.after), channel_id=1, source_target_pairs={{0,32},{1,97},{32,0},{33,65},{64,96},{65,33},{96,64},{97,1},{2,34}... | collective-permute-start | bytes 7864328 | tf_op jit(solution)/shard_map/ppermute | solution.py:837
  43.3 8.1 %up_and_qkv_grad.1 = (bf16[2,128,4096]{2,1,0:T(8,128)(2,1)}, bf16[2,128,4096]{2,1,0:T(8,128)(2,1)}, bf16[2,128,3200]{2,1,0:T(8,128)(2,1)}, bf16[2,128,3200]{2,1,0:T(8,128)(2,1)}) custom-call(bf16[256,1024]{1,0:T(8,128)(2,1)} %get-tuple-element.82.own, bf16[1280,1024]{1,0:T(8,128)(2,1)} %get-tuple-element.83.one, ...), custom_call_target="tpu_custom_call" | custom-call | flops 3758096384 | bytes 16777216 | tf_op jit(solution)/shard_map/up_and_qkv_grad/pallas_call | solution.py:77
  51.3 2.0 %collective-permute-start.3 = (bf16[2,128,3200]{2,1,0:T(8,128)(2,1)}, bf16[2,128,3200]{2,1,0:T(8,128)(2,1)}, u32[]{:S(2)}, u32[]{:S(2)}) collective-permute-start(bf16[2,128,3200]{2,1,0:T(8,128)(2,1)} %get-tuple-element.92.after), channel_id=1, source_target_pairs={{0,2},{1,7},{2,0},{3,5},{4,6},{5,3},{6,4},{7,1},{8,10},{9,15},{10,... | collective-permute-start | bytes 4915208 | tf_op jit(solution)/shard_map/ppermute | solution.py:837
  53.3 1.5 %collective-permute-start.6 = (bf16[2,128,4096]{2,1,0:T(8,128)(2,1)}, bf16[2,128,4096]{2,1,0:T(8,128)(2,1)}, u32[]{:S(2)}, u32[]{:S(2)}) collective-permute-start(bf16[2,128,4096]{2,1,0:T(8,128)(2,1)} %get-tuple-element.100), channel_id=1, source_target_pairs={{0,8},{1,25},{8,0},{9,17},{16,24},{17,9},{24,16},{25,1},{2,10},{3,... | collective-permute-start | bytes 6291464 | tf_op jit(solution)/shard_map/ppermute | solution.py:837
  54.8 8.0 %mixed_output.1 = bf16[256,1024]{1,0:T(8,128)(2,1)} custom-call(f32[1,256]{1,0:T(1,128)S(1)} %bitcast.132, f32[256,1024]{1,0:T(8,128)} %get-tuple-element.80.middle_hbm, bf16[256,4096]{1,0:T(8,128)(2,1)} %get-tuple-element.81.act_hbm, bf16[4096,1024]{1,0:T(8,128)(2,1)} %down_hbm.3, bf16[2,128,3200]{2,1,0:T(8,128)(2,1)} %get-tuple-element.92.after), custom_call_target="tpu_custom_call" | custom-call | flops 2147483648 | bytes 12582912 | tf_op jit(solution)/shard_map/mixed_output/pallas_call | solution.py:77
  62.9 10.6 %collective-permute-done.4 = bf16[2,512,1280]{2,1,0:T(8,128)(2,1)S(1)} collective-permute-done((bf16[2,512,1280]{2,1,0:T(8,128)(2,1)}, bf16[2,512,1280]{2,1,0:T(8,128)(2,1)S(1)}, u32[]{:S(2)}, u32[]{:S(2)}) %collective-permute-start.4) | collective-permute-done | bytes 2621472 | tf_op jit(solution)/shard_map/ppermute | solution.py:837
  73.8 3.2 %collective-permute-start.9 = (bf16[512,1280]{1,0:T(8,128)(2,1)S(1)}, bf16[512,1280]{1,0:T(8,128)(2,1)S(1)}, u32[]{:S(2)}, u32[]{:S(2)}) collective-permute-start(bf16[512,1280]{1,0:T(8,128)(2,1)S(1)} %fusion), channel_id=1, source_target_pairs={{0,96},{1,33},{32,64},{33,1},{64,32},{65,97},{96,0},{97,65},{2,98}... | collective-permute-start | bytes 3932168 | tf_op jit(solution)/shard_map/ppermute | solution.py:841
  77.0 1.3 fusion.2
  78.4 4.1 %collective-permute-start.5 = (bf16[128,3200]{1,0:T(8,128)(2,1)S(1)}, bf16[128,3200]{1,0:T(8,128)(2,1)S(1)}, u32[]{:S(2)}, u32[]{:S(2)}) collective-permute-start(bf16[128,3200]{1,0:T(8,128)(2,1)S(1)} %fusion.2), channel_id=1, source_target_pairs={{0,6},{1,3},{2,4},{3,1},{4,2},{5,7},{6,0},{7,5},{8,14},{9,11},{10,... | collective-permute-start | bytes 2457608 | tf_op jit(solution)/shard_map/ppermute | solution.py:841
  82.5 1.5 %fusion.1 = bf16[128,4096]{1,0:T(8,128)(2,1)S(1)} fusion(bf16[2,128,4096]{2,1,0:T(8,128)(2,1)S(1)} %copy-done.7, bf16[2,128,4096]{2,1,0:T(8,128)(2,1)} %collective-permute-done.6), kind=kLoop, calls=%fused_computation.5 | loop fusion | flops 2097152 | bytes 3145728 | tf_op jit(solution)/shard_map/convert_element_type | solution.py:840
  84.0 2.8 %collective-permute-start.8 = (bf16[128,4096]{1,0:T(8,128)(2,1)S(1)}, bf16[128,4096]{1,0:T(8,128)(2,1)S(1)}, u32[]{:S(2)}, u32[]{:S(2)}) collective-permute-start(bf16[128,4096]{1,0:T(8,128)(2,1)S(1)} %fusion.1), channel_id=1, source_target_pairs={{0,24},{1,9},{8,16},{9,1},{16,8},{17,25},{24,0},{25,17},{2,26},{3,... | collective-permute-start | bytes 3145736 | tf_op jit(solution)/shard_map/ppermute | solution.py:841
  86.8 6.0 %collective-permute-done.5 = bf16[128,3200]{1,0:T(8,128)(2,1)S(1)} collective-permute-done((bf16[128,3200]{1,0:T(8,128)(2,1)S(1)}, bf16[128,3200]{1,0:T(8,128)(2,1)S(1)}, u32[]{:S(2)}, u32[]{:S(2)}) %collective-permute-start.5) | collective-permute-done | bytes 819232 | tf_op jit(solution)/shard_map/ppermute | solution.py:841
  92.8 1.5 %add_bitcast_fusion.5 = (f32[1,4,8,3200]{3,2,1,0:T(8,128)S(1)}, f32[1,4,8,3200]{3,2,1,0:T(8,128)S(1)}, bf16[1,4,8,3200]{3,2,1,0:T(8,128)(2,1)S(1)}, bf16[1,4,8,3200]{3,2,1,0:T(8,128)(2,1)S(1)}) fusion(bf16[1,4,4,8,3200]{4,3,2,1,0:T(8,128)(2,1)S(1)} %bitcast.143, s32[]{:T(128)S(6)} %select_n.26, bf16[2,4,4,8,3200]{4,3,2,1,0:T(8,128)(2,1)S(1)} %bitcast.140, ...), kind=kLoop, calls=%fused_computation.24 | loop fusion | flops 2252800 | bytes 3686416 | tf_op jit(solution)/shard_map/stack;reshape | solution.py:863
  95.3 1.6 %collective-permute-start.12 = (bf16[2,4,32,1280]{3,2,1,0:T(8,128)(2,1)S(1)}, bf16[2,4,32,1280]{3,2,1,0:T(8,128)(2,1)S(1)}, u32[]{:S(2)}, u32[]{:S(2)}) collective-permute-start(bf16[2,4,32,1280]{3,2,1,0:T(8,128)(2,1)S(1)} %pad_maximum_fusion.3), channel_id=1, source_target_pairs={{0,8},{1,25},{8,0},{9,17},{16,24},{17,9},{24,16},{25,1},{2,10},{3,... | collective-permute-start | bytes 1966088 | tf_op jit(solution)/shard_map/ppermute | solution.py:837
  96.9 6.6 %collective-permute-done.8 = bf16[128,4096]{1,0:T(8,128)(2,1)S(1)} collective-permute-done((bf16[128,4096]{1,0:T(8,128)(2,1)S(1)}, bf16[128,4096]{1,0:T(8,128)(2,1)S(1)}, u32[]{:S(2)}, u32[]{:S(2)}) %collective-permute-start.8) | collective-permute-done | bytes 1048608 | tf_op jit(solution)/shard_map/ppermute | solution.py:841
  103.5 1.6 %add_bitcast_fusion.3 = (f32[1,4,8,4096]{3,2,1,0:T(8,128)S(1)}, f32[1,4,8,4096]{3,2,1,0:T(8,128)S(1)}, bf16[1,4,8,4096]{3,2,1,0:T(8,128)(2,1)S(1)}, bf16[1,4,8,4096]{3,2,1,0:T(8,128)(2,1)S(1)}) fusion(bf16[1,4,4,8,4096]{4,3,2,1,0:T(8,128)(2,1)S(1)} %bitcast.142, s32[]{:T(128)S(6)} %select_n.26, bf16[2,4,4,8,4096]{4,3,2,1,0:T(8,128)(2,1)S(1)} %bitcast.139, ...), kind=kLoop, calls=%fused_computation.18 | loop fusion | flops 2883584 | bytes 4718608 | tf_op jit(solution)/shard_map/stack;reshape | solution.py:863
  106.1 2.8 %collective-permute-start.15 = (bf16[4,32,1280]{2,1,0:T(8,128)(2,1)S(1)}, bf16[4,32,1280]{2,1,0:T(8,128)(2,1)S(1)}, u32[]{:S(2)}, u32[]{:S(2)}) collective-permute-start(bf16[4,32,1280]{2,1,0:T(8,128)(2,1)S(1)} %fusion.5), channel_id=1, source_target_pairs={{0,24},{1,9},{8,16},{9,1},{16,8},{17,25},{24,0},{25,17},{2,26},{3,... | collective-permute-start | bytes 983048 | tf_op jit(solution)/shard_map/ppermute | solution.py:841
  108.9 7.4 %collective-permute-done.11 = bf16[2,4,8,4096]{3,2,1,0:T(8,128)(2,1)S(1)} collective-permute-done((bf16[2,4,8,4096]{3,2,1,0:T(8,128)(2,1)S(1)}, bf16[2,4,8,4096]{3,2,1,0:T(8,128)(2,1)S(1)}, u32[]{:S(2)}, u32[]{:S(2)}) %collective-permute-start.11) | collective-permute-done | bytes 524320 | tf_op jit(solution)/shard_map/ppermute | solution.py:837
  117.3 6.8 %collective-permute-done.14 = bf16[4,8,4096]{2,1,0:T(8,128)(2,1)S(1)} collective-permute-done((bf16[4,8,4096]{2,1,0:T(8,128)(2,1)S(1)}, bf16[4,8,4096]{2,1,0:T(8,128)(2,1)S(1)}, u32[]{:S(2)}, u32[]{:S(2)}) %collective-permute-start.14) | collective-permute-done | bytes 262176 | tf_op jit(solution)/shard_map/ppermute | solution.py:841
  124.3 2.8 %collective-permute-start.16 = (bf16[8,3200]{1,0:T(8,128)(2,1)S(1)}, bf16[8,3200]{1,0:T(8,128)(2,1)S(1)}, u32[]{:S(2)}, u32[]{:S(2)}) collective-permute-start(bf16[8,3200]{1,0:T(8,128)(2,1)S(1)} %fusion.30), channel_id=1, source_target_pairs={{0,24},{1,9},{8,16},{9,1},{16,8},{17,25},{24,0},{25,17},{2,26},{3,... | collective-permute-start | bytes 153608 | tf_op jit(solution)/shard_map/ppermute | solution.py:841
  127.4 1.9 %collective-permute-done.19 = bf16[2,8,4096]{2,1,0:T(8,128)(2,1)S(1)} collective-permute-done((bf16[2,8,4096]{2,1,0:T(8,128)(2,1)S(1)}, bf16[2,8,4096]{2,1,0:T(8,128)(2,1)S(1)}, u32[]{:S(2)}, u32[]{:S(2)}) %collective-permute-start.19) | collective-permute-done | bytes 131104 | tf_op jit(solution)/shard_map/ppermute | solution.py:837
  129.3 1.4 %collective-permute-start.20 = (bf16[8,4096]{1,0:T(8,128)(2,1)S(1)}, bf16[8,4096]{1,0:T(8,128)(2,1)S(1)}, u32[]{:S(2)}, u32[]{:S(2)}) collective-permute-start(bf16[8,4096]{1,0:T(8,128)(2,1)S(1)} %fusion.27), channel_id=1, source_target_pairs={{0,6},{1,3},{2,4},{3,1},{4,2},{5,7},{6,0},{7,5},{8,14},{9,11},{10,... | collective-permute-start | bytes 196616 | tf_op jit(solution)/shard_map/ppermute | solution.py:841
  130.7 2.3 %collective-permute-done.18 = bf16[32,1280]{1,0:T(8,128)(2,1)S(1)} collective-permute-done((bf16[32,1280]{1,0:T(8,128)(2,1)S(1)}, bf16[32,1280]{1,0:T(8,128)(2,1)S(1)}, u32[]{:S(2)}, u32[]{:S(2)}) %collective-permute-start.18) | collective-permute-done | bytes 81952 | tf_op jit(solution)/shard_map/ppermute | solution.py:841
  133.0 0.7 add_bitcast_fusion.6
  133.7 0.6 convert_add_fusion.12
  134.3 0.7 add_bitcast_fusion.7
  135.1 0.7 slice_reduce_fusion
  135.9 0.6 shift-left_reduce_fusion
  136.5 0.7 bitcast_add_fusion
  (69 shorter events, 4.7 us)
Async XLA Ops:
  0.6 22.3 %copy-start.1 = (f32[1024]{0:T(1024)S(1)}, f32[1024]{0:T(1024)}, u32[]{:S(2)}) copy-start(f32[1024]{0:T(1024)} %param.15) | copy-start | bytes 12292
  0.7 22.3 %copy-start.2 = (s32[256,1]{0,1:T(1,128)S(1)}, s32[256,1]{0,1:T(1,128)}, u32[]{:S(2)}) copy-start(s32[256,1]{0,1:T(1,128)} %param.22) | copy-start | bytes 3076
  0.7 22.3 %copy-start.3 = (s32[1,3]{1,0:T(1,128)S(1)}, s32[1,3]{1,0:T(1,128)}, u32[]{:S(2)}) copy-start(s32[1,3]{1,0:T(1,128)} %lengths.3) | copy-start | bytes 40
  0.7 22.3 %copy-start.4 = (s32[1,3]{1,0:T(1,128)S(1)}, s32[1,3]{1,0:T(1,128)}, u32[]{:S(2)}) copy-start(s32[1,3]{1,0:T(1,128)} %heads.3) | copy-start | bytes 40
  0.7 22.3 %copy-start.5 = (f32[1,128]{1,0:T(1,128)S(1)}, f32[1,128]{1,0:T(1,128)}, u32[]{:S(2)}) copy-start(f32[1,128]{1,0:T(1,128)} %constant.27.clone.inverse) | copy-start | bytes 1540
  22.3 13.0 %collective-permute-start.2 = (bf16[1152,1024]{1,0:T(8,128)(2,1)}, bf16[1152,1024]{1,0:T(8,128)(2,1)S(1)}, u32[]{:S(2)}, u32[]{:S(2)}) collective-permute-start(bf16[1152,1024]{1,0:T(8,128)(2,1)} %get-tuple-element.85.first_other.one), channel_id=1, source_target_pairs={{0,1},{1,0},{2,3},{3,2},{4,5},{5,4},{6,7},{7,6},{8,9},{9,8},{10,11... | collective-permute-start | bytes 7077896 | tf_op jit(solution)/shard_map/ppermute | solution.py:819
  22.4 20.8 %collective-permute-start = (bf16[1280,1024]{1,0:T(8,128)(2,1)}, bf16[1280,1024]{1,0:T(8,128)(2,1)S(1)}, u32[]{:S(2)}, u32[]{:S(2)}) collective-permute-start(bf16[1280,1024]{1,0:T(8,128)(2,1)} %get-tuple-element.83.one), channel_id=1, source_target_pairs={{0,1},{1,0},{2,3},{3,2},{4,5},{5,4},{6,7},{7,6},{8,9},{9,8},{10,11... | collective-permute-start | bytes 7864328 | tf_op jit(solution)/shard_map/ppermute | solution.py:819
  35.0 8.3 %collective-permute-start.1 = (bf16[896,1024]{1,0:T(8,128)(2,1)}, bf16[896,1024]{1,0:T(8,128)(2,1)S(1)}, u32[]{:S(2)}, u32[]{:S(2)}) collective-permute-start(bf16[896,1024]{1,0:T(8,128)(2,1)} %get-tuple-element.88.three), channel_id=1, source_target_pairs={{0,1},{1,0},{2,3},{3,2},{4,5},{5,4},{6,7},{7,6},{8,9},{9,8},{10,11... | collective-permute-start | bytes 5505032 | tf_op jit(solution)/shard_map/ppermute | solution.py:819
  41.5 31.9 %collective-permute-start.4 = (bf16[2,512,1280]{2,1,0:T(8,128)(2,1)}, bf16[2,512,1280]{2,1,0:T(8,128)(2,1)S(1)}, u32[]{:S(2)}, u32[]{:S(2)}) collective-permute-start(bf16[2,512,1280]{2,1,0:T(8,128)(2,1)} %get-tuple-element.91.after), channel_id=1, source_target_pairs={{0,32},{1,97},{32,0},{33,65},{64,96},{65,33},{96,64},{97,1},{2,34}... | collective-permute-start | bytes 7864328 | tf_op jit(solution)/shard_map/ppermute | solution.py:837
  43.3 11.6 %copy-start = (f32[256]{0:T(256)S(1)}, f32[256]{0:T(256)}, u32[]{:S(2)}) copy-start(f32[256]{0:T(256)} %param.23) | copy-start | bytes 3076
  51.3 25.7 %collective-permute-start.3 = (bf16[2,128,3200]{2,1,0:T(8,128)(2,1)}, bf16[2,128,3200]{2,1,0:T(8,128)(2,1)}, u32[]{:S(2)}, u32[]{:S(2)}) collective-permute-start(bf16[2,128,3200]{2,1,0:T(8,128)(2,1)} %get-tuple-element.92.after), channel_id=1, source_target_pairs={{0,2},{1,7},{2,0},{3,5},{4,6},{5,3},{6,4},{7,1},{8,10},{9,15},{10,... | collective-permute-start | bytes 4915208 | tf_op jit(solution)/shard_map/ppermute | solution.py:837
  53.3 29.1 %collective-permute-start.6 = (bf16[2,128,4096]{2,1,0:T(8,128)(2,1)}, bf16[2,128,4096]{2,1,0:T(8,128)(2,1)}, u32[]{:S(2)}, u32[]{:S(2)}) collective-permute-start(bf16[2,128,4096]{2,1,0:T(8,128)(2,1)} %get-tuple-element.100), channel_id=1, source_target_pairs={{0,8},{1,25},{8,0},{9,17},{16,24},{17,9},{24,16},{25,1},{2,10},{3,... | collective-permute-start | bytes 6291464 | tf_op jit(solution)/shard_map/ppermute | solution.py:837
  54.8 18.6 %copy-start.6 = (bf16[2,512,1280]{2,1,0:T(8,128)(2,1)S(1)}, bf16[2,512,1280]{2,1,0:T(8,128)(2,1)}, u32[]{:S(2)}) copy-start(bf16[2,512,1280]{2,1,0:T(8,128)(2,1)} %get-tuple-element.108) | copy-start | bytes 7864324
  62.9 14.2 %copy-start.8 = (bf16[2,128,3200]{2,1,0:T(8,128)(2,1)S(1)}, bf16[2,128,3200]{2,1,0:T(8,128)(2,1)}, u32[]{:S(2)}) copy-start(bf16[2,128,3200]{2,1,0:T(8,128)(2,1)} %get-tuple-element.105) | copy-start | bytes 4915204
  73.8 8.7 %copy-start.7 = (bf16[2,128,4096]{2,1,0:T(8,128)(2,1)S(1)}, bf16[2,128,4096]{2,1,0:T(8,128)(2,1)}, u32[]{:S(2)}) copy-start(bf16[2,128,4096]{2,1,0:T(8,128)(2,1)} %get-tuple-element.111) | copy-start | bytes 6291460
  73.8 20.9 %collective-permute-start.9 = (bf16[512,1280]{1,0:T(8,128)(2,1)S(1)}, bf16[512,1280]{1,0:T(8,128)(2,1)S(1)}, u32[]{:S(2)}, u32[]{:S(2)}) collective-permute-start(bf16[512,1280]{1,0:T(8,128)(2,1)S(1)} %fusion), channel_id=1, source_target_pairs={{0,96},{1,33},{32,64},{33,1},{64,32},{65,97},{96,0},{97,65},{2,98}... | collective-permute-start | bytes 3932168 | tf_op jit(solution)/shard_map/ppermute | solution.py:841
  78.4 14.4 %collective-permute-start.5 = (bf16[128,3200]{1,0:T(8,128)(2,1)S(1)}, bf16[128,3200]{1,0:T(8,128)(2,1)S(1)}, u32[]{:S(2)}, u32[]{:S(2)}) collective-permute-start(bf16[128,3200]{1,0:T(8,128)(2,1)S(1)} %fusion.2), channel_id=1, source_target_pairs={{0,6},{1,3},{2,4},{3,1},{4,2},{5,7},{6,0},{7,5},{8,14},{9,11},{10,... | collective-permute-start | bytes 2457608 | tf_op jit(solution)/shard_map/ppermute | solution.py:841
  84.0 19.5 %collective-permute-start.8 = (bf16[128,4096]{1,0:T(8,128)(2,1)S(1)}, bf16[128,4096]{1,0:T(8,128)(2,1)S(1)}, u32[]{:S(2)}, u32[]{:S(2)}) collective-permute-start(bf16[128,4096]{1,0:T(8,128)(2,1)S(1)} %fusion.1), channel_id=1, source_target_pairs={{0,24},{1,9},{8,16},{9,1},{16,8},{17,25},{24,0},{25,17},{2,26},{3,... | collective-permute-start | bytes 3145736 | tf_op jit(solution)/shard_map/ppermute | solution.py:841
  94.4 10.8 %collective-permute-start.7 = (bf16[2,4,8,3200]{3,2,1,0:T(8,128)(2,1)S(1)}, bf16[2,4,8,3200]{3,2,1,0:T(8,128)(2,1)S(1)}, u32[]{:S(2)}, u32[]{:S(2)}) collective-permute-start(bf16[2,4,8,3200]{3,2,1,0:T(8,128)(2,1)S(1)} %pad_maximum_fusion.5), channel_id=1, source_target_pairs={{0,32},{1,97},{32,0},{33,65},{64,96},{65,33},{96,64},{97,1},{2,34}... | collective-permute-start | bytes 1228808 | tf_op jit(solution)/shard_map/ppermute | solution.py:837
  95.3 10.7 %collective-permute-start.12 = (bf16[2,4,32,1280]{3,2,1,0:T(8,128)(2,1)S(1)}, bf16[2,4,32,1280]{3,2,1,0:T(8,128)(2,1)S(1)}, u32[]{:S(2)}, u32[]{:S(2)}) collective-permute-start(bf16[2,4,32,1280]{3,2,1,0:T(8,128)(2,1)S(1)} %pad_maximum_fusion.3), channel_id=1, source_target_pairs={{0,8},{1,25},{8,0},{9,17},{16,24},{17,9},{24,16},{25,1},{2,10},{3,... | collective-permute-start | bytes 1966088 | tf_op jit(solution)/shard_map/ppermute | solution.py:837
  105.1 11.2 %collective-permute-start.11 = (bf16[2,4,8,4096]{3,2,1,0:T(8,128)(2,1)S(1)}, bf16[2,4,8,4096]{3,2,1,0:T(8,128)(2,1)S(1)}, u32[]{:S(2)}, u32[]{:S(2)}) collective-permute-start(bf16[2,4,8,4096]{3,2,1,0:T(8,128)(2,1)S(1)} %pad_maximum_fusion.4), channel_id=1, source_target_pairs={{0,32},{1,97},{32,0},{33,65},{64,96},{65,33},{96,64},{97,1},{2,34}... | collective-permute-start | bytes 1572872 | tf_op jit(solution)/shard_map/ppermute | solution.py:837
  105.3 11.2 %collective-permute-start.10 = (bf16[4,8,3200]{2,1,0:T(8,128)(2,1)S(1)}, bf16[4,8,3200]{2,1,0:T(8,128)(2,1)S(1)}, u32[]{:S(2)}, u32[]{:S(2)}) collective-permute-start(bf16[4,8,3200]{2,1,0:T(8,128)(2,1)S(1)} %fusion.11), channel_id=1, source_target_pairs={{0,96},{1,33},{32,64},{33,1},{64,32},{65,97},{96,0},{97,65},{2,98}... | collective-permute-start | bytes 614408 | tf_op jit(solution)/shard_map/ppermute | solution.py:841
  106.1 11.0 %collective-permute-start.15 = (bf16[4,32,1280]{2,1,0:T(8,128)(2,1)S(1)}, bf16[4,32,1280]{2,1,0:T(8,128)(2,1)S(1)}, u32[]{:S(2)}, u32[]{:S(2)}) collective-permute-start(bf16[4,32,1280]{2,1,0:T(8,128)(2,1)S(1)} %fusion.5), channel_id=1, source_target_pairs={{0,24},{1,9},{8,16},{9,1},{16,8},{17,25},{24,0},{25,17},{2,26},{3,... | collective-permute-start | bytes 983048 | tf_op jit(solution)/shard_map/ppermute | solution.py:841
  116.4 7.7 %collective-permute-start.14 = (bf16[4,8,4096]{2,1,0:T(8,128)(2,1)S(1)}, bf16[4,8,4096]{2,1,0:T(8,128)(2,1)S(1)}, u32[]{:S(2)}, u32[]{:S(2)}) collective-permute-start(bf16[4,8,4096]{2,1,0:T(8,128)(2,1)S(1)} %fusion.8), channel_id=1, source_target_pairs={{0,96},{1,33},{32,64},{33,1},{64,32},{65,97},{96,0},{97,65},{2,98}... | collective-permute-start | bytes 786440 | tf_op jit(solution)/shard_map/ppermute | solution.py:841
  116.7 7.7 %collective-permute-start.13 = (bf16[2,8,3200]{2,1,0:T(8,128)(2,1)S(1)}, bf16[2,8,3200]{2,1,0:T(8,128)(2,1)S(1)}, u32[]{:S(2)}, u32[]{:S(2)}) collective-permute-start(bf16[2,8,3200]{2,1,0:T(8,128)(2,1)S(1)} %pad_maximum_fusion.11), channel_id=1, source_target_pairs={{0,8},{1,25},{8,0},{9,17},{16,24},{17,9},{24,16},{25,1},{2,10},{3,... | collective-permute-start | bytes 307208 | tf_op jit(solution)/shard_map/ppermute | solution.py:837
  117.2 10.0 %collective-permute-start.17 = (bf16[2,32,1280]{2,1,0:T(8,128)(2,1)S(1)}, bf16[2,32,1280]{2,1,0:T(8,128)(2,1)S(1)}, u32[]{:S(2)}, u32[]{:S(2)}) collective-permute-start(bf16[2,32,1280]{2,1,0:T(8,128)(2,1)S(1)} %pad_maximum_fusion.9), channel_id=1, source_target_pairs={{0,2},{1,7},{2,0},{3,5},{4,6},{5,3},{6,4},{7,1},{8,10},{9,15},{10,... | collective-permute-start | bytes 491528 | tf_op jit(solution)/shard_map/ppermute | solution.py:837
  124.2 5.0 %collective-permute-start.19 = (bf16[2,8,4096]{2,1,0:T(8,128)(2,1)S(1)}, bf16[2,8,4096]{2,1,0:T(8,128)(2,1)S(1)}, u32[]{:S(2)}, u32[]{:S(2)}) collective-permute-start(bf16[2,8,4096]{2,1,0:T(8,128)(2,1)S(1)} %pad_maximum_fusion.10), channel_id=1, source_target_pairs={{0,2},{1,7},{2,0},{3,5},{4,6},{5,3},{6,4},{7,1},{8,10},{9,15},{10,... | collective-permute-start | bytes 393224 | tf_op jit(solution)/shard_map/ppermute | solution.py:837
  124.3 10.0 %collective-permute-start.16 = (bf16[8,3200]{1,0:T(8,128)(2,1)S(1)}, bf16[8,3200]{1,0:T(8,128)(2,1)S(1)}, u32[]{:S(2)}, u32[]{:S(2)}) collective-permute-start(bf16[8,3200]{1,0:T(8,128)(2,1)S(1)} %fusion.30), channel_id=1, source_target_pairs={{0,24},{1,9},{8,16},{9,1},{16,8},{17,25},{24,0},{25,17},{2,26},{3,... | collective-permute-start | bytes 153608 | tf_op jit(solution)/shard_map/ppermute | solution.py:841
  127.3 5.7 %collective-permute-start.18 = (bf16[32,1280]{1,0:T(8,128)(2,1)S(1)}, bf16[32,1280]{1,0:T(8,128)(2,1)S(1)}, u32[]{:S(2)}, u32[]{:S(2)}) collective-permute-start(bf16[32,1280]{1,0:T(8,128)(2,1)S(1)} %fusion.24), channel_id=1, source_target_pairs={{0,6},{1,3},{2,4},{3,1},{4,2},{5,7},{6,0},{7,5},{8,14},{9,11},{10,... | collective-permute-start | bytes 245768 | tf_op jit(solution)/shard_map/ppermute | solution.py:841
  129.3 7.2 %collective-permute-start.20 = (bf16[8,4096]{1,0:T(8,128)(2,1)S(1)}, bf16[8,4096]{1,0:T(8,128)(2,1)S(1)}, u32[]{:S(2)}, u32[]{:S(2)}) collective-permute-start(bf16[8,4096]{1,0:T(8,128)(2,1)S(1)} %fusion.27), channel_id=1, source_target_pairs={{0,6},{1,3},{2,4},{3,1},{4,2},{5,7},{6,0},{7,5},{8,14},{9,11},{10,... | collective-permute-start | bytes 196616 | tf_op jit(solution)/shard_map/ppermute | solution.py:841

commit v4 on v3

--- a/solution.py
+++ b/solution.py
@@ -22,9 +22,10 @@
 GROUPS = D // GW
 HEADS = GW // HD
 ACT, MERGED, FIRST_OWN, GB, GA, FIRST = 0, 512, 640, 640, 896, 1152
-ZED, NORMED, SECOND_OWN, GP, SECOND = 0, 128, 256, 256, 1280
+ZED, NORMED, ZED_Z, SECOND_OWN, GP, SECOND = 0, 128, 256, 384, 384, 1408
 LINES, THIRD_OWN, GQKV, THIRD = 0, 128, 128, 896
 TURNS = "dquqduqduqduqdudqu"
+UP = 3584
 BITS = 9
 MIB = 1024 * 1024
 
@@ -325,7 +326,7 @@
         return pltpu.make_async_copy(act.at[:, at], act_out.at[:, at], act_sem.at[2, j])
 
     def gp_store(j):
-        rows = pl.ds(pl.multiple_of(GP + T * j, T), T)
+        rows = pl.ds(pl.multiple_of(GP + T * j, 128), T)
         return pltpu.make_async_copy(gp.at[:, columns(j, D)], second_other.at[rows, :], gp_sem.at[j])
 
     def hidden(j, carry):
@@ -349,6 +350,7 @@
 
     lax.fori_loop(0, NEST, hidden, 0)
     store_left(0, zed[...], 1, seconds, ZED)
+    store_left(3, zed[...], 2, seconds, ZED_Z)
     store_left(1, normed[...], 2, seconds, NORMED)
     store_left(2, merged[...], 0, firsts, MERGED)
 
@@ -389,14 +391,14 @@
         sds((2, 512, D), BF16),
         sds((T, FF), BF16),
         sds((4, 4, 4, 2, 8, T), F32),
-        sds((2, 3, 128, D), BF16),
+        sds((2, 4, 128, D), BF16),
         sds((T, D), F32),
         row_b,
         sds((T, T), F32),
         sds((T, GW), jnp.int32),
         sds((T, 1), jnp.int32),
     ]
-    semaphores = [(6,), (2, NEST), (3, NEST), (NEST,), (2, 3), (5,)]
+    semaphores = [(6,), (2, NEST), (3, NEST), (NEST,), (2, 4), (5,)]
     return call(
         front_kernel,
         "front",
@@ -620,7 +622,7 @@
         "mixed_output",
         2 * T * D * FF,
         12 * MIB,
-        24,
+        16,
         in_specs=[vmem()] + [hbm()] * 4,
         out_specs=[hbm()],
         out_shape=[sds((T, D), BF16)],
@@ -699,7 +701,7 @@
         "down_and_out_grad",
         2 * T * D * (FF + D),
         10 * MIB,
-        24,
+        18,
         (2,),
         in_specs=[hbm()] * 3,
         out_specs=[hbm()] * 2,
@@ -732,6 +734,7 @@
     qkv_sent,
     qkv_kept,
     zed,
+    zed_z,
     normed,
     gp,
     gqkv,
@@ -739,6 +742,7 @@
     up_out,
     qkv_out,
     zed_sem,
+    zed_z_sem,
     normed_sem,
     gp_sem,
     gqkv_sem,
@@ -759,17 +763,20 @@
         for i, block in enumerate(block_order("z"))
         for m, ref in enumerate((late_own, four))
     ]
+    zed_z_loads = load_left(split, ZED_Z, 128, "z", zed_z, zed_z_sem)
     normed_loads = load_left(split, NORMED, 128, "z", normed, normed_sem)
     gqkv_loads = [load_right(late, GQKV + T * n, gqkv.at[n], gqkv_sem.at[n]) for n in range(3)]
     stages = [zed_loads + gp_loads[0], *gp_loads[1:], normed_loads + gqkv_loads[0]]
-    stages += [gqkv_loads[1], gqkv_loads[2] + line_loads, []]
+    stages += [gqkv_loads[1], gqkv_loads[2] + zed_z_loads + line_loads, []]
     stores = []
     start(stages[0] + stages[1])
     for n in range(4):
         wait(stages[n])
         start(stages[n + 2])
-        at = pl.ds(n * D, D)
-        up_out[:, :, at] = nn(zed[...], gp[n]).astype(BF16).reshape(4, 128, D)
+        width = min(D, UP - n * D)
+        at = pl.ds(n * D, width)
+        part = nn(zed[...], gp[n, :, :width])
+        up_out[:, :, at] = part.astype(BF16).reshape(4, 128, width)
         stores += store_out(up_out, at, up_sent, up_kept, up_sem.at[n])
     for n in range(3):
         wait(stages[4 + n])
@@ -777,21 +784,25 @@
         at = pl.ds(n * D, D)
         qkv_out[:, :, at] = nn(normed[...], gqkv[n]).astype(BF16).reshape(4, 128, D)
         stores += store_out(qkv_out, at, qkv_sent, qkv_kept, qkv_sem.at[n])
-    at = pl.ds(3 * D, 128)
-    qkv_out[:, :, at] = (lines[:, 0].astype(F32) + lines[:, 1].astype(F32)).astype(BF16)
+    more = FF - UP
+    part = nn(zed_z[...], gp[3, :, D - more :])
+    qkv_out[:, :, pl.ds(3 * D, more)] = part.astype(BF16).reshape(4, 128, more)
+    both_lines = (lines[:, 0].astype(F32) + lines[:, 1].astype(F32)).astype(BF16)
+    qkv_out[:, :, pl.ds(3 * D + more, 128)] = both_lines
+    at = pl.ds(3 * D, more + 128)
     stores += store_out(qkv_out, at, qkv_sent, qkv_kept, qkv_sem.at[3])
     wait(stores)
 
 
 def up_and_qkv_grads(own, one, two, late_own, three, four, after):
-    up = sds((2, 128, FF), BF16)
-    qkv = sds((2, 128, 3 * D + 128), BF16)
+    up = sds((2, 128, UP), BF16)
+    qkv = sds((2, 128, 3 * D + FF - UP + 128), BF16)
     return call(
         up_and_qkv_kernel,
         "up_and_qkv_grad",
         2 * T * D * (FF + 3 * D),
         16 * MIB,
-        28,
+        24,
         (2, 5),
         in_specs=[hbm()] * 7,
         out_specs=[hbm()] * 4,
@@ -799,11 +810,13 @@
         scratch_shapes=[
             pltpu.VMEM((512, 2 * T), BF16),
             pltpu.VMEM((512, 2 * T), BF16),
+            pltpu.VMEM((512, 2 * T), BF16),
             pltpu.VMEM((4, 2 * T, D), BF16),
             pltpu.VMEM((3, 2 * T, D), BF16),
             pltpu.VMEM((4, 2, 128, 128), BF16),
-            pltpu.VMEM((4, 128, FF), BF16),
-            pltpu.VMEM((4, 128, 3 * D + 128), BF16),
+            pltpu.VMEM((4, 128, UP), BF16),
+            pltpu.VMEM((4, 128, 3 * D + FF - UP + 128), BF16),
+            pltpu.SemaphoreType.DMA((4, 2)),
             pltpu.SemaphoreType.DMA((4, 2)),
             pltpu.SemaphoreType.DMA((4, 2)),
             pltpu.SemaphoreType.DMA((4, 2)),
@@ -952,25 +965,28 @@
         return grads["out"]
 
     def up_done(*terms):
-        grads["up"] = total(terms)
+        grads["up"] = jnp.concatenate([total(terms), grads["more_up"]], 1)
         return grads["up"]
 
     def qkv_done(*terms):
         grads["qkv"] = total(terms, every, slice(0, 3 * D))
-        line = total(terms, every, slice(3 * D, 3 * D + 128))
+        end = 3 * D + FF - UP
+        grads["more_up"] = total(terms, every, slice(3 * D, end))
+        line = total(terms, every, slice(end, end + 128))
         grads["gains"] = [line[:, n] for n in range(3)]
         bits = line[0, 3 : 3 + BITS * NEST].astype(jnp.int32).reshape(NEST, BITS)
         grads["counts"] = jnp.sum(bits << jnp.arange(BITS, dtype=jnp.int32)[None, :], 1)
-        done = (grads["qkv"], grads["counts"], *grads["gains"])
-        grads["qkv"], grads["counts"], *grads["gains"] = lax.optimization_barrier(done)
+        done = (grads["qkv"], grads["more_up"], grads["counts"], *grads["gains"])
+        done = lax.optimization_barrier(done)
+        grads["qkv"], grads["more_up"], grads["counts"], *grads["gains"] = done
         return grads["qkv"]
 
     take_turns(
         mixed,
         TURNS,
         d=chain(down_sent, down_kept, "yxz", (4, 4, 32, D + T), down_done),
-        u=chain(up_sent, up_kept, "xyz", (4, 4, 8, FF), up_done),
-        q=chain(qkv_sent, qkv_kept, "zyx", (4, 4, 8, 3 * D + 128), qkv_done),
+        u=chain(up_sent, up_kept, "xyz", (4, 4, 8, UP), up_done),
+        q=chain(qkv_sent, qkv_kept, "zyx", (4, 4, 8, 3 * D + FF - UP + 128), qkv_done),
     )
     gain_grad, ln_gain_grad, ln_bias_grad = grads["gains"]
     return (

time: 138 us -> 135 us (0.978)
  waiting for transfers between devices: 41.9 us -> 30.1 us
  starting transfers between devices: 26.3 us -> 34.2 us
    ppermute x9, waiting for transfers between devices: 21.7 us -> 13.2 us  [chain(): got_2 = lax.ppermute(more, (axis, 'c'), pairs(3, 1))]
    ppermute x9, starting transfers between devices: 17.7 us -> 22.5 us  [chain(): got_2 = lax.ppermute(more, (axis, 'c'), pairs(3, 1))]
    ppermute x9, waiting for transfers between devices: 20.1 us -> 16.9 us  [chain(): got = lax.ppermute(sent, (axis, 'c'), pairs(1, 3))]
    ppermute x9, starting transfers between devices: 7.63 us -> 10.8 us  [chain(): got = lax.ppermute(sent, (axis, 'c'), pairs(1, 3))]
  transfers between devices with their start and end apart: 21 -> 21, of which waited for: 8 -> 9; matrix products, arithmetic and copies ran while one was open for 8% -> 9% of each run, Pallas kernels for 25% -> 26%
where the time goes in v4:
time: 135 us; the launch traced here: 134 us
  Pallas kernels  56.7 us (42%)
  starting transfers between devices  34.2 us (25%)
  waiting for transfers between devices  30.1 us (22%)
  other arithmetic  11.6 us (9%)
    pallas_call x5, Pallas kernels, placed(): run(*(pltpu.with_memory_space_constraint(arg, pltpu.HBM) if in_hbm(spec)...  56.7 us
    ppermute x9, starting transfers between devices, chain(): got_2 = lax.ppermute(more, (axis, 'c'), pairs(3, 1))  22.5 us
    ppermute x9, waiting for transfers between devices, chain(): got = lax.ppermute(sent, (axis, 'c'), pairs(1, 3))  16.9 us
    ppermute x9, waiting for transfers between devices, chain(): got_2 = lax.ppermute(more, (axis, 'c'), pairs(3, 1))  13.2 us
    ppermute x9, starting transfers between devices, chain(): got = lax.ppermute(sent, (axis, 'c'), pairs(1, 3))  10.8 us
    another operation x12, other arithmetic, chain(): kept = jnp.stack([own, second])  4.48 us
    convert_element_type x9, other arithmetic, chain(): more = (got[1].astype(F32) + kept[1].astype(F32)).astype(BF16)  3.54 us
  transfers between devices with their start and end apart: 21, of which 9 were waited for; matrix products, arithmetic and copies ran while one was open for 9% of the time, Pallas kernels for 26%

profile of v4, /device:TPU:0, one launch (start us, length us, event | category | flops | bytes accessed | tf_op | source)
XLA Modules:
  0.0 134.5 jit_solution(17334678654578692491)
XLA Ops:
  0.7 22.2 %front.1 = (f32[8,1024]{1,0:T(8,128)}, bf16[640,1024]{1,0:T(8,128)(2,1)}, bf16[1152,1024]{1,0:T(8,128)(2,1)}, bf16[384,1024]{1,0:T(8,128)(2,1)}, bf16[1408,1024]...) custom-call(s32[1,3]{1,0:T(1,128)} %lengths.3, s32[1,3]{1,0:T(1,128)} %heads.3, ...), custom_call_target="tpu_custom_call" | custom-call | flops 8589934592 | bytes 41943040 | tf_op jit(solution)/shard_map/front/pallas_call | solution.py:78
  23.5 12.0 %back.1 = (bf16[128,1024]{1,0:T(8,128)(2,1)}, bf16[896,1024]{1,0:T(8,128)(2,1)}, f32[256,1024]{1,0:T(8,128)}) custom-call(s32[1,3]{1,0:T(1,128)S(1)} %copy-done.3, s32[1,3]{1,0:T(1,128)S(1)} %copy-done.4, f32[1,1024]{1,0:T(1,128)S(1)} %bitcast.136, f32[1,128]{1,0:T(1,128)S(1)} %copy-done.5, s32[1,256]{1,0:T(1,128)S(1)} %bitcast.138, ...), custom_call_target="tpu_custom_call" | custom-call | flops 4831838208 | bytes 18874368 | tf_op jit(solution)/shard_map/back/pallas_call | solution.py:78
  35.8 6.2 %down_and_out_grad.1 = (bf16[2,512,1280]{2,1,0:T(8,128)(2,1)}, bf16[2,512,1280]{2,1,0:T(8,128)(2,1)}) custom-call(bf16[640,1024]{1,0:T(8,128)(2,1)} %get-tuple-element.90.own, bf16[1152,1024]{1,0:T(8,128)(2,1)} %get-tuple-element.86.first_other.one, bf16[1152,1024]{1,0:T(8,128)(2,1)S(1)} %collective-permute-done.2.two), custom_call_target="tpu_custom_call" | custom-call | flops 2684354560 | bytes 10485760 | tf_op jit(solution)/shard_map/down_and_out_grad/pallas_call | solution.py:78
  42.0 1.7 %collective-permute-start.4 = (bf16[2,512,1280]{2,1,0:T(8,128)(2,1)}, bf16[2,512,1280]{2,1,0:T(8,128)(2,1)S(1)}, u32[]{:S(2)}, u32[]{:S(2)}) collective-permute-start(bf16[2,512,1280]{2,1,0:T(8,128)(2,1)} %get-tuple-element.92.after), channel_id=1, source_target_pairs={{0,32},{1,97},{32,0},{33,65},{64,96},{65,33},{96,64},{97,1},{2,34}... | collective-permute-start | bytes 7864328 | tf_op jit(solution)/shard_map/ppermute | solution.py:850
  43.8 8.4 %up_and_qkv_grad.1 = (bf16[2,128,3584]{2,1,0:T(8,128)(2,1)}, bf16[2,128,3584]{2,1,0:T(8,128)(2,1)}, bf16[2,128,3712]{2,1,0:T(8,128)(2,1)}, bf16[2,128,3712]{2,1,0:T(8,128)(2,1)}) custom-call(bf16[384,1024]{1,0:T(8,128)(2,1)} %get-tuple-element.83.own, bf16[1408,1024]{1,0:T(8,128)(2,1)} %get-tuple-element.84.one, ...), custom_call_target="tpu_custom_call" | custom-call | flops 3758096384 | bytes 16777216 | tf_op jit(solution)/shard_map/up_and_qkv_grad/pallas_call | solution.py:78
  52.1 2.0 %collective-permute-start.3 = (bf16[2,128,3712]{2,1,0:T(8,128)(2,1)}, bf16[2,128,3712]{2,1,0:T(8,128)(2,1)}, u32[]{:S(2)}, u32[]{:S(2)}) collective-permute-start(bf16[2,128,3712]{2,1,0:T(8,128)(2,1)} %get-tuple-element.93.after), channel_id=1, source_target_pairs={{0,2},{1,7},{2,0},{3,5},{4,6},{5,3},{6,4},{7,1},{8,10},{9,15},{10,... | collective-permute-start | bytes 5701640 | tf_op jit(solution)/shard_map/ppermute | solution.py:850
  54.1 1.5 %collective-permute-start.6 = (bf16[2,128,3584]{2,1,0:T(8,128)(2,1)}, bf16[2,128,3584]{2,1,0:T(8,128)(2,1)}, u32[]{:S(2)}, u32[]{:S(2)}) collective-permute-start(bf16[2,128,3584]{2,1,0:T(8,128)(2,1)} %get-tuple-element.101), channel_id=1, source_target_pairs={{0,8},{1,25},{8,0},{9,17},{16,24},{17,9},{24,16},{25,1},{2,10},{3,... | collective-permute-start | bytes 5505032 | tf_op jit(solution)/shard_map/ppermute | solution.py:850
  55.6 8.0 %mixed_output.1 = bf16[256,1024]{1,0:T(8,128)(2,1)} custom-call(f32[1,256]{1,0:T(1,128)S(1)} %bitcast.134, f32[256,1024]{1,0:T(8,128)} %get-tuple-element.81.middle_hbm, bf16[256,4096]{1,0:T(8,128)(2,1)} %get-tuple-element.82.act_hbm, bf16[4096,1024]{1,0:T(8,128)(2,1)} %down_hbm.3, bf16[2,128,3712]{2,1,0:T(8,128)(2,1)} %get-tuple-element.93.after), custom_call_target="tpu_custom_call" | custom-call | flops 2147483648 | bytes 12582912 | tf_op jit(solution)/shard_map/mixed_output/pallas_call | solution.py:78
  63.6 10.3 %collective-permute-done.4 = bf16[2,512,1280]{2,1,0:T(8,128)(2,1)S(1)} collective-permute-done((bf16[2,512,1280]{2,1,0:T(8,128)(2,1)}, bf16[2,512,1280]{2,1,0:T(8,128)(2,1)S(1)}, u32[]{:S(2)}, u32[]{:S(2)}) %collective-permute-start.4) | collective-permute-done | bytes 2621472 | tf_op jit(solution)/shard_map/ppermute | solution.py:850
  74.3 3.2 %collective-permute-start.9 = (bf16[512,1280]{1,0:T(8,128)(2,1)S(1)}, bf16[512,1280]{1,0:T(8,128)(2,1)S(1)}, u32[]{:S(2)}, u32[]{:S(2)}) collective-permute-start(bf16[512,1280]{1,0:T(8,128)(2,1)S(1)} %fusion), channel_id=1, source_target_pairs={{0,96},{1,33},{32,64},{33,1},{64,32},{65,97},{96,0},{97,65},{2,98}... | collective-permute-start | bytes 3932168 | tf_op jit(solution)/shard_map/ppermute | solution.py:854
  77.5 1.5 %fusion.1 = bf16[128,3712]{1,0:T(8,128)(2,1)S(1)} fusion(bf16[2,128,3712]{2,1,0:T(8,128)(2,1)S(1)} %copy-done.7, bf16[2,128,3712]{2,1,0:T(8,128)(2,1)} %collective-permute-done.3), kind=kLoop, calls=%fused_computation.5 | loop fusion | flops 1900544 | bytes 2850816 | tf_op jit(solution)/shard_map/convert_element_type | solution.py:853
  79.0 4.1 %collective-permute-start.5 = (bf16[128,3712]{1,0:T(8,128)(2,1)S(1)}, bf16[128,3712]{1,0:T(8,128)(2,1)S(1)}, u32[]{:S(2)}, u32[]{:S(2)}) collective-permute-start(bf16[128,3712]{1,0:T(8,128)(2,1)S(1)} %fusion.1), channel_id=1, source_target_pairs={{0,6},{1,3},{2,4},{3,1},{4,2},{5,7},{6,0},{7,5},{8,14},{9,11},{10,... | collective-permute-start | bytes 2850824 | tf_op jit(solution)/shard_map/ppermute | solution.py:854
  83.1 1.5 %fusion.2 = bf16[128,3584]{1,0:T(8,128)(2,1)S(1)} fusion(bf16[2,128,3584]{2,1,0:T(8,128)(2,1)S(1)} %copy-done.8, bf16[2,128,3584]{2,1,0:T(8,128)(2,1)} %collective-permute-done.6), kind=kLoop, calls=%fused_computation.7 | loop fusion | flops 1835008 | bytes 2752512 | tf_op jit(solution)/shard_map/convert_element_type | solution.py:853
  84.6 2.8 %collective-permute-start.8 = (bf16[128,3584]{1,0:T(8,128)(2,1)S(1)}, bf16[128,3584]{1,0:T(8,128)(2,1)S(1)}, u32[]{:S(2)}, u32[]{:S(2)}) collective-permute-start(bf16[128,3584]{1,0:T(8,128)(2,1)S(1)} %fusion.2), channel_id=1, source_target_pairs={{0,24},{1,9},{8,16},{9,1},{16,8},{17,25},{24,0},{25,17},{2,26},{3,... | collective-permute-start | bytes 2752520 | tf_op jit(solution)/shard_map/ppermute | solution.py:854
  87.4 7.4 %collective-permute-done.5 = bf16[128,3712]{1,0:T(8,128)(2,1)S(1)} collective-permute-done((bf16[128,3712]{1,0:T(8,128)(2,1)S(1)}, bf16[128,3712]{1,0:T(8,128)(2,1)S(1)}, u32[]{:S(2)}, u32[]{:S(2)}) %collective-permute-start.5) | collective-permute-done | bytes 950304 | tf_op jit(solution)/shard_map/ppermute | solution.py:854
  94.9 1.7 %add_bitcast_fusion.3 = (f32[1,4,8,3712]{3,2,1,0:T(8,128)S(1)}, f32[1,4,8,3712]{3,2,1,0:T(8,128)S(1)}, bf16[1,4,8,3712]{3,2,1,0:T(8,128)(2,1)S(1)}, bf16[1,4,8,3712]{3,2,1,0:T(8,128)(2,1)S(1)}) fusion(bf16[1,4,4,8,3712]{4,3,2,1,0:T(8,128)(2,1)S(1)} %bitcast.144, s32[]{:T(128)S(6)} %select_n.26, bf16[2,4,4,8,3712]{4,3,2,1,0:T(8,128)(2,1)S(1)} %bitcast.141, ...), kind=kLoop, calls=%fused_computation.18 | loop fusion | flops 2613248 | bytes 4276240 | tf_op jit(solution)/shard_map/stack;reshape | solution.py:876
  97.6 1.6 %collective-permute-start.12 = (bf16[2,4,32,1280]{3,2,1,0:T(8,128)(2,1)S(1)}, bf16[2,4,32,1280]{3,2,1,0:T(8,128)(2,1)S(1)}, u32[]{:S(2)}, u32[]{:S(2)}) collective-permute-start(bf16[2,4,32,1280]{3,2,1,0:T(8,128)(2,1)S(1)} %pad_maximum_fusion.3), channel_id=1, source_target_pairs={{0,8},{1,25},{8,0},{9,17},{16,24},{17,9},{24,16},{25,1},{2,10},{3,... | collective-permute-start | bytes 1966088 | tf_op jit(solution)/shard_map/ppermute | solution.py:850
  99.3 1.6 %add_bitcast_fusion.5 = (f32[1,4,8,3584]{3,2,1,0:T(8,128)S(1)}, f32[1,4,8,3584]{3,2,1,0:T(8,128)S(1)}, bf16[1,4,8,3584]{3,2,1,0:T(8,128)(2,1)S(1)}, bf16[1,4,8,3584]{3,2,1,0:T(8,128)(2,1)S(1)}) fusion(bf16[1,4,4,8,3584]{4,3,2,1,0:T(8,128)(2,1)S(1)} %bitcast.145, s32[]{:T(128)S(6)} %select_n.26, bf16[2,4,4,8,3584]{4,3,2,1,0:T(8,128)(2,1)S(1)} %bitcast.142, ...), kind=kLoop, calls=%fused_computation.24 | loop fusion | flops 2523136 | bytes 4128784 | tf_op jit(solution)/shard_map/stack;reshape | solution.py:876
  101.0 1.8 %collective-permute-start.11 = (bf16[2,4,8,3584]{3,2,1,0:T(8,128)(2,1)S(1)}, bf16[2,4,8,3584]{3,2,1,0:T(8,128)(2,1)S(1)}, u32[]{:S(2)}, u32[]{:S(2)}) collective-permute-start(bf16[2,4,8,3584]{3,2,1,0:T(8,128)(2,1)S(1)} %pad_maximum_fusion.5), channel_id=1, source_target_pairs={{0,32},{1,97},{32,0},{33,65},{64,96},{65,33},{96,64},{97,1},{2,34}... | collective-permute-start | bytes 1376264 | tf_op jit(solution)/shard_map/ppermute | solution.py:850
  103.0 2.4 %collective-permute-done.7 = bf16[2,4,8,3712]{3,2,1,0:T(8,128)(2,1)S(1)} collective-permute-done((bf16[2,4,8,3712]{3,2,1,0:T(8,128)(2,1)S(1)}, bf16[2,4,8,3712]{3,2,1,0:T(8,128)(2,1)S(1)}, u32[]{:S(2)}, u32[]{:S(2)}) %collective-permute-start.7) | collective-permute-done | bytes 475168 | tf_op jit(solution)/shard_map/ppermute | solution.py:850
  105.4 1.2 collective-permute-start.10
  106.6 1.6 %collective-permute-done.12 = bf16[2,4,32,1280]{3,2,1,0:T(8,128)(2,1)S(1)} collective-permute-done((bf16[2,4,32,1280]{3,2,1,0:T(8,128)(2,1)S(1)}, bf16[2,4,32,1280]{3,2,1,0:T(8,128)(2,1)S(1)}, u32[]{:S(2)}, u32[]{:S(2)}) %collective-permute-start.12) | collective-permute-done | bytes 655392 | tf_op jit(solution)/shard_map/ppermute | solution.py:850
  108.3 2.8 %collective-permute-start.15 = (bf16[4,32,1280]{2,1,0:T(8,128)(2,1)S(1)}, bf16[4,32,1280]{2,1,0:T(8,128)(2,1)S(1)}, u32[]{:S(2)}, u32[]{:S(2)}) collective-permute-start(bf16[4,32,1280]{2,1,0:T(8,128)(2,1)S(1)} %fusion.5), channel_id=1, source_target_pairs={{0,24},{1,9},{8,16},{9,1},{16,8},{17,25},{24,0},{25,17},{2,26},{3,... | collective-permute-start | bytes 983048 | tf_op jit(solution)/shard_map/ppermute | solution.py:854
  111.1 2.6 %collective-permute-done.11 = bf16[2,4,8,3584]{3,2,1,0:T(8,128)(2,1)S(1)} collective-permute-done((bf16[2,4,8,3584]{3,2,1,0:T(8,128)(2,1)S(1)}, bf16[2,4,8,3584]{3,2,1,0:T(8,128)(2,1)S(1)}, u32[]{:S(2)}, u32[]{:S(2)}) %collective-permute-start.11) | collective-permute-done | bytes 458784 | tf_op jit(solution)/shard_map/ppermute | solution.py:850
  114.5 1.8 %collective-permute-start.13 = (bf16[2,8,3712]{2,1,0:T(8,128)(2,1)S(1)}, bf16[2,8,3712]{2,1,0:T(8,128)(2,1)S(1)}, u32[]{:S(2)}, u32[]{:S(2)}) collective-permute-start(bf16[2,8,3712]{2,1,0:T(8,128)(2,1)S(1)} %pad_maximum_fusion.11), channel_id=1, source_target_pairs={{0,8},{1,25},{8,0},{9,17},{16,24},{17,9},{24,16},{25,1},{2,10},{3,... | collective-permute-start | bytes 356360 | tf_op jit(solution)/shard_map/ppermute | solution.py:850
  116.3 1.0 collective-permute-done.15
  117.5 3.6 %collective-permute-done.14 = bf16[4,8,3584]{2,1,0:T(8,128)(2,1)S(1)} collective-permute-done((bf16[4,8,3584]{2,1,0:T(8,128)(2,1)S(1)}, bf16[4,8,3584]{2,1,0:T(8,128)(2,1)S(1)}, u32[]{:S(2)}, u32[]{:S(2)}) %collective-permute-start.14) | collective-permute-done | bytes 229408 | tf_op jit(solution)/shard_map/ppermute | solution.py:854
  121.3 2.8 %collective-permute-start.16 = (bf16[8,3712]{1,0:T(8,128)(2,1)S(1)}, bf16[8,3712]{1,0:T(8,128)(2,1)S(1)}, u32[]{:S(2)}, u32[]{:S(2)}) collective-permute-start(bf16[8,3712]{1,0:T(8,128)(2,1)S(1)} %fusion.27), channel_id=1, source_target_pairs={{0,24},{1,9},{8,16},{9,1},{16,8},{17,25},{24,0},{25,17},{2,26},{3,... | collective-permute-start | bytes 178184 | tf_op jit(solution)/shard_map/ppermute | solution.py:854
  124.2 3.6 %collective-permute-start.18 = (bf16[32,1280]{1,0:T(8,128)(2,1)S(1)}, bf16[32,1280]{1,0:T(8,128)(2,1)S(1)}, u32[]{:S(2)}, u32[]{:S(2)}) collective-permute-start(bf16[32,1280]{1,0:T(8,128)(2,1)S(1)} %fusion.24), channel_id=1, source_target_pairs={{0,6},{1,3},{2,4},{3,1},{4,2},{5,7},{6,0},{7,5},{8,14},{9,11},{10,... | collective-permute-start | bytes 245768 | tf_op jit(solution)/shard_map/ppermute | solution.py:854
  127.9 1.3 collective-permute-start.20
  129.2 1.1 collective-permute-done.18
  132.3 0.7 slice_reduce_fusion
  (71 shorter events, 7.5 us)
Async XLA Ops:
  0.6 22.8 %copy-start.1 = (f32[1024]{0:T(1024)S(1)}, f32[1024]{0:T(1024)}, u32[]{:S(2)}) copy-start(f32[1024]{0:T(1024)} %param.15) | copy-start | bytes 12292
  0.7 22.8 %copy-start.2 = (s32[256,1]{0,1:T(1,128)S(1)}, s32[256,1]{0,1:T(1,128)}, u32[]{:S(2)}) copy-start(s32[256,1]{0,1:T(1,128)} %param.22) | copy-start | bytes 3076
  0.7 22.8 %copy-start.3 = (s32[1,3]{1,0:T(1,128)S(1)}, s32[1,3]{1,0:T(1,128)}, u32[]{:S(2)}) copy-start(s32[1,3]{1,0:T(1,128)} %lengths.3) | copy-start | bytes 40
  0.7 22.8 %copy-start.4 = (s32[1,3]{1,0:T(1,128)S(1)}, s32[1,3]{1,0:T(1,128)}, u32[]{:S(2)}) copy-start(s32[1,3]{1,0:T(1,128)} %heads.3) | copy-start | bytes 40
  0.7 22.8 %copy-start.5 = (f32[1,128]{1,0:T(1,128)S(1)}, f32[1,128]{1,0:T(1,128)}, u32[]{:S(2)}) copy-start(f32[1,128]{1,0:T(1,128)} %constant.27.clone.inverse) | copy-start | bytes 1540
  22.9 13.0 %collective-permute-start.2 = (bf16[1152,1024]{1,0:T(8,128)(2,1)}, bf16[1152,1024]{1,0:T(8,128)(2,1)S(1)}, u32[]{:S(2)}, u32[]{:S(2)}) collective-permute-start(bf16[1152,1024]{1,0:T(8,128)(2,1)} %get-tuple-element.86.first_other.one), channel_id=1, source_target_pairs={{0,1},{1,0},{2,3},{3,2},{4,5},{5,4},{6,7},{7,6},{8,9},{9,8},{10,11... | collective-permute-start | bytes 7077896 | tf_op jit(solution)/shard_map/ppermute | solution.py:832
  22.9 20.8 %collective-permute-start = (bf16[1408,1024]{1,0:T(8,128)(2,1)}, bf16[1408,1024]{1,0:T(8,128)(2,1)S(1)}, u32[]{:S(2)}, u32[]{:S(2)}) collective-permute-start(bf16[1408,1024]{1,0:T(8,128)(2,1)} %get-tuple-element.84.one), channel_id=1, source_target_pairs={{0,1},{1,0},{2,3},{3,2},{4,5},{5,4},{6,7},{7,6},{8,9},{9,8},{10,11... | collective-permute-start | bytes 8650760 | tf_op jit(solution)/shard_map/ppermute | solution.py:832
  35.5 8.3 %collective-permute-start.1 = (bf16[896,1024]{1,0:T(8,128)(2,1)}, bf16[896,1024]{1,0:T(8,128)(2,1)S(1)}, u32[]{:S(2)}, u32[]{:S(2)}) collective-permute-start(bf16[896,1024]{1,0:T(8,128)(2,1)} %get-tuple-element.89.three), channel_id=1, source_target_pairs={{0,1},{1,0},{2,3},{3,2},{4,5},{5,4},{6,7},{7,6},{8,9},{9,8},{10,11... | collective-permute-start | bytes 5505032 | tf_op jit(solution)/shard_map/ppermute | solution.py:832
  42.0 31.9 %collective-permute-start.4 = (bf16[2,512,1280]{2,1,0:T(8,128)(2,1)}, bf16[2,512,1280]{2,1,0:T(8,128)(2,1)S(1)}, u32[]{:S(2)}, u32[]{:S(2)}) collective-permute-start(bf16[2,512,1280]{2,1,0:T(8,128)(2,1)} %get-tuple-element.92.after), channel_id=1, source_target_pairs={{0,32},{1,97},{32,0},{33,65},{64,96},{65,33},{96,64},{97,1},{2,34}... | collective-permute-start | bytes 7864328 | tf_op jit(solution)/shard_map/ppermute | solution.py:850
  43.7 11.9 %copy-start = (f32[256]{0:T(256)S(1)}, f32[256]{0:T(256)}, u32[]{:S(2)}) copy-start(f32[256]{0:T(256)} %param.23) | copy-start | bytes 3076
  52.1 25.4 %collective-permute-start.3 = (bf16[2,128,3712]{2,1,0:T(8,128)(2,1)}, bf16[2,128,3712]{2,1,0:T(8,128)(2,1)}, u32[]{:S(2)}, u32[]{:S(2)}) collective-permute-start(bf16[2,128,3712]{2,1,0:T(8,128)(2,1)} %get-tuple-element.93.after), channel_id=1, source_target_pairs={{0,2},{1,7},{2,0},{3,5},{4,6},{5,3},{6,4},{7,1},{8,10},{9,15},{10,... | collective-permute-start | bytes 5701640 | tf_op jit(solution)/shard_map/ppermute | solution.py:850
  54.1 29.0 %collective-permute-start.6 = (bf16[2,128,3584]{2,1,0:T(8,128)(2,1)}, bf16[2,128,3584]{2,1,0:T(8,128)(2,1)}, u32[]{:S(2)}, u32[]{:S(2)}) collective-permute-start(bf16[2,128,3584]{2,1,0:T(8,128)(2,1)} %get-tuple-element.101), channel_id=1, source_target_pairs={{0,8},{1,25},{8,0},{9,17},{16,24},{17,9},{24,16},{25,1},{2,10},{3,... | collective-permute-start | bytes 5505032 | tf_op jit(solution)/shard_map/ppermute | solution.py:850
  55.6 18.3 %copy-start.6 = (bf16[2,512,1280]{2,1,0:T(8,128)(2,1)S(1)}, bf16[2,512,1280]{2,1,0:T(8,128)(2,1)}, u32[]{:S(2)}) copy-start(bf16[2,512,1280]{2,1,0:T(8,128)(2,1)} %get-tuple-element.109) | copy-start | bytes 7864324
  73.9 3.6 %copy-start.7 = (bf16[2,128,3712]{2,1,0:T(8,128)(2,1)S(1)}, bf16[2,128,3712]{2,1,0:T(8,128)(2,1)}, u32[]{:S(2)}) copy-start(bf16[2,128,3712]{2,1,0:T(8,128)(2,1)} %get-tuple-element.106) | copy-start | bytes 5701636
  74.3 8.8 %copy-start.8 = (bf16[2,128,3584]{2,1,0:T(8,128)(2,1)S(1)}, bf16[2,128,3584]{2,1,0:T(8,128)(2,1)}, u32[]{:S(2)}) copy-start(bf16[2,128,3584]{2,1,0:T(8,128)(2,1)} %get-tuple-element.112) | copy-start | bytes 5505028
  74.3 22.6 %collective-permute-start.9 = (bf16[512,1280]{1,0:T(8,128)(2,1)S(1)}, bf16[512,1280]{1,0:T(8,128)(2,1)S(1)}, u32[]{:S(2)}, u32[]{:S(2)}) collective-permute-start(bf16[512,1280]{1,0:T(8,128)(2,1)S(1)} %fusion), channel_id=1, source_target_pairs={{0,96},{1,33},{32,64},{33,1},{64,32},{65,97},{96,0},{97,65},{2,98}... | collective-permute-start | bytes 3932168 | tf_op jit(solution)/shard_map/ppermute | solution.py:854
  79.0 15.8 %collective-permute-start.5 = (bf16[128,3712]{1,0:T(8,128)(2,1)S(1)}, bf16[128,3712]{1,0:T(8,128)(2,1)S(1)}, u32[]{:S(2)}, u32[]{:S(2)}) collective-permute-start(bf16[128,3712]{1,0:T(8,128)(2,1)S(1)} %fusion.1), channel_id=1, source_target_pairs={{0,6},{1,3},{2,4},{3,1},{4,2},{5,7},{6,0},{7,5},{8,14},{9,11},{10,... | collective-permute-start | bytes 2850824 | tf_op jit(solution)/shard_map/ppermute | solution.py:854
  84.6 14.7 %collective-permute-start.8 = (bf16[128,3584]{1,0:T(8,128)(2,1)S(1)}, bf16[128,3584]{1,0:T(8,128)(2,1)S(1)}, u32[]{:S(2)}, u32[]{:S(2)}) collective-permute-start(bf16[128,3584]{1,0:T(8,128)(2,1)S(1)} %fusion.2), channel_id=1, source_target_pairs={{0,24},{1,9},{8,16},{9,1},{16,8},{17,25},{24,0},{25,17},{2,26},{3,... | collective-permute-start | bytes 2752520 | tf_op jit(solution)/shard_map/ppermute | solution.py:854
  96.6 8.7 %collective-permute-start.7 = (bf16[2,4,8,3712]{3,2,1,0:T(8,128)(2,1)S(1)}, bf16[2,4,8,3712]{3,2,1,0:T(8,128)(2,1)S(1)}, u32[]{:S(2)}, u32[]{:S(2)}) collective-permute-start(bf16[2,4,8,3712]{3,2,1,0:T(8,128)(2,1)S(1)} %pad_maximum_fusion.4), channel_id=1, source_target_pairs={{0,32},{1,97},{32,0},{33,65},{64,96},{65,33},{96,64},{97,1},{2,34}... | collective-permute-start | bytes 1425416 | tf_op jit(solution)/shard_map/ppermute | solution.py:850
  97.6 10.7 %collective-permute-start.12 = (bf16[2,4,32,1280]{3,2,1,0:T(8,128)(2,1)S(1)}, bf16[2,4,32,1280]{3,2,1,0:T(8,128)(2,1)S(1)}, u32[]{:S(2)}, u32[]{:S(2)}) collective-permute-start(bf16[2,4,32,1280]{3,2,1,0:T(8,128)(2,1)S(1)} %pad_maximum_fusion.3), channel_id=1, source_target_pairs={{0,8},{1,25},{8,0},{9,17},{16,24},{17,9},{24,16},{25,1},{2,10},{3,... | collective-permute-start | bytes 1966088 | tf_op jit(solution)/shard_map/ppermute | solution.py:850
  101.0 12.7 %collective-permute-start.11 = (bf16[2,4,8,3584]{3,2,1,0:T(8,128)(2,1)S(1)}, bf16[2,4,8,3584]{3,2,1,0:T(8,128)(2,1)S(1)}, u32[]{:S(2)}, u32[]{:S(2)}) collective-permute-start(bf16[2,4,8,3584]{3,2,1,0:T(8,128)(2,1)S(1)} %pad_maximum_fusion.5), channel_id=1, source_target_pairs={{0,32},{1,97},{32,0},{33,65},{64,96},{65,33},{96,64},{97,1},{2,34}... | collective-permute-start | bytes 1376264 | tf_op jit(solution)/shard_map/ppermute | solution.py:850
  105.4 8.9 %collective-permute-start.10 = (bf16[4,8,3712]{2,1,0:T(8,128)(2,1)S(1)}, bf16[4,8,3712]{2,1,0:T(8,128)(2,1)S(1)}, u32[]{:S(2)}, u32[]{:S(2)}) collective-permute-start(bf16[4,8,3712]{2,1,0:T(8,128)(2,1)S(1)} %fusion.8), channel_id=1, source_target_pairs={{0,96},{1,33},{32,64},{33,1},{64,32},{65,97},{96,0},{97,65},{2,98}... | collective-permute-start | bytes 712712 | tf_op jit(solution)/shard_map/ppermute | solution.py:854
  108.3 9.0 %collective-permute-start.15 = (bf16[4,32,1280]{2,1,0:T(8,128)(2,1)S(1)}, bf16[4,32,1280]{2,1,0:T(8,128)(2,1)S(1)}, u32[]{:S(2)}, u32[]{:S(2)}) collective-permute-start(bf16[4,32,1280]{2,1,0:T(8,128)(2,1)S(1)} %fusion.5), channel_id=1, source_target_pairs={{0,24},{1,9},{8,16},{9,1},{16,8},{17,25},{24,0},{25,17},{2,26},{3,... | collective-permute-start | bytes 983048 | tf_op jit(solution)/shard_map/ppermute | solution.py:854
  113.8 7.3 %collective-permute-start.14 = (bf16[4,8,3584]{2,1,0:T(8,128)(2,1)S(1)}, bf16[4,8,3584]{2,1,0:T(8,128)(2,1)S(1)}, u32[]{:S(2)}, u32[]{:S(2)}) collective-permute-start(bf16[4,8,3584]{2,1,0:T(8,128)(2,1)S(1)} %fusion.11), channel_id=1, source_target_pairs={{0,96},{1,33},{32,64},{33,1},{64,32},{65,97},{96,0},{97,65},{2,98}... | collective-permute-start | bytes 688136 | tf_op jit(solution)/shard_map/ppermute | solution.py:854
  114.5 6.8 %collective-permute-start.13 = (bf16[2,8,3712]{2,1,0:T(8,128)(2,1)S(1)}, bf16[2,8,3712]{2,1,0:T(8,128)(2,1)S(1)}, u32[]{:S(2)}, u32[]{:S(2)}) collective-permute-start(bf16[2,8,3712]{2,1,0:T(8,128)(2,1)S(1)} %pad_maximum_fusion.11), channel_id=1, source_target_pairs={{0,8},{1,25},{8,0},{9,17},{16,24},{17,9},{24,16},{25,1},{2,10},{3,... | collective-permute-start | bytes 356360 | tf_op jit(solution)/shard_map/ppermute | solution.py:850
  117.4 6.8 %collective-permute-start.17 = (bf16[2,32,1280]{2,1,0:T(8,128)(2,1)S(1)}, bf16[2,32,1280]{2,1,0:T(8,128)(2,1)S(1)}, u32[]{:S(2)}, u32[]{:S(2)}) collective-permute-start(bf16[2,32,1280]{2,1,0:T(8,128)(2,1)S(1)} %pad_maximum_fusion.9), channel_id=1, source_target_pairs={{0,2},{1,7},{2,0},{3,5},{4,6},{5,3},{6,4},{7,1},{8,10},{9,15},{10,... | collective-permute-start | bytes 491528 | tf_op jit(solution)/shard_map/ppermute | solution.py:850
  121.2 6.7 %collective-permute-start.19 = (bf16[2,8,3584]{2,1,0:T(8,128)(2,1)S(1)}, bf16[2,8,3584]{2,1,0:T(8,128)(2,1)S(1)}, u32[]{:S(2)}, u32[]{:S(2)}) collective-permute-start(bf16[2,8,3584]{2,1,0:T(8,128)(2,1)S(1)} %pad_maximum_fusion.12), channel_id=1, source_target_pairs={{0,2},{1,7},{2,0},{3,5},{4,6},{5,3},{6,4},{7,1},{8,10},{9,15},{10,... | collective-permute-start | bytes 344072 | tf_op jit(solution)/shard_map/ppermute | solution.py:850
  121.3 10.2 %collective-permute-start.16 = (bf16[8,3712]{1,0:T(8,128)(2,1)S(1)}, bf16[8,3712]{1,0:T(8,128)(2,1)S(1)}, u32[]{:S(2)}, u32[]{:S(2)}) collective-permute-start(bf16[8,3712]{1,0:T(8,128)(2,1)S(1)} %fusion.27), channel_id=1, source_target_pairs={{0,24},{1,9},{8,16},{9,1},{16,8},{17,25},{24,0},{25,17},{2,26},{3,... | collective-permute-start | bytes 178184 | tf_op jit(solution)/shard_map/ppermute | solution.py:854
  124.2 6.0 %collective-permute-start.18 = (bf16[32,1280]{1,0:T(8,128)(2,1)S(1)}, bf16[32,1280]{1,0:T(8,128)(2,1)S(1)}, u32[]{:S(2)}, u32[]{:S(2)}) collective-permute-start(bf16[32,1280]{1,0:T(8,128)(2,1)S(1)} %fusion.24), channel_id=1, source_target_pairs={{0,6},{1,3},{2,4},{3,1},{4,2},{5,7},{6,0},{7,5},{8,14},{9,11},{10,... | collective-permute-start | bytes 245768 | tf_op jit(solution)/shard_map/ppermute | solution.py:854
  127.9 5.9 %collective-permute-start.20 = (bf16[8,3584]{1,0:T(8,128)(2,1)S(1)}, bf16[8,3584]{1,0:T(8,128)(2,1)S(1)}, u32[]{:S(2)}, u32[]{:S(2)}) collective-permute-start(bf16[8,3584]{1,0:T(8,128)(2,1)S(1)} %fusion.30), channel_id=1, source_target_pairs={{0,6},{1,3},{2,4},{3,1},{4,2},{5,7},{6,0},{7,5},{8,14},{9,11},{10,... | collective-permute-start | bytes 172040 | tf_op jit(solution)/shard_map/ppermute | solution.py:854

commit v5 on v4

--- a/solution.py
+++ b/solution.py
@@ -243,8 +243,10 @@
 
     stores = []
 
-    def store_left(n, value, axis, refs, at):
+    def turn(value):
         turned_f[...] = value.astype(F32).T.reshape(turned_f.shape)
+
+    def store_left(n, axis, refs, at):
         for side, ref in enumerate(refs):
             half = core if side == 0 else 1 - core
             for i in range(4):
@@ -349,10 +351,13 @@
         return carry
 
     lax.fori_loop(0, NEST, hidden, 0)
-    store_left(0, zed[...], 1, seconds, ZED)
-    store_left(3, zed[...], 2, seconds, ZED_Z)
-    store_left(1, normed[...], 2, seconds, NORMED)
-    store_left(2, merged[...], 0, firsts, MERGED)
+    turn(zed[...])
+    store_left(0, 1, seconds, ZED)
+    store_left(3, 2, seconds, ZED_Z)
+    turn(normed[...])
+    store_left(1, 2, seconds, NORMED)
+    turn(merged[...])
+    store_left(2, 0, firsts, MERGED)
 
     grad_zed = nt(gp[...], up[...]).astype(BF16).astype(F32)
     normed_mid, rstd = normalized(middle[...])
@@ -425,7 +430,6 @@
 def back_kernel(
     lengths,
     heads,
-    norm_gain,
     inverse,
     bucket,
     parts_hbm,
@@ -436,11 +440,11 @@
     wo_hbm,
     third_mine,
     third_other,
-    input_grad_out,
+    grad_normed_out,
     parts,
     ga,
     qkv,
-    input_grad,
+    grad_store,
     tokens,
     wqkv,
     wo,
@@ -538,11 +542,8 @@
     rscale = lax.rsqrt(jnp.mean(resid * resid, -1, keepdims=True) + EPS)
     unit = resid * rscale
     gain_part = jnp.sum(grad_normed * unit, 0, keepdims=True)
-    grad_unit = grad_normed * norm_gain[...]
-    input_grad[...] = ga[...].astype(F32) + rscale * (
-        grad_unit - unit * jnp.mean(grad_unit * unit, -1, keepdims=True)
-    )
-    stores = [load(input_grad, input_grad_out, out_sem.at[0])]
+    grad_store[...] = grad_normed
+    stores = [load(grad_store, grad_normed_out, out_sem.at[0])]
 
     item = lax.broadcasted_iota(jnp.int32, (128, 1), 0)
     count = jnp.zeros((128, 1), jnp.int32)
@@ -565,7 +566,7 @@
     wait(stores)
 
 
-def back(lengths, heads, norm_gain, inverse, bucket, parts, *arrays):
+def back(lengths, heads, inverse, bucket, parts, *arrays):
     scratch = [
         sds((8, D), F32),
         sds((T, D), BF16),
@@ -586,18 +587,42 @@
         2 * T * D * 4 * D + 10 * 16 * T * T * 256,
         18 * MIB,
         32,
-        in_specs=[smem()] * 2 + [vmem()] * 3 + [hbm()] * 6,
+        in_specs=[smem()] * 2 + [vmem()] * 2 + [hbm()] * 6,
         out_specs=[hbm()] * 3,
         out_shape=[sds((THIRD_OWN, D), BF16), sds((THIRD, D), BF16), sds((T, D), F32)],
         scratch_shapes=[pltpu.VMEM(s.shape, s.dtype) for s in scratch]
         + [pltpu.SemaphoreType.DMA(s) for s in [(8,), (3,), (3, GROUPS), (3,)]],
-    )(lengths, heads, norm_gain, inverse, bucket, parts, *arrays)
-
-
-def mixed_kernel(
-    router, middle_hbm, act_hbm, down_hbm, after, mixed_out, middle, act, down, mixed, sem, ffn_sem
+    )(lengths, heads, inverse, bucket, parts, *arrays)
+
+
+def ends_kernel(
+    router,
+    norm_gain,
+    grad_normed_hbm,
+    first_other,
+    tokens_hbm,
+    middle_hbm,
+    act_hbm,
+    down_hbm,
+    after,
+    mixed_out,
+    input_grad_out,
+    grad_normed,
+    ga,
+    tokens,
+    middle,
+    act,
+    down,
+    mixed,
+    sem,
+    ffn_sem,
 ):
-    loads = [load(middle_hbm, middle, sem.at[0])]
+    loads = [
+        load(grad_normed_hbm, grad_normed, sem.at[0]),
+        load(tokens_hbm, tokens, sem.at[1]),
+        load(first_other.at[pl.ds(GA, T), :], ga, sem.at[2]),
+    ]
+    middle_load = load(middle_hbm, middle, sem.at[3])
     stages = []
     for j in range(NEST):
         at = pl.ds(j * D, D)
@@ -608,34 +633,46 @@
             ]
         )
         start(stages[j])
+    wait(loads)
+    resid = tokens[...].astype(F32)
+    rscale = lax.rsqrt(jnp.mean(resid * resid, -1, keepdims=True) + EPS)
+    unit = resid * rscale
+    grad_unit = grad_normed[...] * norm_gain[...]
+    grad_normed[...] = ga[...].astype(F32) + rscale * (
+        grad_unit - unit * jnp.mean(grad_unit * unit, -1, keepdims=True)
+    )
+    stores = [load(grad_normed, input_grad_out, sem.at[4])]
     for stage in stages:
         wait(stage)
     branch = nn(act[...], down[...]).astype(BF16).astype(F32)
-    wait(loads)
+    middle_load.wait()
     mixed[...] = (middle[...] + upright(router[...]) * branch).astype(BF16)
-    load(mixed, mixed_out, sem.at[1]).wait()
-
-
-def mixed_output(router, middle, act, down, after):
-    (mixed,) = call(
-        mixed_kernel,
-        "mixed_output",
+    stores.append(load(mixed, mixed_out, sem.at[5]))
+    wait(stores)
+
+
+def ends(router, norm_gain, *arrays):
+    return call(
+        ends_kernel,
+        "ends",
         2 * T * D * FF,
-        12 * MIB,
-        16,
-        in_specs=[vmem()] + [hbm()] * 4,
-        out_specs=[hbm()],
-        out_shape=[sds((T, D), BF16)],
+        16 * MIB,
+        20,
+        in_specs=[vmem()] * 2 + [hbm()] * 7,
+        out_specs=[hbm()] * 2,
+        out_shape=[sds((T, D), BF16), sds((T, D), F32)],
         scratch_shapes=[
+            pltpu.VMEM((T, D), F32),
+            pltpu.VMEM((T, D), BF16),
+            pltpu.VMEM((T, D), BF16),
             pltpu.VMEM((T, D), F32),
             pltpu.VMEM((T, FF), BF16),
             pltpu.VMEM((FF, D), BF16),
             pltpu.VMEM((T, D), BF16),
-            pltpu.SemaphoreType.DMA((2,)),
+            pltpu.SemaphoreType.DMA((6,)),
             pltpu.SemaphoreType.DMA((2, NEST)),
         ],
-    )(router, middle, act, down, after)
-    return mixed
+    )(router, norm_gain, *arrays)
 
 
 def load_left(refs, at, rows, axis, left, sem):
@@ -932,10 +969,9 @@
         down_weight,
     )
     first_2, second_2 = swap_cores(first_other), swap_cores(second_other)
-    third, third_other, input_grad = back(
+    third, third_other, grad_normed = back(
         doc_lengths,
         heads_active,
-        norm_gain,
         inverse,
         levels,
         parts,
@@ -952,7 +988,17 @@
         second, second_other, second_2, third, third_other, third_2, down_sent
     )
 
-    mixed = mixed_output(router, middle, act, down_weight, qkv_sent)
+    mixed, input_grad = ends(
+        router,
+        norm_gain,
+        grad_normed,
+        first_other,
+        tokens,
+        middle,
+        act,
+        down_weight,
+        qkv_sent,
+    )
 
     every = slice(None)
     grads = {}

time: 135 us -> 134 us (level)
  no operation moved by 1% of the time
where the time goes in v5:
time: 134 us
  Pallas kernels  56.5 us (42%)
  starting transfers between devices  34.6 us (26%)
  waiting for transfers between devices  29 us (22%)
  other arithmetic  11.6 us (9%)
    pallas_call x5, Pallas kernels, placed(): run(*(pltpu.with_memory_space_constraint(arg, pltpu.HBM) if in_hbm(spec)...  56.5 us
    ppermute x9, starting transfers between devices, chain(): got_2 = lax.ppermute(more, (axis, 'c'), pairs(3, 1))  22.9 us
    ppermute x9, waiting for transfers between devices, chain(): got = lax.ppermute(sent, (axis, 'c'), pairs(1, 3))  16.1 us
    ppermute x9, waiting for transfers between devices, chain(): got_2 = lax.ppermute(more, (axis, 'c'), pairs(3, 1))  12.9 us
    ppermute x9, starting transfers between devices, chain(): got = lax.ppermute(sent, (axis, 'c'), pairs(1, 3))  10.8 us
    another operation x12, other arithmetic, chain(): kept = jnp.stack([own, second])  4.48 us
    convert_element_type x9, other arithmetic, chain(): more = (got[1].astype(F32) + kept[1].astype(F32)).astype(BF16)  3.49 us
  transfers between devices with their start and end apart: 21, of which 9 were waited for; matrix products, arithmetic and copies ran while one was open for 9% of the time, Pallas kernels for 26%

profile of v5, /device:TPU:0, one launch (start us, length us, event | category | flops | bytes accessed | tf_op | source)
XLA Modules:
  0.0 133.5 jit_solution(1252614127462246921)
XLA Ops:
  0.7 21.6 %front.1 = (f32[8,1024]{1,0:T(8,128)}, bf16[640,1024]{1,0:T(8,128)(2,1)}, bf16[1152,1024]{1,0:T(8,128)(2,1)}, bf16[384,1024]{1,0:T(8,128)(2,1)}, bf16[1408,1024]...) custom-call(s32[1,3]{1,0:T(1,128)} %lengths.3, s32[1,3]{1,0:T(1,128)} %heads.3, ...), custom_call_target="tpu_custom_call" | custom-call | flops 8589934592 | bytes 41943040 | tf_op jit(solution)/shard_map/front/pallas_call | solution.py:78
  22.9 11.7 %back.1 = (bf16[128,1024]{1,0:T(8,128)(2,1)}, bf16[896,1024]{1,0:T(8,128)(2,1)}, f32[256,1024]{1,0:T(8,128)}) custom-call(s32[1,3]{1,0:T(1,128)S(1)} %copy-done.3, s32[1,3]{1,0:T(1,128)S(1)} %copy-done.4, f32[1,128]{1,0:T(1,128)S(1)} %copy-done.5, s32[1,256]{1,0:T(1,128)S(1)} %bitcast.138, f32[8,1024]{1,0:T(8,128)} %get-tuple-element.83.parts_hbm, ...), custom_call_target="tpu_custom_call" | custom-call | flops 4831838208 | bytes 18874368 | tf_op jit(solution)/shard_map/back/pallas_call | solution.py:78
  35.0 6.2 %down_and_out_grad.1 = (bf16[2,512,1280]{2,1,0:T(8,128)(2,1)}, bf16[2,512,1280]{2,1,0:T(8,128)(2,1)}) custom-call(bf16[640,1024]{1,0:T(8,128)(2,1)} %get-tuple-element.93.own, bf16[1152,1024]{1,0:T(8,128)(2,1)} %get-tuple-element.84.first_other.one, bf16[1152,1024]{1,0:T(8,128)(2,1)S(1)} %collective-permute-done.2.two), custom_call_target="tpu_custom_call" | custom-call | flops 2684354560 | bytes 10485760 | tf_op jit(solution)/shard_map/down_and_out_grad/pallas_call | solution.py:78
  41.2 1.7 %collective-permute-start.4 = (bf16[2,512,1280]{2,1,0:T(8,128)(2,1)}, bf16[2,512,1280]{2,1,0:T(8,128)(2,1)S(1)}, u32[]{:S(2)}, u32[]{:S(2)}) collective-permute-start(bf16[2,512,1280]{2,1,0:T(8,128)(2,1)} %get-tuple-element.95.after), channel_id=1, source_target_pairs={{0,32},{1,97},{32,0},{33,65},{64,96},{65,33},{96,64},{97,1},{2,34}... | collective-permute-start | bytes 7864328 | tf_op jit(solution)/shard_map/ppermute | solution.py:887
  43.0 8.4 %up_and_qkv_grad.1 = (bf16[2,128,3584]{2,1,0:T(8,128)(2,1)}, bf16[2,128,3584]{2,1,0:T(8,128)(2,1)}, bf16[2,128,3712]{2,1,0:T(8,128)(2,1)}, bf16[2,128,3712]{2,1,0:T(8,128)(2,1)}) custom-call(bf16[384,1024]{1,0:T(8,128)(2,1)} %get-tuple-element.89.own, bf16[1408,1024]{1,0:T(8,128)(2,1)} %get-tuple-element.90.one, ...), custom_call_target="tpu_custom_call" | custom-call | flops 3758096384 | bytes 16777216 | tf_op jit(solution)/shard_map/up_and_qkv_grad/pallas_call | solution.py:78
  51.3 2.0 %collective-permute-start.3 = (bf16[2,128,3712]{2,1,0:T(8,128)(2,1)}, bf16[2,128,3712]{2,1,0:T(8,128)(2,1)}, u32[]{:S(2)}, u32[]{:S(2)}) collective-permute-start(bf16[2,128,3712]{2,1,0:T(8,128)(2,1)} %get-tuple-element.96.after), channel_id=1, source_target_pairs={{0,2},{1,7},{2,0},{3,5},{4,6},{5,3},{6,4},{7,1},{8,10},{9,15},{10,... | collective-permute-start | bytes 5701640 | tf_op jit(solution)/shard_map/ppermute | solution.py:887
  53.3 1.5 %collective-permute-start.6 = (bf16[2,128,3584]{2,1,0:T(8,128)(2,1)}, bf16[2,128,3584]{2,1,0:T(8,128)(2,1)}, u32[]{:S(2)}, u32[]{:S(2)}) collective-permute-start(bf16[2,128,3584]{2,1,0:T(8,128)(2,1)} %get-tuple-element.105), channel_id=1, source_target_pairs={{0,8},{1,25},{8,0},{9,17},{16,24},{17,9},{24,16},{25,1},{2,10},{3,... | collective-permute-start | bytes 5505032 | tf_op jit(solution)/shard_map/ppermute | solution.py:887
  54.8 8.7 %ends.1 = (bf16[256,1024]{1,0:T(8,128)(2,1)}, f32[256,1024]{1,0:T(8,128)}) custom-call(f32[1,256]{1,0:T(1,128)S(1)} %bitcast.136, f32[1,1024]{1,0:T(1,128)S(1)} %bitcast.134, f32[256,1024]{1,0:T(8,128)} %get-tuple-element.86.grad_normed_hbm, bf16[1152,1024]{1,0:T(8,128)(2,1)} %get-tuple-element.84.first_other.one, bf16[256,1024]{1,0:T(8,128)(2,1)} %tokens_hbm.5, ...), custom_call_target="tpu_custom_call" | custom-call | flops 2147483648 | bytes 16777216 | tf_op jit(solution)/shard_map/ends/pallas_call | solution.py:78
  63.5 9.6 %collective-permute-done.4 = bf16[2,512,1280]{2,1,0:T(8,128)(2,1)S(1)} collective-permute-done((bf16[2,512,1280]{2,1,0:T(8,128)(2,1)}, bf16[2,512,1280]{2,1,0:T(8,128)(2,1)S(1)}, u32[]{:S(2)}, u32[]{:S(2)}) %collective-permute-start.4) | collective-permute-done | bytes 2621472 | tf_op jit(solution)/shard_map/ppermute | solution.py:887
  73.5 3.2 %collective-permute-start.9 = (bf16[512,1280]{1,0:T(8,128)(2,1)S(1)}, bf16[512,1280]{1,0:T(8,128)(2,1)S(1)}, u32[]{:S(2)}, u32[]{:S(2)}) collective-permute-start(bf16[512,1280]{1,0:T(8,128)(2,1)S(1)} %fusion), channel_id=1, source_target_pairs={{0,96},{1,33},{32,64},{33,1},{64,32},{65,97},{96,0},{97,65},{2,98}... | collective-permute-start | bytes 3932168 | tf_op jit(solution)/shard_map/ppermute | solution.py:891
  76.6 1.5 %fusion.1 = bf16[128,3712]{1,0:T(8,128)(2,1)S(1)} fusion(bf16[2,128,3712]{2,1,0:T(8,128)(2,1)S(1)} %copy-done.7, bf16[2,128,3712]{2,1,0:T(8,128)(2,1)} %collective-permute-done.3), kind=kLoop, calls=%fused_computation.5 | loop fusion | flops 1900544 | bytes 2850816 | tf_op jit(solution)/shard_map/convert_element_type | solution.py:890
  78.1 4.1 %collective-permute-start.5 = (bf16[128,3712]{1,0:T(8,128)(2,1)S(1)}, bf16[128,3712]{1,0:T(8,128)(2,1)S(1)}, u32[]{:S(2)}, u32[]{:S(2)}) collective-permute-start(bf16[128,3712]{1,0:T(8,128)(2,1)S(1)} %fusion.1), channel_id=1, source_target_pairs={{0,6},{1,3},{2,4},{3,1},{4,2},{5,7},{6,0},{7,5},{8,14},{9,11},{10,... | collective-permute-start | bytes 2850824 | tf_op jit(solution)/shard_map/ppermute | solution.py:891
  82.3 1.5 %fusion.2 = bf16[128,3584]{1,0:T(8,128)(2,1)S(1)} fusion(bf16[2,128,3584]{2,1,0:T(8,128)(2,1)S(1)} %copy-done.8, bf16[2,128,3584]{2,1,0:T(8,128)(2,1)} %collective-permute-done.6), kind=kLoop, calls=%fused_computation.7 | loop fusion | flops 1835008 | bytes 2752512 | tf_op jit(solution)/shard_map/convert_element_type | solution.py:890
  83.7 2.8 %collective-permute-start.8 = (bf16[128,3584]{1,0:T(8,128)(2,1)S(1)}, bf16[128,3584]{1,0:T(8,128)(2,1)S(1)}, u32[]{:S(2)}, u32[]{:S(2)}) collective-permute-start(bf16[128,3584]{1,0:T(8,128)(2,1)S(1)} %fusion.2), channel_id=1, source_target_pairs={{0,24},{1,9},{8,16},{9,1},{16,8},{17,25},{24,0},{25,17},{2,26},{3,... | collective-permute-start | bytes 2752520 | tf_op jit(solution)/shard_map/ppermute | solution.py:891
  86.6 7.4 %collective-permute-done.5 = bf16[128,3712]{1,0:T(8,128)(2,1)S(1)} collective-permute-done((bf16[128,3712]{1,0:T(8,128)(2,1)S(1)}, bf16[128,3712]{1,0:T(8,128)(2,1)S(1)}, u32[]{:S(2)}, u32[]{:S(2)}) %collective-permute-start.5) | collective-permute-done | bytes 950304 | tf_op jit(solution)/shard_map/ppermute | solution.py:891
  94.0 1.7 %add_bitcast_fusion.3 = (f32[1,4,8,3712]{3,2,1,0:T(8,128)S(1)}, f32[1,4,8,3712]{3,2,1,0:T(8,128)S(1)}, bf16[1,4,8,3712]{3,2,1,0:T(8,128)(2,1)S(1)}, bf16[1,4,8,3712]{3,2,1,0:T(8,128)(2,1)S(1)}) fusion(bf16[1,4,4,8,3712]{4,3,2,1,0:T(8,128)(2,1)S(1)} %bitcast.144, s32[]{:T(128)S(6)} %select_n.26, bf16[2,4,4,8,3712]{4,3,2,1,0:T(8,128)(2,1)S(1)} %bitcast.141, ...), kind=kLoop, calls=%fused_computation.18 | loop fusion | flops 2613248 | bytes 4276240 | tf_op jit(solution)/shard_map/stack;reshape | solution.py:913
  96.7 1.6 %collective-permute-start.12 = (bf16[2,4,32,1280]{3,2,1,0:T(8,128)(2,1)S(1)}, bf16[2,4,32,1280]{3,2,1,0:T(8,128)(2,1)S(1)}, u32[]{:S(2)}, u32[]{:S(2)}) collective-permute-start(bf16[2,4,32,1280]{3,2,1,0:T(8,128)(2,1)S(1)} %pad_maximum_fusion.3), channel_id=1, source_target_pairs={{0,8},{1,25},{8,0},{9,17},{16,24},{17,9},{24,16},{25,1},{2,10},{3,... | collective-permute-start | bytes 1966088 | tf_op jit(solution)/shard_map/ppermute | solution.py:887
  98.4 1.6 %add_bitcast_fusion.5 = (f32[1,4,8,3584]{3,2,1,0:T(8,128)S(1)}, f32[1,4,8,3584]{3,2,1,0:T(8,128)S(1)}, bf16[1,4,8,3584]{3,2,1,0:T(8,128)(2,1)S(1)}, bf16[1,4,8,3584]{3,2,1,0:T(8,128)(2,1)S(1)}) fusion(bf16[1,4,4,8,3584]{4,3,2,1,0:T(8,128)(2,1)S(1)} %bitcast.145, s32[]{:T(128)S(6)} %select_n.26, bf16[2,4,4,8,3584]{4,3,2,1,0:T(8,128)(2,1)S(1)} %bitcast.142, ...), kind=kLoop, calls=%fused_computation.24 | loop fusion | flops 2523136 | bytes 4128784 | tf_op jit(solution)/shard_map/stack;reshape | solution.py:913
  100.1 1.8 %collective-permute-start.11 = (bf16[2,4,8,3584]{3,2,1,0:T(8,128)(2,1)S(1)}, bf16[2,4,8,3584]{3,2,1,0:T(8,128)(2,1)S(1)}, u32[]{:S(2)}, u32[]{:S(2)}) collective-permute-start(bf16[2,4,8,3584]{3,2,1,0:T(8,128)(2,1)S(1)} %pad_maximum_fusion.5), channel_id=1, source_target_pairs={{0,32},{1,97},{32,0},{33,65},{64,96},{65,33},{96,64},{97,1},{2,34}... | collective-permute-start | bytes 1376264 | tf_op jit(solution)/shard_map/ppermute | solution.py:887
  102.1 2.4 %collective-permute-done.7 = bf16[2,4,8,3712]{3,2,1,0:T(8,128)(2,1)S(1)} collective-permute-done((bf16[2,4,8,3712]{3,2,1,0:T(8,128)(2,1)S(1)}, bf16[2,4,8,3712]{3,2,1,0:T(8,128)(2,1)S(1)}, u32[]{:S(2)}, u32[]{:S(2)}) %collective-permute-start.7) | collective-permute-done | bytes 475168 | tf_op jit(solution)/shard_map/ppermute | solution.py:887
  104.5 1.3 collective-permute-start.10
  105.8 1.6 %collective-permute-done.12 = bf16[2,4,32,1280]{3,2,1,0:T(8,128)(2,1)S(1)} collective-permute-done((bf16[2,4,32,1280]{3,2,1,0:T(8,128)(2,1)S(1)}, bf16[2,4,32,1280]{3,2,1,0:T(8,128)(2,1)S(1)}, u32[]{:S(2)}, u32[]{:S(2)}) %collective-permute-start.12) | collective-permute-done | bytes 655392 | tf_op jit(solution)/shard_map/ppermute | solution.py:887
  107.4 2.8 %collective-permute-start.15 = (bf16[4,32,1280]{2,1,0:T(8,128)(2,1)S(1)}, bf16[4,32,1280]{2,1,0:T(8,128)(2,1)S(1)}, u32[]{:S(2)}, u32[]{:S(2)}) collective-permute-start(bf16[4,32,1280]{2,1,0:T(8,128)(2,1)S(1)} %fusion.5), channel_id=1, source_target_pairs={{0,24},{1,9},{8,16},{9,1},{16,8},{17,25},{24,0},{25,17},{2,26},{3,... | collective-permute-start | bytes 983048 | tf_op jit(solution)/shard_map/ppermute | solution.py:891
  110.3 2.5 %collective-permute-done.11 = bf16[2,4,8,3584]{3,2,1,0:T(8,128)(2,1)S(1)} collective-permute-done((bf16[2,4,8,3584]{3,2,1,0:T(8,128)(2,1)S(1)}, bf16[2,4,8,3584]{3,2,1,0:T(8,128)(2,1)S(1)}, u32[]{:S(2)}, u32[]{:S(2)}) %collective-permute-start.11) | collective-permute-done | bytes 458784 | tf_op jit(solution)/shard_map/ppermute | solution.py:887
  113.7 1.8 %collective-permute-start.13 = (bf16[2,8,3712]{2,1,0:T(8,128)(2,1)S(1)}, bf16[2,8,3712]{2,1,0:T(8,128)(2,1)S(1)}, u32[]{:S(2)}, u32[]{:S(2)}) collective-permute-start(bf16[2,8,3712]{2,1,0:T(8,128)(2,1)S(1)} %pad_maximum_fusion.11), channel_id=1, source_target_pairs={{0,8},{1,25},{8,0},{9,17},{16,24},{17,9},{24,16},{25,1},{2,10},{3,... | collective-permute-start | bytes 356360 | tf_op jit(solution)/shard_map/ppermute | solution.py:887
  115.5 0.8 collective-permute-done.15
  116.5 3.6 %collective-permute-done.14 = bf16[4,8,3584]{2,1,0:T(8,128)(2,1)S(1)} collective-permute-done((bf16[4,8,3584]{2,1,0:T(8,128)(2,1)S(1)}, bf16[4,8,3584]{2,1,0:T(8,128)(2,1)S(1)}, u32[]{:S(2)}, u32[]{:S(2)}) %collective-permute-start.14) | collective-permute-done | bytes 229408 | tf_op jit(solution)/shard_map/ppermute | solution.py:891
  120.4 2.8 %collective-permute-start.16 = (bf16[8,3712]{1,0:T(8,128)(2,1)S(1)}, bf16[8,3712]{1,0:T(8,128)(2,1)S(1)}, u32[]{:S(2)}, u32[]{:S(2)}) collective-permute-start(bf16[8,3712]{1,0:T(8,128)(2,1)S(1)} %fusion.27), channel_id=1, source_target_pairs={{0,24},{1,9},{8,16},{9,1},{16,8},{17,25},{24,0},{25,17},{2,26},{3,... | collective-permute-start | bytes 178184 | tf_op jit(solution)/shard_map/ppermute | solution.py:891
  123.3 3.6 %collective-permute-start.18 = (bf16[32,1280]{1,0:T(8,128)(2,1)S(1)}, bf16[32,1280]{1,0:T(8,128)(2,1)S(1)}, u32[]{:S(2)}, u32[]{:S(2)}) collective-permute-start(bf16[32,1280]{1,0:T(8,128)(2,1)S(1)} %fusion.24), channel_id=1, source_target_pairs={{0,6},{1,3},{2,4},{3,1},{4,2},{5,7},{6,0},{7,5},{8,14},{9,11},{10,... | collective-permute-start | bytes 245768 | tf_op jit(solution)/shard_map/ppermute | solution.py:891
  126.9 1.4 %collective-permute-start.20 = (bf16[8,3584]{1,0:T(8,128)(2,1)S(1)}, bf16[8,3584]{1,0:T(8,128)(2,1)S(1)}, u32[]{:S(2)}, u32[]{:S(2)}) collective-permute-start(bf16[8,3584]{1,0:T(8,128)(2,1)S(1)} %fusion.30), channel_id=1, source_target_pairs={{0,6},{1,3},{2,4},{3,1},{4,2},{5,7},{6,0},{7,5},{8,14},{9,11},{10,... | collective-permute-start | bytes 172040 | tf_op jit(solution)/shard_map/ppermute | solution.py:891
  128.4 1.0 collective-permute-done.18
  131.4 0.7 slice_reduce_fusion
  (71 shorter events, 7.6 us)
Async XLA Ops:
  0.6 22.3 %copy-start.2 = (s32[256,1]{0,1:T(1,128)S(1)}, s32[256,1]{0,1:T(1,128)}, u32[]{:S(2)}) copy-start(s32[256,1]{0,1:T(1,128)} %param.22) | copy-start | bytes 3076
  0.7 22.2 %copy-start.3 = (s32[1,3]{1,0:T(1,128)S(1)}, s32[1,3]{1,0:T(1,128)}, u32[]{:S(2)}) copy-start(s32[1,3]{1,0:T(1,128)} %lengths.3) | copy-start | bytes 40
  0.7 22.2 %copy-start.4 = (s32[1,3]{1,0:T(1,128)S(1)}, s32[1,3]{1,0:T(1,128)}, u32[]{:S(2)}) copy-start(s32[1,3]{1,0:T(1,128)} %heads.3) | copy-start | bytes 40
  0.7 22.2 %copy-start.5 = (f32[1,128]{1,0:T(1,128)S(1)}, f32[1,128]{1,0:T(1,128)}, u32[]{:S(2)}) copy-start(f32[1,128]{1,0:T(1,128)} %constant.27.clone.inverse) | copy-start | bytes 1540
  22.3 12.7 %collective-permute-start.2 = (bf16[1152,1024]{1,0:T(8,128)(2,1)}, bf16[1152,1024]{1,0:T(8,128)(2,1)S(1)}, u32[]{:S(2)}, u32[]{:S(2)}) collective-permute-start(bf16[1152,1024]{1,0:T(8,128)(2,1)} %get-tuple-element.84.first_other.one), channel_id=1, source_target_pairs={{0,1},{1,0},{2,3},{3,2},{4,5},{5,4},{6,7},{7,6},{8,9},{9,8},{10,11... | collective-permute-start | bytes 7077896 | tf_op jit(solution)/shard_map/ppermute | solution.py:869
  22.4 20.5 %collective-permute-start = (bf16[1408,1024]{1,0:T(8,128)(2,1)}, bf16[1408,1024]{1,0:T(8,128)(2,1)S(1)}, u32[]{:S(2)}, u32[]{:S(2)}) collective-permute-start(bf16[1408,1024]{1,0:T(8,128)(2,1)} %get-tuple-element.90.one), channel_id=1, source_target_pairs={{0,1},{1,0},{2,3},{3,2},{4,5},{5,4},{6,7},{7,6},{8,9},{9,8},{10,11... | collective-permute-start | bytes 8650760 | tf_op jit(solution)/shard_map/ppermute | solution.py:869
  34.6 8.3 %collective-permute-start.1 = (bf16[896,1024]{1,0:T(8,128)(2,1)}, bf16[896,1024]{1,0:T(8,128)(2,1)S(1)}, u32[]{:S(2)}, u32[]{:S(2)}) collective-permute-start(bf16[896,1024]{1,0:T(8,128)(2,1)} %get-tuple-element.92.three), channel_id=1, source_target_pairs={{0,1},{1,0},{2,3},{3,2},{4,5},{5,4},{6,7},{7,6},{8,9},{9,8},{10,11... | collective-permute-start | bytes 5505032 | tf_op jit(solution)/shard_map/ppermute | solution.py:869
  41.2 31.9 %collective-permute-start.4 = (bf16[2,512,1280]{2,1,0:T(8,128)(2,1)}, bf16[2,512,1280]{2,1,0:T(8,128)(2,1)S(1)}, u32[]{:S(2)}, u32[]{:S(2)}) collective-permute-start(bf16[2,512,1280]{2,1,0:T(8,128)(2,1)} %get-tuple-element.95.after), channel_id=1, source_target_pairs={{0,32},{1,97},{32,0},{33,65},{64,96},{65,33},{96,64},{97,1},{2,34}... | collective-permute-start | bytes 7864328 | tf_op jit(solution)/shard_map/ppermute | solution.py:887
  42.9 11.9 %copy-start = (f32[1024]{0:T(1024)S(1)}, f32[1024]{0:T(1024)}, u32[]{:S(2)}) copy-start(f32[1024]{0:T(1024)} %param.15) | copy-start | bytes 12292
  42.9 11.9 %copy-start.1 = (f32[256]{0:T(256)S(1)}, f32[256]{0:T(256)}, u32[]{:S(2)}) copy-start(f32[256]{0:T(256)} %param.23) | copy-start | bytes 3076
  51.3 25.3 %collective-permute-start.3 = (bf16[2,128,3712]{2,1,0:T(8,128)(2,1)}, bf16[2,128,3712]{2,1,0:T(8,128)(2,1)}, u32[]{:S(2)}, u32[]{:S(2)}) collective-permute-start(bf16[2,128,3712]{2,1,0:T(8,128)(2,1)} %get-tuple-element.96.after), channel_id=1, source_target_pairs={{0,2},{1,7},{2,0},{3,5},{4,6},{5,3},{6,4},{7,1},{8,10},{9,15},{10,... | collective-permute-start | bytes 5701640 | tf_op jit(solution)/shard_map/ppermute | solution.py:887
  53.3 28.9 %collective-permute-start.6 = (bf16[2,128,3584]{2,1,0:T(8,128)(2,1)}, bf16[2,128,3584]{2,1,0:T(8,128)(2,1)}, u32[]{:S(2)}, u32[]{:S(2)}) collective-permute-start(bf16[2,128,3584]{2,1,0:T(8,128)(2,1)} %get-tuple-element.105), channel_id=1, source_target_pairs={{0,8},{1,25},{8,0},{9,17},{16,24},{17,9},{24,16},{25,1},{2,10},{3,... | collective-permute-start | bytes 5505032 | tf_op jit(solution)/shard_map/ppermute | solution.py:887
  54.8 18.3 %copy-start.6 = (bf16[2,512,1280]{2,1,0:T(8,128)(2,1)S(1)}, bf16[2,512,1280]{2,1,0:T(8,128)(2,1)}, u32[]{:S(2)}) copy-start(bf16[2,512,1280]{2,1,0:T(8,128)(2,1)} %get-tuple-element.113) | copy-start | bytes 7864324
  73.1 3.5 %copy-start.7 = (bf16[2,128,3712]{2,1,0:T(8,128)(2,1)S(1)}, bf16[2,128,3712]{2,1,0:T(8,128)(2,1)}, u32[]{:S(2)}) copy-start(bf16[2,128,3712]{2,1,0:T(8,128)(2,1)} %get-tuple-element.110) | copy-start | bytes 5701636
  73.5 8.8 %copy-start.8 = (bf16[2,128,3584]{2,1,0:T(8,128)(2,1)S(1)}, bf16[2,128,3584]{2,1,0:T(8,128)(2,1)}, u32[]{:S(2)}) copy-start(bf16[2,128,3584]{2,1,0:T(8,128)(2,1)} %get-tuple-element.116) | copy-start | bytes 5505028
  73.5 22.5 %collective-permute-start.9 = (bf16[512,1280]{1,0:T(8,128)(2,1)S(1)}, bf16[512,1280]{1,0:T(8,128)(2,1)S(1)}, u32[]{:S(2)}, u32[]{:S(2)}) collective-permute-start(bf16[512,1280]{1,0:T(8,128)(2,1)S(1)} %fusion), channel_id=1, source_target_pairs={{0,96},{1,33},{32,64},{33,1},{64,32},{65,97},{96,0},{97,65},{2,98}... | collective-permute-start | bytes 3932168 | tf_op jit(solution)/shard_map/ppermute | solution.py:891
  78.1 15.8 %collective-permute-start.5 = (bf16[128,3712]{1,0:T(8,128)(2,1)S(1)}, bf16[128,3712]{1,0:T(8,128)(2,1)S(1)}, u32[]{:S(2)}, u32[]{:S(2)}) collective-permute-start(bf16[128,3712]{1,0:T(8,128)(2,1)S(1)} %fusion.1), channel_id=1, source_target_pairs={{0,6},{1,3},{2,4},{3,1},{4,2},{5,7},{6,0},{7,5},{8,14},{9,11},{10,... | collective-permute-start | bytes 2850824 | tf_op jit(solution)/shard_map/ppermute | solution.py:891
  83.7 14.7 %collective-permute-start.8 = (bf16[128,3584]{1,0:T(8,128)(2,1)S(1)}, bf16[128,3584]{1,0:T(8,128)(2,1)S(1)}, u32[]{:S(2)}, u32[]{:S(2)}) collective-permute-start(bf16[128,3584]{1,0:T(8,128)(2,1)S(1)} %fusion.2), channel_id=1, source_target_pairs={{0,24},{1,9},{8,16},{9,1},{16,8},{17,25},{24,0},{25,17},{2,26},{3,... | collective-permute-start | bytes 2752520 | tf_op jit(solution)/shard_map/ppermute | solution.py:891
  95.7 8.7 %collective-permute-start.7 = (bf16[2,4,8,3712]{3,2,1,0:T(8,128)(2,1)S(1)}, bf16[2,4,8,3712]{3,2,1,0:T(8,128)(2,1)S(1)}, u32[]{:S(2)}, u32[]{:S(2)}) collective-permute-start(bf16[2,4,8,3712]{3,2,1,0:T(8,128)(2,1)S(1)} %pad_maximum_fusion.4), channel_id=1, source_target_pairs={{0,32},{1,97},{32,0},{33,65},{64,96},{65,33},{96,64},{97,1},{2,34}... | collective-permute-start | bytes 1425416 | tf_op jit(solution)/shard_map/ppermute | solution.py:887
  96.7 10.7 %collective-permute-start.12 = (bf16[2,4,32,1280]{3,2,1,0:T(8,128)(2,1)S(1)}, bf16[2,4,32,1280]{3,2,1,0:T(8,128)(2,1)S(1)}, u32[]{:S(2)}, u32[]{:S(2)}) collective-permute-start(bf16[2,4,32,1280]{3,2,1,0:T(8,128)(2,1)S(1)} %pad_maximum_fusion.3), channel_id=1, source_target_pairs={{0,8},{1,25},{8,0},{9,17},{16,24},{17,9},{24,16},{25,1},{2,10},{3,... | collective-permute-start | bytes 1966088 | tf_op jit(solution)/shard_map/ppermute | solution.py:887
  100.1 12.7 %collective-permute-start.11 = (bf16[2,4,8,3584]{3,2,1,0:T(8,128)(2,1)S(1)}, bf16[2,4,8,3584]{3,2,1,0:T(8,128)(2,1)S(1)}, u32[]{:S(2)}, u32[]{:S(2)}) collective-permute-start(bf16[2,4,8,3584]{3,2,1,0:T(8,128)(2,1)S(1)} %pad_maximum_fusion.5), channel_id=1, source_target_pairs={{0,32},{1,97},{32,0},{33,65},{64,96},{65,33},{96,64},{97,1},{2,34}... | collective-permute-start | bytes 1376264 | tf_op jit(solution)/shard_map/ppermute | solution.py:887
  104.5 9.0 %collective-permute-start.10 = (bf16[4,8,3712]{2,1,0:T(8,128)(2,1)S(1)}, bf16[4,8,3712]{2,1,0:T(8,128)(2,1)S(1)}, u32[]{:S(2)}, u32[]{:S(2)}) collective-permute-start(bf16[4,8,3712]{2,1,0:T(8,128)(2,1)S(1)} %fusion.8), channel_id=1, source_target_pairs={{0,96},{1,33},{32,64},{33,1},{64,32},{65,97},{96,0},{97,65},{2,98}... | collective-permute-start | bytes 712712 | tf_op jit(solution)/shard_map/ppermute | solution.py:891
  107.4 8.9 %collective-permute-start.15 = (bf16[4,32,1280]{2,1,0:T(8,128)(2,1)S(1)}, bf16[4,32,1280]{2,1,0:T(8,128)(2,1)S(1)}, u32[]{:S(2)}, u32[]{:S(2)}) collective-permute-start(bf16[4,32,1280]{2,1,0:T(8,128)(2,1)S(1)} %fusion.5), channel_id=1, source_target_pairs={{0,24},{1,9},{8,16},{9,1},{16,8},{17,25},{24,0},{25,17},{2,26},{3,... | collective-permute-start | bytes 983048 | tf_op jit(solution)/shard_map/ppermute | solution.py:891
  112.8 7.3 %collective-permute-start.14 = (bf16[4,8,3584]{2,1,0:T(8,128)(2,1)S(1)}, bf16[4,8,3584]{2,1,0:T(8,128)(2,1)S(1)}, u32[]{:S(2)}, u32[]{:S(2)}) collective-permute-start(bf16[4,8,3584]{2,1,0:T(8,128)(2,1)S(1)} %fusion.11), channel_id=1, source_target_pairs={{0,96},{1,33},{32,64},{33,1},{64,32},{65,97},{96,0},{97,65},{2,98}... | collective-permute-start | bytes 688136 | tf_op jit(solution)/shard_map/ppermute | solution.py:891
  113.7 6.7 %collective-permute-start.13 = (bf16[2,8,3712]{2,1,0:T(8,128)(2,1)S(1)}, bf16[2,8,3712]{2,1,0:T(8,128)(2,1)S(1)}, u32[]{:S(2)}, u32[]{:S(2)}) collective-permute-start(bf16[2,8,3712]{2,1,0:T(8,128)(2,1)S(1)} %pad_maximum_fusion.11), channel_id=1, source_target_pairs={{0,8},{1,25},{8,0},{9,17},{16,24},{17,9},{24,16},{25,1},{2,10},{3,... | collective-permute-start | bytes 356360 | tf_op jit(solution)/shard_map/ppermute | solution.py:887
  116.4 6.8 %collective-permute-start.17 = (bf16[2,32,1280]{2,1,0:T(8,128)(2,1)S(1)}, bf16[2,32,1280]{2,1,0:T(8,128)(2,1)S(1)}, u32[]{:S(2)}, u32[]{:S(2)}) collective-permute-start(bf16[2,32,1280]{2,1,0:T(8,128)(2,1)S(1)} %pad_maximum_fusion.9), channel_id=1, source_target_pairs={{0,2},{1,7},{2,0},{3,5},{4,6},{5,3},{6,4},{7,1},{8,10},{9,15},{10,... | collective-permute-start | bytes 491528 | tf_op jit(solution)/shard_map/ppermute | solution.py:887
  120.2 6.7 %collective-permute-start.19 = (bf16[2,8,3584]{2,1,0:T(8,128)(2,1)S(1)}, bf16[2,8,3584]{2,1,0:T(8,128)(2,1)S(1)}, u32[]{:S(2)}, u32[]{:S(2)}) collective-permute-start(bf16[2,8,3584]{2,1,0:T(8,128)(2,1)S(1)} %pad_maximum_fusion.12), channel_id=1, source_target_pairs={{0,2},{1,7},{2,0},{3,5},{4,6},{5,3},{6,4},{7,1},{8,10},{9,15},{10,... | collective-permute-start | bytes 344072 | tf_op jit(solution)/shard_map/ppermute | solution.py:887
  120.4 10.3 %collective-permute-start.16 = (bf16[8,3712]{1,0:T(8,128)(2,1)S(1)}, bf16[8,3712]{1,0:T(8,128)(2,1)S(1)}, u32[]{:S(2)}, u32[]{:S(2)}) collective-permute-start(bf16[8,3712]{1,0:T(8,128)(2,1)S(1)} %fusion.27), channel_id=1, source_target_pairs={{0,24},{1,9},{8,16},{9,1},{16,8},{17,25},{24,0},{25,17},{2,26},{3,... | collective-permute-start | bytes 178184 | tf_op jit(solution)/shard_map/ppermute | solution.py:891
  123.3 6.0 %collective-permute-start.18 = (bf16[32,1280]{1,0:T(8,128)(2,1)S(1)}, bf16[32,1280]{1,0:T(8,128)(2,1)S(1)}, u32[]{:S(2)}, u32[]{:S(2)}) collective-permute-start(bf16[32,1280]{1,0:T(8,128)(2,1)S(1)} %fusion.24), channel_id=1, source_target_pairs={{0,6},{1,3},{2,4},{3,1},{4,2},{5,7},{6,0},{7,5},{8,14},{9,11},{10,... | collective-permute-start | bytes 245768 | tf_op jit(solution)/shard_map/ppermute | solution.py:891
  126.9 5.9 %collective-permute-start.20 = (bf16[8,3584]{1,0:T(8,128)(2,1)S(1)}, bf16[8,3584]{1,0:T(8,128)(2,1)S(1)}, u32[]{:S(2)}, u32[]{:S(2)}) collective-permute-start(bf16[8,3584]{1,0:T(8,128)(2,1)S(1)} %fusion.30), channel_id=1, source_target_pairs={{0,6},{1,3},{2,4},{3,1},{4,2},{5,7},{6,0},{7,5},{8,14},{9,11},{10,... | collective-permute-start | bytes 172040 | tf_op jit(solution)/shard_map/ppermute | solution.py:891

commit v6 on v5

--- a/solution.py
+++ b/solution.py
@@ -1031,7 +1031,7 @@
         mixed,
         TURNS,
         d=chain(down_sent, down_kept, "yxz", (4, 4, 32, D + T), down_done),
-        u=chain(up_sent, up_kept, "xyz", (4, 4, 8, UP), up_done),
+        u=chain(up_sent, up_kept, "xzy", (4, 4, 8, UP), up_done),
         q=chain(qkv_sent, qkv_kept, "zyx", (4, 4, 8, 3 * D + FF - UP + 128), qkv_done),
     )
     gain_grad, ln_gain_grad, ln_bias_grad = grads["gains"]

time: 134 us -> 134 us (level)
    ppermute x9, waiting for transfers between devices: 12.9 us -> 11.5 us  [chain(): got_2 = lax.ppermute(more, (axis, 'c'), pairs(3, 1))]
  transfers between devices with their start and end apart: 21 -> 21, of which waited for: 9 -> 8; matrix products, arithmetic and copies ran while one was open for 9% -> 9% of each run, Pallas kernels for 26% -> 26%
where the time goes in v6:
time: 134 us; the launch traced here: 133 us
  Pallas kernels  56.5 us (42%)
  starting transfers between devices  34.8 us (26%)
  waiting for transfers between devices  28.6 us (21%)
  other arithmetic  11.6 us (9%)
    pallas_call x5, Pallas kernels, placed(): run(*(pltpu.with_memory_space_constraint(arg, pltpu.HBM) if in_hbm(spec)...  56.5 us
    ppermute x9, starting transfers between devices, chain(): got_2 = lax.ppermute(more, (axis, 'c'), pairs(3, 1))  23.4 us
    ppermute x9, waiting for transfers between devices, chain(): got = lax.ppermute(sent, (axis, 'c'), pairs(1, 3))  17.1 us
    ppermute x9, waiting for transfers between devices, chain(): got_2 = lax.ppermute(more, (axis, 'c'), pairs(3, 1))  11.5 us
    ppermute x9, starting transfers between devices, chain(): got = lax.ppermute(sent, (axis, 'c'), pairs(1, 3))  10.4 us
    another operation x12, other arithmetic, chain(): kept = jnp.stack([own, second])  4.47 us
    convert_element_type x9, other arithmetic, chain(): more = (got[1].astype(F32) + kept[1].astype(F32)).astype(BF16)  3.48 us
  transfers between devices with their start and end apart: 21, of which 8 were waited for; matrix products, arithmetic and copies ran while one was open for 9% of the time, Pallas kernels for 26%

profile of v6, /device:TPU:0, one launch (start us, length us, event | category | flops | bytes accessed | tf_op | source)
XLA Modules:
  0.0 133.3 jit_solution(4105687659507741757)
XLA Ops:
  0.7 21.6 %front.1 = (f32[8,1024]{1,0:T(8,128)}, bf16[640,1024]{1,0:T(8,128)(2,1)}, bf16[1152,1024]{1,0:T(8,128)(2,1)}, bf16[384,1024]{1,0:T(8,128)(2,1)}, bf16[1408,1024]...) custom-call(s32[1,3]{1,0:T(1,128)} %lengths.3, s32[1,3]{1,0:T(1,128)} %heads.3, ...), custom_call_target="tpu_custom_call" | custom-call | flops 8589934592 | bytes 41943040 | tf_op jit(solution)/shard_map/front/pallas_call | solution.py:78
  22.9 11.7 %back.1 = (bf16[128,1024]{1,0:T(8,128)(2,1)}, bf16[896,1024]{1,0:T(8,128)(2,1)}, f32[256,1024]{1,0:T(8,128)}) custom-call(s32[1,3]{1,0:T(1,128)S(1)} %copy-done.3, s32[1,3]{1,0:T(1,128)S(1)} %copy-done.4, f32[1,128]{1,0:T(1,128)S(1)} %copy-done.5, s32[1,256]{1,0:T(1,128)S(1)} %bitcast.162, f32[8,1024]{1,0:T(8,128)} %get-tuple-element.83.parts_hbm, ...), custom_call_target="tpu_custom_call" | custom-call | flops 4831838208 | bytes 18874368 | tf_op jit(solution)/shard_map/back/pallas_call | solution.py:78
  35.0 6.2 %down_and_out_grad.1 = (bf16[2,512,1280]{2,1,0:T(8,128)(2,1)}, bf16[2,512,1280]{2,1,0:T(8,128)(2,1)}) custom-call(bf16[640,1024]{1,0:T(8,128)(2,1)} %get-tuple-element.93.own, bf16[1152,1024]{1,0:T(8,128)(2,1)} %get-tuple-element.84.first_other.one, bf16[1152,1024]{1,0:T(8,128)(2,1)S(1)} %collective-permute-done.2.two), custom_call_target="tpu_custom_call" | custom-call | flops 2684354560 | bytes 10485760 | tf_op jit(solution)/shard_map/down_and_out_grad/pallas_call | solution.py:78
  41.2 1.7 %collective-permute-start.4 = (bf16[2,512,1280]{2,1,0:T(8,128)(2,1)}, bf16[2,512,1280]{2,1,0:T(8,128)(2,1)S(1)}, u32[]{:S(2)}, u32[]{:S(2)}) collective-permute-start(bf16[2,512,1280]{2,1,0:T(8,128)(2,1)} %get-tuple-element.95.after), channel_id=1, source_target_pairs={{0,32},{1,97},{32,0},{33,65},{64,96},{65,33},{96,64},{97,1},{2,34}... | collective-permute-start | bytes 7864328 | tf_op jit(solution)/shard_map/ppermute | solution.py:887
  43.0 8.4 %up_and_qkv_grad.1 = (bf16[2,128,3584]{2,1,0:T(8,128)(2,1)}, bf16[2,128,3584]{2,1,0:T(8,128)(2,1)}, bf16[2,128,3712]{2,1,0:T(8,128)(2,1)}, bf16[2,128,3712]{2,1,0:T(8,128)(2,1)}) custom-call(bf16[384,1024]{1,0:T(8,128)(2,1)} %get-tuple-element.89.own, bf16[1408,1024]{1,0:T(8,128)(2,1)} %get-tuple-element.90.one, ...), custom_call_target="tpu_custom_call" | custom-call | flops 3758096384 | bytes 16777216 | tf_op jit(solution)/shard_map/up_and_qkv_grad/pallas_call | solution.py:78
  51.3 2.0 %collective-permute-start.3 = (bf16[2,128,3712]{2,1,0:T(8,128)(2,1)}, bf16[2,128,3712]{2,1,0:T(8,128)(2,1)}, u32[]{:S(2)}, u32[]{:S(2)}) collective-permute-start(bf16[2,128,3712]{2,1,0:T(8,128)(2,1)} %get-tuple-element.96.after), channel_id=1, source_target_pairs={{0,2},{1,7},{2,0},{3,5},{4,6},{5,3},{6,4},{7,1},{8,10},{9,15},{10,... | collective-permute-start | bytes 5701640 | tf_op jit(solution)/shard_map/ppermute | solution.py:887
  53.3 1.5 %collective-permute-start.6 = (bf16[2,128,3584]{2,1,0:T(8,128)(2,1)}, bf16[2,128,3584]{2,1,0:T(8,128)(2,1)}, u32[]{:S(2)}, u32[]{:S(2)}) collective-permute-start(bf16[2,128,3584]{2,1,0:T(8,128)(2,1)} %get-tuple-element.105), channel_id=1, source_target_pairs={{0,8},{1,25},{8,0},{9,17},{16,24},{17,9},{24,16},{25,1},{2,10},{3,... | collective-permute-start | bytes 5505032 | tf_op jit(solution)/shard_map/ppermute | solution.py:887
  54.8 8.7 %ends.1 = (bf16[256,1024]{1,0:T(8,128)(2,1)}, f32[256,1024]{1,0:T(8,128)}) custom-call(f32[1,256]{1,0:T(1,128)S(1)} %bitcast.160, f32[1,1024]{1,0:T(1,128)S(1)} %bitcast.158, f32[256,1024]{1,0:T(8,128)} %get-tuple-element.86.grad_normed_hbm, bf16[1152,1024]{1,0:T(8,128)(2,1)} %get-tuple-element.84.first_other.one, bf16[256,1024]{1,0:T(8,128)(2,1)} %tokens_hbm.5, ...), custom_call_target="tpu_custom_call" | custom-call | flops 2147483648 | bytes 16777216 | tf_op jit(solution)/shard_map/ends/pallas_call | solution.py:78
  63.5 9.6 %collective-permute-done.4 = bf16[2,512,1280]{2,1,0:T(8,128)(2,1)S(1)} collective-permute-done((bf16[2,512,1280]{2,1,0:T(8,128)(2,1)}, bf16[2,512,1280]{2,1,0:T(8,128)(2,1)S(1)}, u32[]{:S(2)}, u32[]{:S(2)}) %collective-permute-start.4) | collective-permute-done | bytes 2621472 | tf_op jit(solution)/shard_map/ppermute | solution.py:887
  73.5 3.2 %collective-permute-start.9 = (bf16[512,1280]{1,0:T(8,128)(2,1)S(1)}, bf16[512,1280]{1,0:T(8,128)(2,1)S(1)}, u32[]{:S(2)}, u32[]{:S(2)}) collective-permute-start(bf16[512,1280]{1,0:T(8,128)(2,1)S(1)} %fusion), channel_id=1, source_target_pairs={{0,96},{1,33},{32,64},{33,1},{64,32},{65,97},{96,0},{97,65},{2,98}... | collective-permute-start | bytes 3932168 | tf_op jit(solution)/shard_map/ppermute | solution.py:891
  76.6 1.5 %fusion.1 = bf16[128,3712]{1,0:T(8,128)(2,1)S(1)} fusion(bf16[2,128,3712]{2,1,0:T(8,128)(2,1)S(1)} %copy-done.7, bf16[2,128,3712]{2,1,0:T(8,128)(2,1)} %collective-permute-done.3), kind=kLoop, calls=%fused_computation.5 | loop fusion | flops 1900544 | bytes 2850816 | tf_op jit(solution)/shard_map/convert_element_type | solution.py:890
  78.1 4.1 %collective-permute-start.5 = (bf16[128,3712]{1,0:T(8,128)(2,1)S(1)}, bf16[128,3712]{1,0:T(8,128)(2,1)S(1)}, u32[]{:S(2)}, u32[]{:S(2)}) collective-permute-start(bf16[128,3712]{1,0:T(8,128)(2,1)S(1)} %fusion.1), channel_id=1, source_target_pairs={{0,6},{1,3},{2,4},{3,1},{4,2},{5,7},{6,0},{7,5},{8,14},{9,11},{10,... | collective-permute-start | bytes 2850824 | tf_op jit(solution)/shard_map/ppermute | solution.py:891
  82.3 1.5 %fusion.2 = bf16[128,3584]{1,0:T(8,128)(2,1)S(1)} fusion(bf16[2,128,3584]{2,1,0:T(8,128)(2,1)S(1)} %copy-done.8, bf16[2,128,3584]{2,1,0:T(8,128)(2,1)} %collective-permute-done.6), kind=kLoop, calls=%fused_computation.7 | loop fusion | flops 1835008 | bytes 2752512 | tf_op jit(solution)/shard_map/convert_element_type | solution.py:890
  83.7 2.8 %collective-permute-start.8 = (bf16[128,3584]{1,0:T(8,128)(2,1)S(1)}, bf16[128,3584]{1,0:T(8,128)(2,1)S(1)}, u32[]{:S(2)}, u32[]{:S(2)}) collective-permute-start(bf16[128,3584]{1,0:T(8,128)(2,1)S(1)} %fusion.2), channel_id=1, source_target_pairs={{0,24},{1,9},{8,16},{9,1},{16,8},{17,25},{24,0},{25,17},{2,26},{3,... | collective-permute-start | bytes 2752520 | tf_op jit(solution)/shard_map/ppermute | solution.py:891
  86.6 7.4 %collective-permute-done.5 = bf16[128,3712]{1,0:T(8,128)(2,1)S(1)} collective-permute-done((bf16[128,3712]{1,0:T(8,128)(2,1)S(1)}, bf16[128,3712]{1,0:T(8,128)(2,1)S(1)}, u32[]{:S(2)}, u32[]{:S(2)}) %collective-permute-start.5) | collective-permute-done | bytes 950304 | tf_op jit(solution)/shard_map/ppermute | solution.py:891
  94.0 1.7 %add_bitcast_fusion.3 = (f32[1,4,8,3712]{3,2,1,0:T(8,128)S(1)}, f32[1,4,8,3712]{3,2,1,0:T(8,128)S(1)}, bf16[1,4,8,3712]{3,2,1,0:T(8,128)(2,1)S(1)}, bf16[1,4,8,3712]{3,2,1,0:T(8,128)(2,1)S(1)}) fusion(bf16[1,4,4,8,3712]{4,3,2,1,0:T(8,128)(2,1)S(1)} %bitcast.168, s32[]{:T(128)S(6)} %select_n.26, bf16[2,4,4,8,3712]{4,3,2,1,0:T(8,128)(2,1)S(1)} %bitcast.165, ...), kind=kLoop, calls=%fused_computation.18 | loop fusion | flops 2613248 | bytes 4276240 | tf_op jit(solution)/shard_map/stack;reshape | solution.py:913
  96.7 1.6 %collective-permute-start.12 = (bf16[2,4,32,1280]{3,2,1,0:T(8,128)(2,1)S(1)}, bf16[2,4,32,1280]{3,2,1,0:T(8,128)(2,1)S(1)}, u32[]{:S(2)}, u32[]{:S(2)}) collective-permute-start(bf16[2,4,32,1280]{3,2,1,0:T(8,128)(2,1)S(1)} %pad_maximum_fusion.3), channel_id=1, source_target_pairs={{0,8},{1,25},{8,0},{9,17},{16,24},{17,9},{24,16},{25,1},{2,10},{3,... | collective-permute-start | bytes 1966088 | tf_op jit(solution)/shard_map/ppermute | solution.py:887
  98.4 1.6 %add_bitcast_fusion.5 = (f32[1,4,8,3584]{3,2,1,0:T(8,128)S(1)}, bf16[1,4,8,3584]{3,2,1,0:T(8,128)(2,1)S(1)}, bf16[1,4,8,3584]{3,2,1,0:T(8,128)(2,1)S(1)}, f32[1,4,8,3584]{3,2,1,0:T(8,128)S(1)}) fusion(bf16[1,4,4,8,3584]{4,3,2,1,0:T(8,128)(2,1)S(1)} %bitcast.169, s32[]{:T(128)S(6)} %select_n.32, bf16[2,4,4,8,3584]{4,3,2,1,0:T(8,128)(2,1)S(1)} %bitcast.166, ...), kind=kLoop, calls=%fused_computation.24 | loop fusion | flops 2523136 | bytes 4128784 | tf_op jit(solution)/shard_map/stack;reshape | solution.py:913
  100.4 4.1 %collective-permute-done.7 = bf16[2,4,8,3712]{3,2,1,0:T(8,128)(2,1)S(1)} collective-permute-done((bf16[2,4,8,3712]{3,2,1,0:T(8,128)(2,1)S(1)}, bf16[2,4,8,3712]{3,2,1,0:T(8,128)(2,1)S(1)}, u32[]{:S(2)}, u32[]{:S(2)}) %collective-permute-start.7) | collective-permute-done | bytes 475168 | tf_op jit(solution)/shard_map/ppermute | solution.py:887
  104.5 1.3 collective-permute-start.10
  105.8 1.6 %collective-permute-done.12 = bf16[2,4,32,1280]{3,2,1,0:T(8,128)(2,1)S(1)} collective-permute-done((bf16[2,4,32,1280]{3,2,1,0:T(8,128)(2,1)S(1)}, bf16[2,4,32,1280]{3,2,1,0:T(8,128)(2,1)S(1)}, u32[]{:S(2)}, u32[]{:S(2)}) %collective-permute-start.12) | collective-permute-done | bytes 655392 | tf_op jit(solution)/shard_map/ppermute | solution.py:887
  107.4 2.8 %collective-permute-start.15 = (bf16[4,32,1280]{2,1,0:T(8,128)(2,1)S(1)}, bf16[4,32,1280]{2,1,0:T(8,128)(2,1)S(1)}, u32[]{:S(2)}, u32[]{:S(2)}) collective-permute-start(bf16[4,32,1280]{2,1,0:T(8,128)(2,1)S(1)} %fusion.5), channel_id=1, source_target_pairs={{0,24},{1,9},{8,16},{9,1},{16,8},{17,25},{24,0},{25,17},{2,26},{3,... | collective-permute-start | bytes 983048 | tf_op jit(solution)/shard_map/ppermute | solution.py:891
  110.3 3.3 %collective-permute-start.14 = (bf16[4,8,3584]{2,1,0:T(8,128)(2,1)S(1)}, bf16[4,8,3584]{2,1,0:T(8,128)(2,1)S(1)}, u32[]{:S(2)}, u32[]{:S(2)}) collective-permute-start(bf16[4,8,3584]{2,1,0:T(8,128)(2,1)S(1)} %fusion.11), channel_id=1, source_target_pairs={{0,6},{1,3},{2,4},{3,1},{4,2},{5,7},{6,0},{7,5},{8,14},{9,11},{10,... | collective-permute-start | bytes 688136 | tf_op jit(solution)/shard_map/ppermute | solution.py:891
  114.1 3.0 %collective-permute-done.15 = bf16[4,32,1280]{2,1,0:T(8,128)(2,1)S(1)} collective-permute-done((bf16[4,32,1280]{2,1,0:T(8,128)(2,1)S(1)}, bf16[4,32,1280]{2,1,0:T(8,128)(2,1)S(1)}, u32[]{:S(2)}, u32[]{:S(2)}) %collective-permute-start.15) | collective-permute-done | bytes 327712 | tf_op jit(solution)/shard_map/ppermute | solution.py:891
  117.3 0.9 collective-permute-done.14
  118.3 3.0 %collective-permute-start.19 = (bf16[2,8,3584]{2,1,0:T(8,128)(2,1)S(1)}, bf16[2,8,3584]{2,1,0:T(8,128)(2,1)S(1)}, u32[]{:S(2)}, u32[]{:S(2)}) collective-permute-start(bf16[2,8,3584]{2,1,0:T(8,128)(2,1)S(1)} %pad_maximum_fusion.12), channel_id=1, source_target_pairs={{0,32},{1,97},{32,0},{33,65},{64,96},{65,33},{96,64},{97,1},{2,34}... | collective-permute-start | bytes 344072 | tf_op jit(solution)/shard_map/ppermute | solution.py:887
  121.4 1.8 %collective-permute-done.17 = bf16[2,32,1280]{2,1,0:T(8,128)(2,1)S(1)} collective-permute-done((bf16[2,32,1280]{2,1,0:T(8,128)(2,1)S(1)}, bf16[2,32,1280]{2,1,0:T(8,128)(2,1)S(1)}, u32[]{:S(2)}, u32[]{:S(2)}) %collective-permute-start.17) | collective-permute-done | bytes 163872 | tf_op jit(solution)/shard_map/ppermute | solution.py:887
  123.3 3.3 %collective-permute-start.18 = (bf16[32,1280]{1,0:T(8,128)(2,1)S(1)}, bf16[32,1280]{1,0:T(8,128)(2,1)S(1)}, u32[]{:S(2)}, u32[]{:S(2)}) collective-permute-start(bf16[32,1280]{1,0:T(8,128)(2,1)S(1)} %fusion.24), channel_id=1, source_target_pairs={{0,6},{1,3},{2,4},{3,1},{4,2},{5,7},{6,0},{7,5},{8,14},{9,11},{10,... | collective-permute-start | bytes 245768 | tf_op jit(solution)/shard_map/ppermute | solution.py:891
  126.6 2.4 %collective-permute-start.20 = (bf16[8,3584]{1,0:T(8,128)(2,1)S(1)}, bf16[8,3584]{1,0:T(8,128)(2,1)S(1)}, u32[]{:S(2)}, u32[]{:S(2)}) collective-permute-start(bf16[8,3584]{1,0:T(8,128)(2,1)S(1)} %fusion.30), channel_id=1, source_target_pairs={{0,96},{1,33},{32,64},{33,1},{64,32},{65,97},{96,0},{97,65},{2,98}... | collective-permute-start | bytes 172040 | tf_op jit(solution)/shard_map/ppermute | solution.py:891
  129.1 0.7 add_bitcast_fusion.6
  131.1 0.7 slice_reduce_fusion
  132.6 0.7 pad_maximum_fusion.10
  (71 shorter events, 6.0 us)
Async XLA Ops:
  0.6 22.3 %copy-start.2 = (s32[256,1]{0,1:T(1,128)S(1)}, s32[256,1]{0,1:T(1,128)}, u32[]{:S(2)}) copy-start(s32[256,1]{0,1:T(1,128)} %param.22) | copy-start | bytes 3076
  0.7 22.2 %copy-start.3 = (s32[1,3]{1,0:T(1,128)S(1)}, s32[1,3]{1,0:T(1,128)}, u32[]{:S(2)}) copy-start(s32[1,3]{1,0:T(1,128)} %lengths.3) | copy-start | bytes 40
  0.7 22.2 %copy-start.4 = (s32[1,3]{1,0:T(1,128)S(1)}, s32[1,3]{1,0:T(1,128)}, u32[]{:S(2)}) copy-start(s32[1,3]{1,0:T(1,128)} %heads.3) | copy-start | bytes 40
  0.7 22.2 %copy-start.5 = (f32[1,128]{1,0:T(1,128)S(1)}, f32[1,128]{1,0:T(1,128)}, u32[]{:S(2)}) copy-start(f32[1,128]{1,0:T(1,128)} %constant.27.clone.inverse) | copy-start | bytes 1540
  22.3 12.7 %collective-permute-start.2 = (bf16[1152,1024]{1,0:T(8,128)(2,1)}, bf16[1152,1024]{1,0:T(8,128)(2,1)S(1)}, u32[]{:S(2)}, u32[]{:S(2)}) collective-permute-start(bf16[1152,1024]{1,0:T(8,128)(2,1)} %get-tuple-element.84.first_other.one), channel_id=1, source_target_pairs={{0,1},{1,0},{2,3},{3,2},{4,5},{5,4},{6,7},{7,6},{8,9},{9,8},{10,11... | collective-permute-start | bytes 7077896 | tf_op jit(solution)/shard_map/ppermute | solution.py:869
  22.4 20.5 %collective-permute-start = (bf16[1408,1024]{1,0:T(8,128)(2,1)}, bf16[1408,1024]{1,0:T(8,128)(2,1)S(1)}, u32[]{:S(2)}, u32[]{:S(2)}) collective-permute-start(bf16[1408,1024]{1,0:T(8,128)(2,1)} %get-tuple-element.90.one), channel_id=1, source_target_pairs={{0,1},{1,0},{2,3},{3,2},{4,5},{5,4},{6,7},{7,6},{8,9},{9,8},{10,11... | collective-permute-start | bytes 8650760 | tf_op jit(solution)/shard_map/ppermute | solution.py:869
  34.6 8.3 %collective-permute-start.1 = (bf16[896,1024]{1,0:T(8,128)(2,1)}, bf16[896,1024]{1,0:T(8,128)(2,1)S(1)}, u32[]{:S(2)}, u32[]{:S(2)}) collective-permute-start(bf16[896,1024]{1,0:T(8,128)(2,1)} %get-tuple-element.92.three), channel_id=1, source_target_pairs={{0,1},{1,0},{2,3},{3,2},{4,5},{5,4},{6,7},{7,6},{8,9},{9,8},{10,11... | collective-permute-start | bytes 5505032 | tf_op jit(solution)/shard_map/ppermute | solution.py:869
  41.2 31.9 %collective-permute-start.4 = (bf16[2,512,1280]{2,1,0:T(8,128)(2,1)}, bf16[2,512,1280]{2,1,0:T(8,128)(2,1)S(1)}, u32[]{:S(2)}, u32[]{:S(2)}) collective-permute-start(bf16[2,512,1280]{2,1,0:T(8,128)(2,1)} %get-tuple-element.95.after), channel_id=1, source_target_pairs={{0,32},{1,97},{32,0},{33,65},{64,96},{65,33},{96,64},{97,1},{2,34}... | collective-permute-start | bytes 7864328 | tf_op jit(solution)/shard_map/ppermute | solution.py:887
  42.9 11.9 %copy-start = (f32[1024]{0:T(1024)S(1)}, f32[1024]{0:T(1024)}, u32[]{:S(2)}) copy-start(f32[1024]{0:T(1024)} %param.15) | copy-start | bytes 12292
  42.9 11.9 %copy-start.1 = (f32[256]{0:T(256)S(1)}, f32[256]{0:T(256)}, u32[]{:S(2)}) copy-start(f32[256]{0:T(256)} %param.23) | copy-start | bytes 3076
  51.3 25.3 %collective-permute-start.3 = (bf16[2,128,3712]{2,1,0:T(8,128)(2,1)}, bf16[2,128,3712]{2,1,0:T(8,128)(2,1)}, u32[]{:S(2)}, u32[]{:S(2)}) collective-permute-start(bf16[2,128,3712]{2,1,0:T(8,128)(2,1)} %get-tuple-element.96.after), channel_id=1, source_target_pairs={{0,2},{1,7},{2,0},{3,5},{4,6},{5,3},{6,4},{7,1},{8,10},{9,15},{10,... | collective-permute-start | bytes 5701640 | tf_op jit(solution)/shard_map/ppermute | solution.py:887
  53.3 28.9 %collective-permute-start.6 = (bf16[2,128,3584]{2,1,0:T(8,128)(2,1)}, bf16[2,128,3584]{2,1,0:T(8,128)(2,1)}, u32[]{:S(2)}, u32[]{:S(2)}) collective-permute-start(bf16[2,128,3584]{2,1,0:T(8,128)(2,1)} %get-tuple-element.105), channel_id=1, source_target_pairs={{0,8},{1,25},{8,0},{9,17},{16,24},{17,9},{24,16},{25,1},{2,10},{3,... | collective-permute-start | bytes 5505032 | tf_op jit(solution)/shard_map/ppermute | solution.py:887
  54.8 18.3 %copy-start.6 = (bf16[2,512,1280]{2,1,0:T(8,128)(2,1)S(1)}, bf16[2,512,1280]{2,1,0:T(8,128)(2,1)}, u32[]{:S(2)}) copy-start(bf16[2,512,1280]{2,1,0:T(8,128)(2,1)} %get-tuple-element.113) | copy-start | bytes 7864324
  73.1 3.5 %copy-start.7 = (bf16[2,128,3712]{2,1,0:T(8,128)(2,1)S(1)}, bf16[2,128,3712]{2,1,0:T(8,128)(2,1)}, u32[]{:S(2)}) copy-start(bf16[2,128,3712]{2,1,0:T(8,128)(2,1)} %get-tuple-element.110) | copy-start | bytes 5701636
  73.5 8.8 %copy-start.8 = (bf16[2,128,3584]{2,1,0:T(8,128)(2,1)S(1)}, bf16[2,128,3584]{2,1,0:T(8,128)(2,1)}, u32[]{:S(2)}) copy-start(bf16[2,128,3584]{2,1,0:T(8,128)(2,1)} %get-tuple-element.116) | copy-start | bytes 5505028
  73.5 22.5 %collective-permute-start.9 = (bf16[512,1280]{1,0:T(8,128)(2,1)S(1)}, bf16[512,1280]{1,0:T(8,128)(2,1)S(1)}, u32[]{:S(2)}, u32[]{:S(2)}) collective-permute-start(bf16[512,1280]{1,0:T(8,128)(2,1)S(1)} %fusion), channel_id=1, source_target_pairs={{0,96},{1,33},{32,64},{33,1},{64,32},{65,97},{96,0},{97,65},{2,98}... | collective-permute-start | bytes 3932168 | tf_op jit(solution)/shard_map/ppermute | solution.py:891
  78.1 15.8 %collective-permute-start.5 = (bf16[128,3712]{1,0:T(8,128)(2,1)S(1)}, bf16[128,3712]{1,0:T(8,128)(2,1)S(1)}, u32[]{:S(2)}, u32[]{:S(2)}) collective-permute-start(bf16[128,3712]{1,0:T(8,128)(2,1)S(1)} %fusion.1), channel_id=1, source_target_pairs={{0,6},{1,3},{2,4},{3,1},{4,2},{5,7},{6,0},{7,5},{8,14},{9,11},{10,... | collective-permute-start | bytes 2850824 | tf_op jit(solution)/shard_map/ppermute | solution.py:891
  83.7 14.7 %collective-permute-start.8 = (bf16[128,3584]{1,0:T(8,128)(2,1)S(1)}, bf16[128,3584]{1,0:T(8,128)(2,1)S(1)}, u32[]{:S(2)}, u32[]{:S(2)}) collective-permute-start(bf16[128,3584]{1,0:T(8,128)(2,1)S(1)} %fusion.2), channel_id=1, source_target_pairs={{0,24},{1,9},{8,16},{9,1},{16,8},{17,25},{24,0},{25,17},{2,26},{3,... | collective-permute-start | bytes 2752520 | tf_op jit(solution)/shard_map/ppermute | solution.py:891
  95.7 8.7 %collective-permute-start.7 = (bf16[2,4,8,3712]{3,2,1,0:T(8,128)(2,1)S(1)}, bf16[2,4,8,3712]{3,2,1,0:T(8,128)(2,1)S(1)}, u32[]{:S(2)}, u32[]{:S(2)}) collective-permute-start(bf16[2,4,8,3712]{3,2,1,0:T(8,128)(2,1)S(1)} %pad_maximum_fusion.4), channel_id=1, source_target_pairs={{0,32},{1,97},{32,0},{33,65},{64,96},{65,33},{96,64},{97,1},{2,34}... | collective-permute-start | bytes 1425416 | tf_op jit(solution)/shard_map/ppermute | solution.py:887
  96.7 10.7 %collective-permute-start.12 = (bf16[2,4,32,1280]{3,2,1,0:T(8,128)(2,1)S(1)}, bf16[2,4,32,1280]{3,2,1,0:T(8,128)(2,1)S(1)}, u32[]{:S(2)}, u32[]{:S(2)}) collective-permute-start(bf16[2,4,32,1280]{3,2,1,0:T(8,128)(2,1)S(1)} %pad_maximum_fusion.3), channel_id=1, source_target_pairs={{0,8},{1,25},{8,0},{9,17},{16,24},{17,9},{24,16},{25,1},{2,10},{3,... | collective-permute-start | bytes 1966088 | tf_op jit(solution)/shard_map/ppermute | solution.py:887
  100.1 10.2 %collective-permute-start.11 = (bf16[2,4,8,3584]{3,2,1,0:T(8,128)(2,1)S(1)}, bf16[2,4,8,3584]{3,2,1,0:T(8,128)(2,1)S(1)}, u32[]{:S(2)}, u32[]{:S(2)}) collective-permute-start(bf16[2,4,8,3584]{3,2,1,0:T(8,128)(2,1)S(1)} %pad_maximum_fusion.5), channel_id=1, source_target_pairs={{0,2},{1,7},{2,0},{3,5},{4,6},{5,3},{6,4},{7,1},{8,10},{9,15},{10,... | collective-permute-start | bytes 1376264 | tf_op jit(solution)/shard_map/ppermute | solution.py:887
  104.5 9.1 %collective-permute-start.10 = (bf16[4,8,3712]{2,1,0:T(8,128)(2,1)S(1)}, bf16[4,8,3712]{2,1,0:T(8,128)(2,1)S(1)}, u32[]{:S(2)}, u32[]{:S(2)}) collective-permute-start(bf16[4,8,3712]{2,1,0:T(8,128)(2,1)S(1)} %fusion.8), channel_id=1, source_target_pairs={{0,96},{1,33},{32,64},{33,1},{64,32},{65,97},{96,0},{97,65},{2,98}... | collective-permute-start | bytes 712712 | tf_op jit(solution)/shard_map/ppermute | solution.py:891
  107.4 9.6 %collective-permute-start.15 = (bf16[4,32,1280]{2,1,0:T(8,128)(2,1)S(1)}, bf16[4,32,1280]{2,1,0:T(8,128)(2,1)S(1)}, u32[]{:S(2)}, u32[]{:S(2)}) collective-permute-start(bf16[4,32,1280]{2,1,0:T(8,128)(2,1)S(1)} %fusion.5), channel_id=1, source_target_pairs={{0,24},{1,9},{8,16},{9,1},{16,8},{17,25},{24,0},{25,17},{2,26},{3,... | collective-permute-start | bytes 983048 | tf_op jit(solution)/shard_map/ppermute | solution.py:891
  110.3 7.9 %collective-permute-start.14 = (bf16[4,8,3584]{2,1,0:T(8,128)(2,1)S(1)}, bf16[4,8,3584]{2,1,0:T(8,128)(2,1)S(1)}, u32[]{:S(2)}, u32[]{:S(2)}) collective-permute-start(bf16[4,8,3584]{2,1,0:T(8,128)(2,1)S(1)} %fusion.11), channel_id=1, source_target_pairs={{0,6},{1,3},{2,4},{3,1},{4,2},{5,7},{6,0},{7,5},{8,14},{9,11},{10,... | collective-permute-start | bytes 688136 | tf_op jit(solution)/shard_map/ppermute | solution.py:891
  113.8 7.5 %collective-permute-start.13 = (bf16[2,8,3712]{2,1,0:T(8,128)(2,1)S(1)}, bf16[2,8,3712]{2,1,0:T(8,128)(2,1)S(1)}, u32[]{:S(2)}, u32[]{:S(2)}) collective-permute-start(bf16[2,8,3712]{2,1,0:T(8,128)(2,1)S(1)} %pad_maximum_fusion.11), channel_id=1, source_target_pairs={{0,8},{1,25},{8,0},{9,17},{16,24},{17,9},{24,16},{25,1},{2,10},{3,... | collective-permute-start | bytes 356360 | tf_op jit(solution)/shard_map/ppermute | solution.py:887
  117.2 6.1 %collective-permute-start.17 = (bf16[2,32,1280]{2,1,0:T(8,128)(2,1)S(1)}, bf16[2,32,1280]{2,1,0:T(8,128)(2,1)S(1)}, u32[]{:S(2)}, u32[]{:S(2)}) collective-permute-start(bf16[2,32,1280]{2,1,0:T(8,128)(2,1)S(1)} %pad_maximum_fusion.9), channel_id=1, source_target_pairs={{0,2},{1,7},{2,0},{3,5},{4,6},{5,3},{6,4},{7,1},{8,10},{9,15},{10,... | collective-permute-start | bytes 491528 | tf_op jit(solution)/shard_map/ppermute | solution.py:887
  118.3 8.3 %collective-permute-start.19 = (bf16[2,8,3584]{2,1,0:T(8,128)(2,1)S(1)}, bf16[2,8,3584]{2,1,0:T(8,128)(2,1)S(1)}, u32[]{:S(2)}, u32[]{:S(2)}) collective-permute-start(bf16[2,8,3584]{2,1,0:T(8,128)(2,1)S(1)} %pad_maximum_fusion.12), channel_id=1, source_target_pairs={{0,32},{1,97},{32,0},{33,65},{64,96},{65,33},{96,64},{97,1},{2,34}... | collective-permute-start | bytes 344072 | tf_op jit(solution)/shard_map/ppermute | solution.py:887
  121.3 9.1 %collective-permute-start.16 = (bf16[8,3712]{1,0:T(8,128)(2,1)S(1)}, bf16[8,3712]{1,0:T(8,128)(2,1)S(1)}, u32[]{:S(2)}, u32[]{:S(2)}) collective-permute-start(bf16[8,3712]{1,0:T(8,128)(2,1)S(1)} %fusion.27), channel_id=1, source_target_pairs={{0,24},{1,9},{8,16},{9,1},{16,8},{17,25},{24,0},{25,17},{2,26},{3,... | collective-permute-start | bytes 178184 | tf_op jit(solution)/shard_map/ppermute | solution.py:891
  123.3 5.8 %collective-permute-start.18 = (bf16[32,1280]{1,0:T(8,128)(2,1)S(1)}, bf16[32,1280]{1,0:T(8,128)(2,1)S(1)}, u32[]{:S(2)}, u32[]{:S(2)}) collective-permute-start(bf16[32,1280]{1,0:T(8,128)(2,1)S(1)} %fusion.24), channel_id=1, source_target_pairs={{0,6},{1,3},{2,4},{3,1},{4,2},{5,7},{6,0},{7,5},{8,14},{9,11},{10,... | collective-permute-start | bytes 245768 | tf_op jit(solution)/shard_map/ppermute | solution.py:891
  126.6 6.0 %collective-permute-start.20 = (bf16[8,3584]{1,0:T(8,128)(2,1)S(1)}, bf16[8,3584]{1,0:T(8,128)(2,1)S(1)}, u32[]{:S(2)}, u32[]{:S(2)}) collective-permute-start(bf16[8,3584]{1,0:T(8,128)(2,1)S(1)} %fusion.30), channel_id=1, source_target_pairs={{0,96},{1,33},{32,64},{33,1},{64,32},{65,97},{96,0},{97,65},{2,98}... | collective-permute-start | bytes 172040 | tf_op jit(solution)/shard_map/ppermute | solution.py:891
